TPU v7x, 32 devices: a whole 2x2x4 slice. The times are simulated.
32 devices in a mesh: tok: 16 (over z, y, x), ch: 2 (over core).
Axes of the slice: x: 2, y: 2, z: 4, core: 2. Of those that a mesh axis runs over, the one named last changes fastest.
Arguments:
- fields: float32 [16384, 1024], P('tok', 'ch'), may hold values from -20 to 20
- gain_one: float32 [1024], P('ch'), may hold values from 0.1 to 1.9
- tok_in_weight: float32 [3072, 16384], P('ch', 'tok'), may hold values from -0.046875 to 0.046875
- tok_in_bias: float32 [3072], P('ch'), may hold values from -3 to 3
- tok_out_weight: float32 [16384, 3072], P('tok', 'ch'), may hold values from -0.109375 to 0.109375
- gain_two: float32 [1024], P('ch'), may hold values from 0.1 to 1.9
- ch_in_weight: float32 [1024, 6144], P('tok', 'ch'), may hold values from -0.1875 to 0.1875
- ch_in_bias: float32 [6144], P('ch'), may hold values from -3 to 3
- ch_out_weight: float32 [6144, 1024], P('ch', 'tok'), may hold values from -0.078125 to 0.078125
Outputs:
- block_out: float32 [16384, 1024], P('tok', 'ch')
All inputs are finite; a program needn't handle non-finite values.
Results may differ from a plain program's by a relative error of at most 0.000086.
Values sent between devices are 32-bit elements; how exact they have to be, the bound alone decides.
No kernel may reach another device: no remote copies, remote signals or barrier semaphores. Data moves between devices by JAX's collectives and lax.ppermute only.
A program may use at most 128 MiB of HBM per device.

v0:
```python
import functools

import jax
import jax.numpy as jnp
from jax import lax
from jax.experimental import pallas as pl
from jax.experimental.pallas import tpu as pltpu
from jax.sharding import PartitionSpec as P

epsilon = 1e-05
grant = 255 * 1024 * 256


light = pl.CostEstimate(flops=0, bytes_accessed=0, transcendentals=0)


def empty_kernel(*refs):
    pass


def fence(*values):
    anywhere = [pl.BlockSpec(memory_space=pl.ANY)] * len(values)
    return pl.pallas_call(
        empty_kernel,
        in_specs=anywhere,
        out_specs=anywhere,
        out_shape=[jax.ShapeDtypeStruct(value.shape, value.dtype) for value in values],
        input_output_aliases={n: n for n in range(len(values))},
        compiler_params=pltpu.CompilerParams(vmem_limit_bytes=grant),
        cost_estimate=light,
        name="fence",
    )(*values)


def halves(value):
    high = value.astype(jnp.bfloat16)
    return high, (value - high.astype(jnp.float32)).astype(jnp.bfloat16)


def three_pass(left, right):
    def product(a, b):
        return jnp.dot(a, b, preferred_element_type=jnp.float32)

    return product(left[0], right[0]) + (product(left[0], right[1]) + product(left[1], right[0]))


def column_norm(values, gain):
    centre = jnp.mean(values, axis=0, keepdims=True)
    centred = values - centre
    spread = jnp.mean(centred * centred, axis=0, keepdims=True)
    return centred * lax.rsqrt(spread + epsilon) * gain


def tile_of(size):
    return 256 if size % 256 == 0 else size


class Grid:
    def __init__(self, tok, ch):
        self.tok, self.ch, self.deep = tok, ch, tok // 4
        self.keys = [(c, b, a) for b in range(2) for a in range(2) for c in range(self.deep)]

    def index(self, z, y, x):
        return (z * 2 + y) * 2 + x

    def place(self, chip):
        return chip // 4, chip // 2 % 2, chip % 2

    def move(self, value, dz=0, dy=0, dx=0):
        pairs = []
        for chip in range(self.tok):
            z, y, x = self.place(chip)
            pairs.append((chip, self.index((z + dz) % self.deep, (y + dy) % 2, (x + dx) % 2)))
        return lax.ppermute(value, "tok", pairs)

    def to_core(self, value, step):
        return lax.ppermute(value, "ch", [(core, (core + step) % self.ch) for core in range(self.ch)])

    def line(self, own, arrived):
        return [own] + list(arrived)[::-1]

    def segments(self, orders, rows):
        where = {key: (n, m * rows) for n, order in enumerate(orders) for m, key in enumerate(order)}
        groups = []
        for start in range(0, len(self.keys), self.deep):
            group = []
            for key in self.keys[start : start + self.deep]:
                piece, row = where[key]
                if group and group[-1][0] == piece and group[-1][1] + group[-1][2] == row:
                    group[-1] = piece, group[-1][1], group[-1][2] + rows
                else:
                    group.append((piece, row, rows))
            groups.append(group)
        return groups


def block_starts(grid, place_ref, rows, per_core):
    z, y, x, core = (place_ref[n] for n in range(4))
    starts = []
    for c, b, a in grid.keys:
        owner = grid.index(lax.rem(z + c, grid.deep), lax.rem(y + b, 2), lax.rem(x + a, 2))
        half = lax.rem(lax.div(owner, per_core) + grid.ch - core, grid.ch)
        starts.append(pl.multiple_of((half * per_core + lax.rem(owner, per_core)) * rows, rows))
    return starts


def norm_one_kernel(grid, rows, per_core, place_ref, gain_ref, *refs):
    sources, (fields_ref, high_ref, low_ref, raw, ready) = refs[: grid.ch], refs[grid.ch :]
    values = jnp.concatenate([ref[...].T for ref in sources], axis=0)
    raw[...] = values
    ready[...] = column_norm(values, gain_ref[...])
    for n, start in enumerate(block_starts(grid, place_ref, rows, per_core)):
        target = slice(n * rows, (n + 1) * rows)
        fields_ref[target, :] = raw[pl.ds(start, rows), :]
        high_ref[target, :], low_ref[target, :] = halves(ready[pl.ds(start, rows), :])


def norm_one(grid, place, gain, sources, per_core):
    height, width = sources[0].shape
    channels = width * grid.ch
    tile = tile_of(height)
    whole = pl.BlockSpec((channels, tile), lambda n, place: (0, n))
    return pl.pallas_call(
        functools.partial(norm_one_kernel, grid, channels // grid.tok, per_core),
        grid_spec=pltpu.PrefetchScalarGridSpec(
            num_scalar_prefetch=1,
            grid=(height // tile,),
            in_specs=[pl.BlockSpec((channels, 1), lambda n, place: (0, 0))]
            + [pl.BlockSpec((tile, width), lambda n, place: (n, 0))] * grid.ch,
            out_specs=[whole] * 3,
            scratch_shapes=[pltpu.VMEM((channels, tile), jnp.float32)] * 2,
        ),
        out_shape=[
            jax.ShapeDtypeStruct((channels, height), kind) for kind in (jnp.float32, jnp.bfloat16, jnp.bfloat16)
        ],
        compiler_params=pltpu.CompilerParams(vmem_limit_bytes=grant),
        cost_estimate=light,
        name="norm_one",
    )(place, gain, *sources)


def mix_kernel(high_one, high_two, low_one, low_two, weight_ref, out_ref):
    normed = join([high_one[...], high_two[...]]), join([low_one[...], low_two[...]])
    out_ref[...] = three_pass(normed, halves(weight_ref[...].T))


def mix(high, low, weight, part, quarters):
    channels, height = high.shape
    units = weight.shape[0] // 2
    tile = tile_of(units)
    picked = [pl.BlockSpec((channels // 4, height), lambda n, q=q: (q, 0)) for q in quarters]
    return pl.pallas_call(
        mix_kernel,
        grid=(units // tile,),
        in_specs=picked * 2 + [pl.BlockSpec((tile, height), lambda n: (n + part * (units // tile), 0))],
        out_specs=pl.BlockSpec((channels // 2, tile), lambda n: (0, n)),
        out_shape=jax.ShapeDtypeStruct((channels // 2, units), jnp.float32),
        compiler_params=pltpu.CompilerParams(vmem_limit_bytes=grant),
        cost_estimate=light,
        name="mix",
    )(high, high, low, low, weight)


def stack_kernel(count, parts, *refs):
    for out_ref, (top, bottom, left, right) in zip(refs[count:], parts):
        for n, ref in enumerate(refs[:count]):
            out_ref[n * (bottom - top) : (n + 1) * (bottom - top), :] = ref[top:bottom, left:right]


def stack(values, parts):
    shapes = [(len(values) * (bottom - top), right - left) for top, bottom, left, right in parts]
    return pl.pallas_call(
        functools.partial(stack_kernel, len(values), parts),
        grid=(1,),
        in_specs=[pl.BlockSpec(value.shape, lambda n: (0, 0)) for value in values],
        out_specs=[pl.BlockSpec(shape, lambda n: (0, 0)) for shape in shapes],
        out_shape=[jax.ShapeDtypeStruct(shape, jnp.float32) for shape in shapes],
        compiler_params=pltpu.CompilerParams(vmem_limit_bytes=grant),
        cost_estimate=light,
        name="stack",
    )(*values)


def halve_kernel(kept_a, sent_a, kept_b, sent_b, *outs):
    for kept, sent, (top, bottom) in ((kept_a, sent_a, outs[:2]), (kept_b, sent_b, outs[2:])):
        total = kept[...] + sent[...]
        top[...], bottom[...] = total[: total.shape[0] // 2], total[total.shape[0] // 2 :]


def merge_kernel(kept_a, sent_a, kept_b, sent_b, *outs):
    middle = kept_a.shape[1]
    for n, out_ref in enumerate(outs):
        block = slice(n * out_ref.shape[0], (n + 1) * out_ref.shape[0])
        out_ref[:, :middle] = kept_a[block, :] + sent_a[block, :]
        out_ref[:, middle:] = kept_b[block, :] + sent_b[block, :]


def sums(kernel, values, count, shape):
    return pl.pallas_call(
        kernel,
        grid=(1,),
        in_specs=[pl.BlockSpec(value.shape, lambda n: (0, 0)) for value in values],
        out_specs=[pl.BlockSpec(shape, lambda n: (0, 0))] * count,
        out_shape=[jax.ShapeDtypeStruct(shape, jnp.float32)] * count,
        compiler_params=pltpu.CompilerParams(vmem_limit_bytes=grant),
        cost_estimate=light,
        name="sums",
    )(*values)


def project_kernel(rows, places, weight_ref, *refs):
    pieces, earlier, (out_ref, active_high, active_low) = refs[:4], refs[4:-3], refs[-3:]
    middle = pieces[0].shape[1]

    @pl.when(pl.program_id(0) == 0)
    def _():
        for n, piece in enumerate(pieces):
            active_high[n * rows : (n + 1) * rows, :], active_low[n * rows : (n + 1) * rows, :] = halves(piece[...])

    high, low = halves(weight_ref[...].T)
    sums = []
    for part in range(2):
        taken, units = slice(part * 2 * rows, (part + 1) * 2 * rows), slice(part * middle, (part + 1) * middle)
        product = three_pass((active_high[taken, :], active_low[taken, :]), (high[units, :], low[units, :]))
        sums += [product[:rows], product[rows:]]
    for group in range(out_ref.shape[0] // rows):
        target = slice(group * rows, (group + 1) * rows)
        terms = [value for value, place in zip(sums, places) if place == group]
        terms += [ref[target, :] for ref in earlier if group < ref.shape[0] // rows]
        out_ref[target, :] = functools.reduce(lambda a, b: a + b, terms)


def project(weight, pieces, places, groups, earlier=()):
    width, units = weight.shape
    rows = pieces[0].shape[0]
    tile = tile_of(width)
    return pl.pallas_call(
        functools.partial(project_kernel, rows, places),
        grid=(width // tile,),
        in_specs=[pl.BlockSpec((tile, units), lambda n: (n, 0))]
        + [pl.BlockSpec(piece.shape, lambda n: (0, 0)) for piece in pieces]
        + [pl.BlockSpec((value.shape[0], tile), lambda n: (0, n)) for value in earlier],
        out_specs=pl.BlockSpec((groups * rows, tile), lambda n: (0, n)),
        out_shape=jax.ShapeDtypeStruct((groups * rows, width), jnp.float32),
        scratch_shapes=[pltpu.VMEM((4 * rows, units // 2), jnp.bfloat16)] * 2,
        compiler_params=pltpu.CompilerParams(vmem_limit_bytes=grant),
        cost_estimate=light,
        name="project",
    )(weight, *pieces, *earlier)


def norm_two_kernel(grid, rows, per_core, place_ref, gain_ref, fields_ref, *refs):
    terms, (mixed_ref, high_ref, low_ref) = refs[:-3], refs[-3:]
    starts = block_starts(grid, place_ref, rows, per_core)
    gain = jnp.concatenate([gain_ref[pl.ds(start, rows), :] for start in starts], axis=0)
    total = terms[0][...]
    for ref in terms[1:]:
        total = total + ref[...]
    mixed = fields_ref[...] + total
    mixed_ref[...] = mixed
    high_ref[...], low_ref[...] = halves(column_norm(mixed, gain))


def norm_two(grid, place, gain, fields, terms, per_core):
    channels, width = fields.shape
    tile = tile_of(width)
    whole = pl.BlockSpec((channels, tile), lambda n, place: (0, n))
    return pl.pallas_call(
        functools.partial(norm_two_kernel, grid, channels // grid.tok, per_core),
        grid_spec=pltpu.PrefetchScalarGridSpec(
            num_scalar_prefetch=1,
            grid=(width // tile,),
            in_specs=[pl.BlockSpec((channels, 1), lambda n, place: (0, 0))] + [whole] * (1 + len(terms)),
            out_specs=[whole] * 3,
        ),
        out_shape=[
            jax.ShapeDtypeStruct((channels, width), kind) for kind in (jnp.float32, jnp.bfloat16, jnp.bfloat16)
        ],
        compiler_params=pltpu.CompilerParams(vmem_limit_bytes=grant),
        cost_estimate=light,
        name="norm_two",
    )(place, gain, fields, *terms)


def expand_kernel(groups, count, high_ref, low_ref, bias_ref, *refs):
    pieces, (out_high, out_low, weight_high, weight_low) = refs[:count], refs[count:]

    @pl.when(pl.program_id(0) == 0)
    def _():
        column = 0
        for group in groups:
            value = jnp.concatenate([pieces[n][start : start + rows, :] for n, start, rows in group], axis=0)
            columns = slice(column, column + value.shape[0])
            weight_high[:, columns], weight_low[:, columns] = halves(value.T)
            column += value.shape[0]

    total = three_pass((weight_high[...], weight_low[...]), (high_ref[...], low_ref[...])) + bias_ref[...]
    active = 0.5 * total * (1.0 + lax.erf(total * 0.7071067811865476))
    out_high[...], out_low[...] = halves(active)


def expand(high, low, bias, pieces, groups):
    depth, width = high.shape
    units = pieces[0].shape[1]
    tile = tile_of(width)
    normed = pl.BlockSpec((depth, tile), lambda n: (0, n))
    return pl.pallas_call(
        functools.partial(expand_kernel, groups, len(pieces)),
        grid=(width // tile,),
        in_specs=[normed, normed, pl.BlockSpec((units, 1), lambda n: (0, 0))]
        + [pl.BlockSpec(piece.shape, lambda n: (0, 0)) for piece in pieces],
        out_specs=[pl.BlockSpec((units, tile), lambda n: (0, n))] * 2,
        out_shape=[jax.ShapeDtypeStruct((units, width), jnp.bfloat16)] * 2,
        scratch_shapes=[pltpu.VMEM((units, depth), jnp.bfloat16)] * 2,
        compiler_params=pltpu.CompilerParams(vmem_limit_bytes=grant),
        cost_estimate=light,
        name="expand",
    )(high, low, bias, *pieces)


def reduce_kernel(groups, count, first, spread, *refs):
    if spread:
        place_ref, refs = refs[0], refs[1:]
    (high_ref, low_ref), pieces, refs = refs[:2], refs[2 : 2 + count], refs[2 + count :]
    if not first:
        start_ref, refs = refs[0], refs[1:]
    if spread:
        mixed_ref, refs = refs[0], refs[1:]
    outs, (weight_high, weight_low) = refs[:-2], refs[-2:]

    @pl.when(pl.program_id(0) == 0)
    def _():
        row = 0
        for group in groups:
            for piece, start, rows in group:
                high, low = halves(pieces[piece][start : start + rows, :])
                weight_high[row : row + rows, :] = high
                weight_low[row : row + rows, :] = low
                row += rows

    total = three_pass((weight_high[...], weight_low[...]), (high_ref[...], low_ref[...]))
    if not first:
        total = start_ref[...] + total
    if not spread:
        outs[0][...] = total
        return
    grid, rows, per_core = spread
    for n, start in enumerate(block_starts(grid, place_ref, rows, per_core)):
        block = slice(n * rows, (n + 1) * rows)
        row = pl.multiple_of(lax.rem(start, per_core * rows), rows)
        step = lax.div(start, per_core * rows)
        for core, out_ref in enumerate(outs):
            value = total[block] + mixed_ref[block, :] if core == 0 else total[block]

            @pl.when(step == core)
            def _():
                out_ref[pl.ds(row, rows), :] = value


def reduce(high, low, pieces, groups, start, spread=None, place=None, mixed=None):
    units, width = high.shape
    rows = sum(piece.shape[0] for piece in pieces)
    tile = tile_of(width)
    hidden = pl.BlockSpec((units, tile), lambda n, *_: (0, n))
    total = pl.BlockSpec((rows, tile), lambda n, *_: (0, n))
    first = start is None
    outs = spread[0].ch if spread else 1
    return pl.pallas_call(
        functools.partial(reduce_kernel, groups, len(pieces), first, spread),
        grid_spec=pltpu.PrefetchScalarGridSpec(
            num_scalar_prefetch=1 if spread else 0,
            grid=(width // tile,),
            in_specs=[hidden, hidden]
            + [pl.BlockSpec(piece.shape, lambda n, *_: (0, 0)) for piece in pieces]
            + [total] * ((not first) + (mixed is not None)),
            out_specs=[pl.BlockSpec((rows // outs, tile), lambda n, *_: (0, n))] * outs,
            scratch_shapes=[pltpu.VMEM((rows, units), jnp.bfloat16)] * 2,
        ),
        out_shape=[jax.ShapeDtypeStruct((rows // outs, width), jnp.float32)] * outs,
        compiler_params=pltpu.CompilerParams(vmem_limit_bytes=grant),
        cost_estimate=light,
        name="reduce",
    )(*([place] if spread else []), high, low, *pieces, *([] if first else [start]), *([mixed] if spread else []))


def finish_kernel(*refs):
    total = refs[0][...]
    for ref in refs[1:-1]:
        total = total + ref[...]
    refs[-1][...] = total.T


def finish(values):
    channels, width = values[0].shape
    tile = tile_of(width)
    return pl.pallas_call(
        finish_kernel,
        grid=(width // tile,),
        in_specs=[pl.BlockSpec((channels, tile), lambda n: (0, n))] * len(values),
        out_specs=pl.BlockSpec((tile, channels), lambda n: (n, 0)),
        out_shape=jax.ShapeDtypeStruct((width, channels), jnp.float32),
        compiler_params=pltpu.CompilerParams(vmem_limit_bytes=grant),
        cost_estimate=light,
        name="finish",
    )(*values)


def join(values, axis=0):
    return jnp.concatenate(list(values), axis=axis)


def shards(
    grid,
    fields,
    gain_one,
    tok_in_weight,
    tok_in_bias,
    tok_out_weight,
    gain_two,
    ch_in_weight,
    ch_in_bias,
    ch_out_weight,
):
    ch, deep, move = grid.ch, grid.deep, grid.move
    width = fields.shape[1]
    rows = ch * width // grid.tok
    per_core = width // rows
    core = lax.axis_index("ch")
    z, y, x = grid.place(lax.axis_index("tok"))
    place = jnp.stack([z, y, x, core]).astype(jnp.int32)

    def keys(outer, inner, low=0, high=2):
        fixed = {"y": range(2), "x": range(2), "z": range(deep), outer: range(low, high)}
        names = outer + inner
        return [
            (dict(zip(names, key))["z"], dict(zip(names, key))["y"], dict(zip(names, key))["x"])
            for key in ((o, m, i) for o in fixed[names[0]] for m in fixed[names[1]] for i in fixed[names[2]])
        ]

    def lone(outer, inner):
        return [keys(outer, inner, n, n + 1) for n in range(deep if outer == "z" else 2)]

    whole = keys("z", "yx", 0, deep)
    corner = {(b, a): [key for key in whole if key[1:] == (b, a)] for b in range(2) for a in range(2)}
    y_last = grid.segments([corner[0, 0], corner[0, 1], corner[1, 0], corner[1, 1]], rows)
    x_last = grid.segments([corner[0, 0], corner[1, 0], corner[0, 1], corner[1, 1]], rows)
    y_last_pair = grid.segments([corner[0, 0] + corner[0, 1], corner[1, 0] + corner[1, 1]], rows)
    x_last_pair = grid.segments([corner[0, 0] + corner[1, 0], corner[0, 1] + corner[1, 1]], rows)
    z_after_xy = grid.segments(lone("z", "yx"), rows)
    z_after_yx = grid.segments(lone("z", "xy"), rows)

    units = ch_in_weight.shape[1]
    ends = [units * n // 3 for n in range(4)]
    spans = list(zip(ends, ends[1:]))
    out_rows = ch_out_weight.T

    others = [grid.to_core(fields, ch - step) for step in range(1, ch)]
    pair_gain = jnp.stack([gain_one, gain_two])
    gains = join([pair_gain] + [grid.to_core(pair_gain, ch - step) for step in range(1, ch)], 1).T
    own = join([ch_in_weight[:, : ends[2]], out_rows[:, : ends[2]]])
    in_last, out_last = ch_in_weight[:, ends[2] :], out_rows[:, ends[2] :]
    ring = [move(own, dz=1)]
    in_step, out_step = move(in_last, dx=1), move(out_last, dy=1)
    full, high, low = norm_one(grid, place, gains[:, :1], [fields] + others, per_core)
    high, in_step, out_step = fence(high, in_step, out_step)
    in_last, out_last = join([in_last, in_step]), join([out_last, out_step])
    in_step, out_step = move(in_last, dy=1), move(out_last, dx=1)

    middle = tok_in_weight.shape[0] // 2
    quarter = deep * rows
    sent_a = mix(high, low, tok_in_weight, 0, (1, 3))
    sent_b = mix(high, low, tok_in_weight, 1, (2, 3))
    sent_a, sent_b, ring[0] = fence(sent_a, sent_b, ring[0])
    sent_a, sent_b = move(sent_a, dx=1), move(sent_b, dy=1)
    ring.append(move(ring[0], dz=1))
    kept_a = mix(high, low, tok_in_weight, 0, (0, 2))
    kept_b = mix(high, low, tok_in_weight, 1, (0, 1))
    biases = [ch_in_bias[a:b, None] for a, b in spans]
    sent_a, sent_b, kept_a, kept_b, in_step, out_step, ring[1], *biases = fence(
        sent_a, sent_b, kept_a, kept_b, in_step, out_step, ring[1], *biases
    )
    kept_a, sent_a, kept_b, sent_b = sums(halve_kernel, [kept_a, sent_a, kept_b, sent_b], 4, (quarter, middle))
    sent_a, sent_b = move(sent_a, dy=1), move(sent_b, dx=1)
    in_last, out_last = join([in_last, in_step]), join([out_last, out_step])
    for _ in range(2, deep - 1):
        ring.append(move(ring[-1], dz=1))
    sent_a, sent_b, in_last, out_last, ring[-1] = fence(sent_a, sent_b, in_last, out_last, ring[-1])

    partial = sums(merge_kernel, [kept_a, sent_a, kept_b, sent_b], deep, (rows, 2 * middle))
    total = partial[deep - 1]
    for step in range(2, deep + 1):
        total = move(total, dz=1) + partial[deep - step]
    lines = stack(grid.line(own, ring), [(r, r + rows, a, b) for r in (0, rows) for a, b in spans[:2]])
    first, second = [[line] for line in lines[:2]], [[line] for line in lines[2:]]
    first_step = [move(first[0][0], dx=1), move(first[1][0], dy=1)]
    activated = jax.nn.gelu(total + tok_in_bias[None, :], approximate=False)

    activated, *lines = fence(activated, first[0][0], first[1][0], *first_step)
    first = [[lines[0], lines[2]], [lines[1], lines[3]]]
    ring = []
    for step in range(1, deep):
        ring.append(move(ring[-1] if ring else activated, dz=1))
    first_step = [move(value, dy=1) for value in first[0]] + [move(value, dx=1) for value in first[1]]
    ring[-1], in_last, *first_step = fence(ring[-1], in_last, *first_step)
    first = [first[0] + first_step[:2], first[1] + first_step[2:]]

    active_a, active_b = stack(grid.line(activated, ring), [(0, rows, 0, middle), (0, rows, middle, 2 * middle)])
    step_a, step_b = move(active_a, dy=1), move(active_b, dx=1)
    in_ring = [move(in_last, dz=1)]
    step_a, step_b, in_ring[0] = fence(step_a, step_b, in_ring[0])
    arrived = [move(active_a, dx=1), move(step_a, dx=1), move(active_b, dy=1), move(step_b, dy=1)]
    in_ring.append(move(in_ring[0], dz=1))
    terms = project(tok_out_weight, [active_a, step_a, active_b, step_b], (0, 2, 0, 1), 3)
    terms, in_ring[1], *arrived = fence(terms, in_ring[1], *arrived)

    for _ in range(2, deep - 1):
        in_ring.append(move(in_ring[-1], dz=1))
    second_step = [move(second[0][0], dy=1), move(second[1][0], dx=1)]
    terms = project(tok_out_weight, arrived, (1, 3, 2, 3), 4, [terms])
    terms = [terms] + [grid.to_core(terms, step) for step in range(1, ch)]
    mixed, high, low = norm_two(grid, place, gains[:, 1:], full, terms, per_core)

    high, out_last, in_ring[-1], *second_step = fence(high, out_last, in_ring[-1], *second_step)
    second = [stack([line[0], step], [(0, quarter, 0, step.shape[1])])[0] for line, step in zip(second, second_step)]
    second_step = [move(second[0], dx=1), move(second[1], dy=1)]
    out_ring = [move(out_last, dz=1)]
    hidden = [
        expand(high, low, biases[0], first[0], y_last),
        expand(high, low, biases[1], first[1], x_last),
    ]
    hidden_high, out_ring[0] = fence(hidden[1][0], out_ring[0])
    hidden[1] = hidden_high, hidden[1][1]
    out_ring.append(move(out_ring[0], dz=1))
    hidden.append(expand(high, low, biases[2], grid.line(in_last, in_ring), z_after_xy))
    hidden_high, out_ring[1] = fence(hidden[2][0], out_ring[1])
    hidden[2] = hidden_high, hidden[2][1]
    for _ in range(2, deep - 1):
        out_ring.append(move(out_ring[-1], dz=1))
    (result,) = reduce(*hidden[0], [second[0], second_step[0]], x_last_pair, None)
    (result,) = reduce(*hidden[1], [second[1], second_step[1]], y_last_pair, result)
    spread = grid, rows, per_core
    parts = reduce(*hidden[2], grid.line(out_last, out_ring), z_after_yx, result, spread, place, mixed)
    return finish([parts[0]] + [grid.to_core(part, step) for step, part in enumerate(parts) if step])


def solution(mesh):
    grid = Grid(mesh.shape["tok"], mesh.shape["ch"])
    in_specs = (
        P("tok", "ch"),
        P("ch"),
        P("ch", "tok"),
        P("ch"),
        P("tok", "ch"),
        P("ch"),
        P("tok", "ch"),
        P("ch"),
        P("ch", "tok"),
    )

    def block(*arrays):
        return shards(grid, *arrays)

    return jax.shard_map(block, mesh=mesh, in_specs=in_specs, out_specs=P("tok", "ch"), check_vma=False)
```

profile of v0, /device:TPU:0, one launch (start us, length us, event | category | flops | bytes accessed | tf_op | source)
XLA Modules:
  0.0 399.2 jit_solution(10775599065790646360)
XLA Ops:
  13.0 8.0 %norm_one.1 = (f32[1024,1024]{1,0:T(8,128)}, bf16[1024,1024]{1,0:T(8,128)(2,1)}, bf16[1024,1024]{1,0:T(8,128)(2,1)}) custom-call(s32[4]{0:T(128)} %pad_add_fusion.place_ref.refs_0_, f32[1024,1]{1,0:T(8,128)} %get-tuple-element.161.gain_ref, f32[1024,512]{1,0:T(8,128)} %refs_0_.1, f32[1024,512]{1,0:T(8,128)} %collective-permute-done.1.refs_1_), custom_call_target="tpu_custom_call" | custom-call | tf_op jit(solution)/shard_map/norm_one/pallas_call | solution.py:123
  21.0 6.4 %mix.5.refs_1_ = f32[512,768]{1,0:T(8,128)} custom-call(bf16[1024,1024]{1,0:T(8,128)(2,1)} %get-tuple-element.85.high_one.high_two, bf16[1024,1024]{1,0:T(8,128)(2,1)} %get-tuple-element.85.high_one.high_two, bf16[1024,1024]{1,0:T(8,128)(2,1)} %get-tuple-element.86.low_one.low_two, bf16[1024,1024]{1,0:T(8,128)(2,1)} %get-tuple-element.86.low_one.low_two, ...), custom_call_target="tpu_custom_call" | custom-call | tf_op jit(solution)/shard_map/mix/pallas_call | solution.py:152
  27.4 6.4 %mix.4.refs_0_ = f32[512,768]{1,0:T(8,128)} custom-call(bf16[1024,1024]{1,0:T(8,128)(2,1)} %get-tuple-element.85.high_one.high_two, bf16[1024,1024]{1,0:T(8,128)(2,1)} %get-tuple-element.85.high_one.high_two, bf16[1024,1024]{1,0:T(8,128)(2,1)} %get-tuple-element.86.low_one.low_two, bf16[1024,1024]{1,0:T(8,128)(2,1)} %get-tuple-element.86.low_one.low_two, ...), custom_call_target="tpu_custom_call" | custom-call | tf_op jit(solution)/shard_map/mix/pallas_call | solution.py:152
  46.5 6.4 %mix.6.refs_2_ = f32[512,768]{1,0:T(8,128)} custom-call(bf16[1024,1024]{1,0:T(8,128)(2,1)} %get-tuple-element.85.high_one.high_two, bf16[1024,1024]{1,0:T(8,128)(2,1)} %get-tuple-element.85.high_one.high_two, bf16[1024,1024]{1,0:T(8,128)(2,1)} %get-tuple-element.86.low_one.low_two, bf16[1024,1024]{1,0:T(8,128)(2,1)} %get-tuple-element.86.low_one.low_two, ...), custom_call_target="tpu_custom_call" | custom-call | tf_op jit(solution)/shard_map/mix/pallas_call | solution.py:152
  52.9 6.4 %mix.7.refs_3_ = f32[512,768]{1,0:T(8,128)} custom-call(bf16[1024,1024]{1,0:T(8,128)(2,1)} %get-tuple-element.85.high_one.high_two, bf16[1024,1024]{1,0:T(8,128)(2,1)} %get-tuple-element.85.high_one.high_two, bf16[1024,1024]{1,0:T(8,128)(2,1)} %get-tuple-element.86.low_one.low_two, bf16[1024,1024]{1,0:T(8,128)(2,1)} %get-tuple-element.86.low_one.low_two, ...), custom_call_target="tpu_custom_call" | custom-call | tf_op jit(solution)/shard_map/mix/pallas_call | solution.py:152
  59.3 22.5 %collective-permute-done.7.refs_4_ = f32[128,1024]{1,0:T(8,128)} collective-permute-done((f32[128,1024]{1,0:T(8,128)}, f32[128,1024]{1,0:T(8,128)}, u32[]{:S(2)}, u32[]{:S(2)}) %collective-permute-start.7) | collective-permute-done | bytes 524320 | tf_op jit(solution)/shard_map/ppermute | solution.py:74
  83.5 4.6 %sums.2 = (f32[256,768]{1,0:T(8,128)}, f32[256,768]{1,0:T(8,128)}, f32[256,768]{1,0:T(8,128)}, f32[256,768]{1,0:T(8,128)}) custom-call(f32[512,768]{1,0:T(8,128)} %get-tuple-element.92.kept_a, f32[512,768]{1,0:T(8,128)} %get-tuple-element.93.sent_a, f32[512,768]{1,0:T(8,128)} %get-tuple-element.94.kept_b, f32[512,768]{1,0:T(8,128)} %get-tuple-element.95.sent_b), custom_call_target="tpu_custom_call" | custom-call | tf_op jit(solution)/shard_map/sums/pallas_call | solution.py:199
  93.2 13.0 %collective-permute-done.10.refs_0_ = f32[256,768]{1,0:T(8,128)} collective-permute-done((f32[256,768]{1,0:T(8,128)}, f32[256,768]{1,0:T(8,128)}, u32[]{:S(2)}, u32[]{:S(2)}) %collective-permute-start.10) | collective-permute-done | bytes 786464 | tf_op jit(solution)/shard_map/ppermute | solution.py:74
  111.0 10.4 %collective-permute-done.13 = f32[64,1536]{1,0:T(8,128)S(1)} collective-permute-done((f32[64,1536]{1,0:T(8,128)}, f32[64,1536]{1,0:T(8,128)S(1)}, u32[]{:S(2)}, u32[]{:S(2)}) %collective-permute-start.13) | collective-permute-done | bytes 393248 | tf_op jit(solution)/shard_map/ppermute | solution.py:74
  134.3 9.6 %collective-permute-done.15 = f32[64,1536]{1,0:T(8,128)S(1)} collective-permute-done((f32[64,1536]{1,0:T(8,128)S(1)}, f32[64,1536]{1,0:T(8,128)S(1)}, u32[]{:S(2)}, u32[]{:S(2)}) %collective-permute-start.15) | collective-permute-done | bytes 393248 | tf_op jit(solution)/shard_map/ppermute | solution.py:74
  156.2 7.6 %collective-permute-done.18.refs_3_ = f32[64,1536]{1,0:T(8,128)S(1)} collective-permute-done((f32[64,1536]{1,0:T(8,128)}, f32[64,1536]{1,0:T(8,128)S(1)}, u32[]{:S(2)}, u32[]{:S(2)}) %collective-permute-start.18) | collective-permute-done | bytes 393248 | tf_op jit(solution)/shard_map/ppermute | solution.py:74
  164.6 12.8 %collective-permute-done.19.refs_2_ = f32[64,1536]{1,0:T(8,128)S(1)} collective-permute-done((f32[64,1536]{1,0:T(8,128)S(1)}, f32[64,1536]{1,0:T(8,128)S(1)}, u32[]{:S(2)}, u32[]{:S(2)}) %collective-permute-start.19) | collective-permute-done | bytes 393248 | tf_op jit(solution)/shard_map/ppermute | solution.py:74
  178.5 17.0 %collective-permute-done.22.refs_3_ = f32[256,1024]{1,0:T(8,128)} collective-permute-done((f32[256,1024]{1,0:T(8,128)}, f32[256,1024]{1,0:T(8,128)}, u32[]{:S(2)}, u32[]{:S(2)}) %collective-permute-start.22) | collective-permute-done | bytes 1048608 | tf_op jit(solution)/shard_map/ppermute | solution.py:74
  199.5 13.2 %collective-permute-done.25.refs_0_ = f32[256,768]{1,0:T(8,128)} collective-permute-done((f32[256,768]{1,0:T(8,128)}, f32[256,768]{1,0:T(8,128)}, u32[]{:S(2)}, u32[]{:S(2)}) %collective-permute-start.25) | collective-permute-done | bytes 786464 | tf_op jit(solution)/shard_map/ppermute | solution.py:74
  213.0 6.0 %collective-permute-done.27.refs_2_ = f32[256,1024]{1,0:T(8,128)} collective-permute-done((f32[256,1024]{1,0:T(8,128)}, f32[256,1024]{1,0:T(8,128)}, u32[]{:S(2)}, u32[]{:S(2)}) %collective-permute-start.27) | collective-permute-done | bytes 1048608 | tf_op jit(solution)/shard_map/ppermute | solution.py:74
  223.0 10.2 %project.2.refs_0_ = f32[768,1024]{1,0:T(8,128)} custom-call(f32[1024,1536]{1,0:T(8,128)} %weight_ref.11, f32[256,768]{1,0:T(8,128)} %get-tuple-element.119.refs_0_, f32[256,768]{1,0:T(8,128)} %get-tuple-element.122.refs_1_, f32[256,768]{1,0:T(8,128)} %get-tuple-element.120.refs_2_, f32[256,768]{1,0:T(8,128)} %get-tuple-element.123.refs_3_), custom_call_target="tpu_custom_call" | custom-call | tf_op jit(solution)/shard_map/project/pallas_call | solution.py:237
  233.2 6.2 %collective-permute-done.29.refs_2_ = f32[256,768]{1,0:T(8,128)} collective-permute-done((f32[256,768]{1,0:T(8,128)}, f32[256,768]{1,0:T(8,128)}, u32[]{:S(2)}, u32[]{:S(2)}) %collective-permute-start.29) | collective-permute-done | bytes 786464 | tf_op jit(solution)/shard_map/ppermute | solution.py:74
  239.9 7.9 %collective-permute-done.30.refs_3_ = f32[256,768]{1,0:T(8,128)} collective-permute-done((f32[256,768]{1,0:T(8,128)}, f32[256,768]{1,0:T(8,128)}, u32[]{:S(2)}, u32[]{:S(2)}) %collective-permute-start.30) | collective-permute-done | bytes 786464 | tf_op jit(solution)/shard_map/ppermute | solution.py:74
  248.3 10.9 %project.3.refs_0_ = f32[1024,1024]{1,0:T(8,128)} custom-call(f32[1024,1536]{1,0:T(8,128)} %weight_ref.11, f32[256,768]{1,0:T(8,128)} %get-tuple-element.125.refs_0_, f32[256,768]{1,0:T(8,128)} %get-tuple-element.126.refs_1_, f32[256,768]{1,0:T(8,128)} %get-tuple-element.127.refs_2_, f32[256,768]{1,0:T(8,128)} %get-tuple-element.128.refs_3_, ...), custom_call_target="tpu_custom_call" | custom-call | tf_op jit(solution)/shard_map/project/pallas_call | solution.py:237
  261.9 4.9 %collective-permute-done.33.refs_1_ = f32[1024,1024]{1,0:T(8,128)} collective-permute-done((f32[1024,1024]{1,0:T(8,128)}, f32[1024,1024]{1,0:T(8,128)}, u32[]{:S(2)}, u32[]{:S(2)}) %collective-permute-start.33) | collective-permute-done | bytes 4194336 | tf_op jit(solution)/shard_map/ppermute | solution.py:77
  266.8 9.8 %norm_two.1 = (f32[1024,1024]{1,0:T(8,128)}, bf16[1024,1024]{1,0:T(8,128)(2,1)}, bf16[1024,1024]{1,0:T(8,128)(2,1)}) custom-call(s32[4]{0:T(128)} %pad_add_fusion.place_ref.refs_0_, f32[1024,1]{1,0:T(8,128)} %get-tuple-element.162.gain_ref, f32[1024,1024]{1,0:T(8,128)} %get-tuple-element.83.fields_ref, f32[1024,1024]{1,0:T(8,128)} %project.3.refs_0_, ...), custom_call_target="tpu_custom_call" | custom-call | tf_op jit(solution)/shard_map/norm_two/pallas_call | solution.py:268
  276.6 8.6 %collective-permute-done.35.refs_3_ = f32[256,1024]{1,0:T(8,128)} collective-permute-done((f32[256,1024]{1,0:T(8,128)}, f32[256,1024]{1,0:T(8,128)}, u32[]{:S(2)}, u32[]{:S(2)}) %collective-permute-start.35) | collective-permute-done | bytes 1048608 | tf_op jit(solution)/shard_map/ppermute | solution.py:74
  296.4 12.7 %expand.4 = (bf16[1024,1024]{1,0:T(8,128)(2,1)}, bf16[1024,1024]{1,0:T(8,128)(2,1)}) custom-call(bf16[1024,1024]{1,0:T(8,128)(2,1)} %get-tuple-element.135.high_ref, bf16[1024,1024]{1,0:T(8,128)(2,1)} %get-tuple-element.136.low_ref, f32[1024,1]{1,0:T(8,128)} %get-tuple-element.140.bias_ref, f32[256,1024]{1,0:T(8,128)} %get-tuple-element.116.refs_0_, ...), custom_call_target="tpu_custom_call" | custom-call | tf_op jit(solution)/shard_map/expand/pallas_call | solution.py:307
  309.1 5.4 %collective-permute-done.37.refs_1_ = f32[256,1024]{1,0:T(8,128)} collective-permute-done((f32[256,1024]{1,0:T(8,128)}, f32[256,1024]{1,0:T(8,128)}, u32[]{:S(2)}, u32[]{:S(2)}) %collective-permute-start.37) | collective-permute-done | bytes 1048608 | tf_op jit(solution)/shard_map/ppermute | solution.py:74
  314.5 12.7 %expand.3 = (bf16[1024,1024]{1,0:T(8,128)(2,1)}, bf16[1024,1024]{1,0:T(8,128)(2,1)}) custom-call(bf16[1024,1024]{1,0:T(8,128)(2,1)} %get-tuple-element.135.high_ref, bf16[1024,1024]{1,0:T(8,128)(2,1)} %get-tuple-element.136.low_ref, f32[1024,1]{1,0:T(8,128)} %get-tuple-element.137.bias_ref, f32[256,1024]{1,0:T(8,128)} %get-tuple-element.121.refs_0_, ...), custom_call_target="tpu_custom_call" | custom-call | tf_op jit(solution)/shard_map/expand/pallas_call | solution.py:307
  327.1 12.7 %collective-permute-done.38.refs_1_ = f32[256,1024]{1,0:T(8,128)} collective-permute-done((f32[256,1024]{1,0:T(8,128)}, f32[256,1024]{1,0:T(8,128)}, u32[]{:S(2)}, u32[]{:S(2)}) %collective-permute-start.38) | collective-permute-done | bytes 1048608 | tf_op jit(solution)/shard_map/ppermute | solution.py:74
  339.8 12.7 %expand.5 = (bf16[1024,1024]{1,0:T(8,128)(2,1)}, bf16[1024,1024]{1,0:T(8,128)(2,1)}) custom-call(bf16[1024,1024]{1,0:T(8,128)(2,1)} %get-tuple-element.135.high_ref, bf16[1024,1024]{1,0:T(8,128)(2,1)} %get-tuple-element.136.low_ref, f32[1024,1]{1,0:T(8,128)} %get-tuple-element.152.bias_ref, f32[256,1024]{1,0:T(8,128)} %get-tuple-element.114.refs_0_, ...), custom_call_target="tpu_custom_call" | custom-call | tf_op jit(solution)/shard_map/expand/pallas_call | solution.py:307
  352.5 11.4 %reduce.3.refs_4_ = f32[1024,1024]{1,0:T(8,128)} custom-call(bf16[1024,1024]{1,0:T(8,128)(2,1)} %get-tuple-element.155.refs_0_, bf16[1024,1024]{1,0:T(8,128)(2,1)} %get-tuple-element.156.refs_1_, f32[512,1024]{1,0:T(8,128)} %stack.39.refs_2_, f32[512,1024]{1,0:T(8,128)} %collective-permute-done.41.refs_3_), custom_call_target="tpu_custom_call" | custom-call | tf_op jit(solution)/shard_map/reduce/pallas_call | solution.py:368
  363.9 12.1 %reduce.4.refs_7_ = f32[1024,1024]{1,0:T(8,128)} custom-call(bf16[1024,1024]{1,0:T(8,128)(2,1)} %get-tuple-element.149.refs_0_, bf16[1024,1024]{1,0:T(8,128)(2,1)} %get-tuple-element.150.refs_1_, f32[512,1024]{1,0:T(8,128)} %stack.38.refs_2_, f32[512,1024]{1,0:T(8,128)} %collective-permute-done.40.refs_3_, f32[1024,1024]{1,0:T(8,128)} %reduce.3.refs_4_), custom_call_target="tpu_custom_call" | custom-call | tf_op jit(solution)/shard_map/reduce/pallas_call | solution.py:368
  376.0 14.2 %reduce.5 = (f32[512,1024]{1,0:T(8,128)}, f32[512,1024]{1,0:T(8,128)}) custom-call(s32[4]{0:T(128)} %pad_add_fusion.place_ref.refs_0_, bf16[1024,1024]{1,0:T(8,128)(2,1)} %get-tuple-element.146.refs_1_, bf16[1024,1024]{1,0:T(8,128)(2,1)} %get-tuple-element.147.refs_2_, f32[256,1024]{1,0:T(8,128)} %get-tuple-element.144.refs_3_, ...), custom_call_target="tpu_custom_call" | custom-call | tf_op jit(solution)/shard_map/reduce/pallas_call | solution.py:368
  390.2 4.5 %collective-permute-done.42.refs_1_ = f32[512,1024]{1,0:T(8,128)} collective-permute-done((f32[512,1024]{1,0:T(8,128)}, f32[512,1024]{1,0:T(8,128)}, u32[]{:S(2)}, u32[]{:S(2)}) %collective-permute-start.42) | collective-permute-done | bytes 2097184 | tf_op jit(solution)/shard_map/ppermute | solution.py:77
  394.7 4.5 %finish.1 = f32[1024,512]{1,0:T(8,128)} custom-call(f32[512,1024]{1,0:T(8,128)} %get-tuple-element.159.refs_0_, f32[512,1024]{1,0:T(8,128)} %collective-permute-done.42.refs_1_), custom_call_target="tpu_custom_call" | custom-call | tf_op jit(solution)/shard_map/finish/pallas_call | solution.py:396
  (121 shorter events, 87.5 us)
Async XLA Ops:
  2.7 31.2 %collective-permute-start.4 = (f32[128,2048]{1,0:T(8,128)}, f32[128,2048]{1,0:T(8,128)}, u32[]{:S(2)}, u32[]{:S(2)}) collective-permute-start(f32[128,2048]{1,0:T(8,128)} %pad_maximum_fusion.refs_0_), channel_id=1, source_target_pairs={{0,8},{2,10},{4,12},{6,14},{8,16},{10,18},{12,20},{14,22},{16,24},... | collective-permute-start | bytes 3145736 | tf_op jit(solution)/shard_map/ppermute | solution.py:74
  33.8 47.9 %collective-permute-start.5 = (f32[512,768]{1,0:T(8,128)}, f32[512,768]{1,0:T(8,128)}, u32[]{:S(2)}, u32[]{:S(2)}) collective-permute-start(f32[512,768]{1,0:T(8,128)} %get-tuple-element.87), channel_id=1, source_target_pairs={{0,2},{2,0},{4,6},{6,4},{8,10},{10,8},{12,14},{14,12},{16,18},{18,... | collective-permute-start | bytes 4718600 | tf_op jit(solution)/shard_map/ppermute | solution.py:74
  34.4 47.4 %collective-permute-start.6 = (f32[512,768]{1,0:T(8,128)}, f32[512,768]{1,0:T(8,128)}, u32[]{:S(2)}, u32[]{:S(2)}) collective-permute-start(f32[512,768]{1,0:T(8,128)} %get-tuple-element.88), channel_id=1, source_target_pairs={{0,4},{2,6},{4,0},{6,2},{8,12},{10,14},{12,8},{14,10},{16,20},{18,... | collective-permute-start | bytes 4718600 | tf_op jit(solution)/shard_map/ppermute | solution.py:74
  34.9 46.9 %collective-permute-start.9 = (f32[128,2048]{1,0:T(8,128)}, f32[128,2048]{1,0:T(8,128)}, u32[]{:S(2)}, u32[]{:S(2)}) collective-permute-start(f32[128,2048]{1,0:T(8,128)} %get-tuple-element.91.refs_3_), channel_id=1, source_target_pairs={{0,8},{2,10},{4,12},{6,14},{8,16},{10,18},{12,20},{14,22},{16,24},... | collective-permute-start | bytes 3145736 | tf_op jit(solution)/shard_map/ppermute | solution.py:74
  38.4 43.4 %collective-permute-start.7 = (f32[128,1024]{1,0:T(8,128)}, f32[128,1024]{1,0:T(8,128)}, u32[]{:S(2)}, u32[]{:S(2)}) collective-permute-start(f32[128,1024]{1,0:T(8,128)} %pad_maximum_fusion.3), channel_id=1, source_target_pairs={{0,4},{2,6},{4,0},{6,2},{8,12},{10,14},{12,8},{14,10},{16,20},{18,... | collective-permute-start | bytes 1572872 | tf_op jit(solution)/shard_map/ppermute | solution.py:74
  41.8 40.0 %collective-permute-start.8 = (f32[128,1024]{1,0:T(8,128)}, f32[128,1024]{1,0:T(8,128)}, u32[]{:S(2)}, u32[]{:S(2)}) collective-permute-start(f32[128,1024]{1,0:T(8,128)} %pad_maximum_fusion.4), channel_id=1, source_target_pairs={{0,2},{2,0},{4,6},{6,4},{8,10},{10,8},{12,14},{14,12},{16,18},{18,... | collective-permute-start | bytes 1572872 | tf_op jit(solution)/shard_map/ppermute | solution.py:74
  81.8 25.8 %collective-permute-start.12 = (f32[128,2048]{1,0:T(8,128)}, f32[128,2048]{1,0:T(8,128)}, u32[]{:S(2)}, u32[]{:S(2)}) collective-permute-start(f32[128,2048]{1,0:T(8,128)} %get-tuple-element.101.refs_2_), channel_id=1, source_target_pairs={{0,8},{2,10},{4,12},{6,14},{8,16},{10,18},{12,20},{14,22},{16,24},... | collective-permute-start | bytes 3145736 | tf_op jit(solution)/shard_map/ppermute | solution.py:74
  88.0 18.1 %collective-permute-start.10 = (f32[256,768]{1,0:T(8,128)}, f32[256,768]{1,0:T(8,128)}, u32[]{:S(2)}, u32[]{:S(2)}) collective-permute-start(f32[256,768]{1,0:T(8,128)} %get-tuple-element.97), channel_id=1, source_target_pairs={{0,4},{2,6},{4,0},{6,2},{8,12},{10,14},{12,8},{14,10},{16,20},{18,... | collective-permute-start | bytes 2359304 | tf_op jit(solution)/shard_map/ppermute | solution.py:74
  88.5 17.8 %collective-permute-start.11 = (f32[256,768]{1,0:T(8,128)}, f32[256,768]{1,0:T(8,128)}, u32[]{:S(2)}, u32[]{:S(2)}) collective-permute-start(f32[256,768]{1,0:T(8,128)} %get-tuple-element.98), channel_id=1, source_target_pairs={{0,2},{2,0},{4,6},{6,4},{8,10},{10,8},{12,14},{14,12},{16,18},{18,... | collective-permute-start | bytes 2359304 | tf_op jit(solution)/shard_map/ppermute | solution.py:74
  127.4 22.1 %collective-permute-start.16 = (f32[256,1024]{1,0:T(8,128)}, f32[256,1024]{1,0:T(8,128)}, u32[]{:S(2)}, u32[]{:S(2)}) collective-permute-start(f32[256,1024]{1,0:T(8,128)} %get-tuple-element.110.refs_1_), channel_id=1, source_target_pairs={{0,2},{2,0},{4,6},{6,4},{8,10},{10,8},{12,14},{14,12},{16,18},{18,... | collective-permute-start | bytes 3145736 | tf_op jit(solution)/shard_map/ppermute | solution.py:74
  128.8 23.3 %collective-permute-start.17 = (f32[256,1024]{1,0:T(8,128)}, f32[256,1024]{1,0:T(8,128)}, u32[]{:S(2)}, u32[]{:S(2)}) collective-permute-start(f32[256,1024]{1,0:T(8,128)} %get-tuple-element.111.refs_2_), channel_id=1, source_target_pairs={{0,4},{2,6},{4,0},{6,2},{8,12},{10,14},{12,8},{14,10},{16,20},{18,... | collective-permute-start | bytes 3145736 | tf_op jit(solution)/shard_map/ppermute | solution.py:74
  152.1 26.4 %collective-permute-start.21 = (f32[256,1024]{1,0:T(8,128)}, f32[256,1024]{1,0:T(8,128)}, u32[]{:S(2)}, u32[]{:S(2)}) collective-permute-start(f32[256,1024]{1,0:T(8,128)} %get-tuple-element.114.refs_0_), channel_id=1, source_target_pairs={{0,4},{2,6},{4,0},{6,2},{8,12},{10,14},{12,8},{14,10},{16,20},{18,... | collective-permute-start | bytes 3145736 | tf_op jit(solution)/shard_map/ppermute | solution.py:74
  152.6 42.9 %collective-permute-start.22 = (f32[256,1024]{1,0:T(8,128)}, f32[256,1024]{1,0:T(8,128)}, u32[]{:S(2)}, u32[]{:S(2)}) collective-permute-start(f32[256,1024]{1,0:T(8,128)} %get-tuple-element.115.refs_1_), channel_id=1, source_target_pairs={{0,4},{2,6},{4,0},{6,2},{8,12},{10,14},{12,8},{14,10},{16,20},{18,... | collective-permute-start | bytes 3145736 | tf_op jit(solution)/shard_map/ppermute | solution.py:74
  154.1 41.4 %collective-permute-start.23 = (f32[256,1024]{1,0:T(8,128)}, f32[256,1024]{1,0:T(8,128)}, u32[]{:S(2)}, u32[]{:S(2)}) collective-permute-start(f32[256,1024]{1,0:T(8,128)} %get-tuple-element.116.refs_0_), channel_id=1, source_target_pairs={{0,2},{2,0},{4,6},{6,4},{8,10},{10,8},{12,14},{14,12},{16,18},{18,... | collective-permute-start | bytes 3145736 | tf_op jit(solution)/shard_map/ppermute | solution.py:74
  154.8 40.8 %collective-permute-start.24 = (f32[256,1024]{1,0:T(8,128)}, f32[256,1024]{1,0:T(8,128)}, u32[]{:S(2)}, u32[]{:S(2)}) collective-permute-start(f32[256,1024]{1,0:T(8,128)} %get-tuple-element.117.refs_1_), channel_id=1, source_target_pairs={{0,2},{2,0},{4,6},{6,4},{8,10},{10,8},{12,14},{14,12},{16,18},{18,... | collective-permute-start | bytes 3145736 | tf_op jit(solution)/shard_map/ppermute | solution.py:74
  178.1 17.5 %collective-permute-start.20 = (f32[64,1536]{1,0:T(8,128)S(1)}, f32[64,1536]{1,0:T(8,128)}, u32[]{:S(2)}, u32[]{:S(2)}) collective-permute-start(f32[64,1536]{1,0:T(8,128)S(1)} %collective-permute-done.19.refs_2_), channel_id=1, source_target_pairs={{0,8},{2,10},{4,12},{6,14},{8,16},{10,18},{12,20},{14,22},{16,24},... | collective-permute-start | bytes 1179656 | tf_op jit(solution)/shard_map/ppermute | solution.py:74
  195.6 23.4 %collective-permute-start.27 = (f32[256,1024]{1,0:T(8,128)}, f32[256,1024]{1,0:T(8,128)}, u32[]{:S(2)}, u32[]{:S(2)}) collective-permute-start(f32[256,1024]{1,0:T(8,128)} %get-tuple-element.121.refs_0_), channel_id=1, source_target_pairs={{0,8},{2,10},{4,12},{6,14},{8,16},{10,18},{12,20},{14,22},{16,24},... | collective-permute-start | bytes 3145736 | tf_op jit(solution)/shard_map/ppermute | solution.py:74
  198.3 14.4 %collective-permute-start.25 = (f32[256,768]{1,0:T(8,128)}, f32[256,768]{1,0:T(8,128)}, u32[]{:S(2)}, u32[]{:S(2)}) collective-permute-start(f32[256,768]{1,0:T(8,128)} %get-tuple-element.119.refs_0_), channel_id=1, source_target_pairs={{0,4},{2,6},{4,0},{6,2},{8,12},{10,14},{12,8},{14,10},{16,20},{18,... | collective-permute-start | bytes 2359304 | tf_op jit(solution)/shard_map/ppermute | solution.py:74
  198.8 14.2 %collective-permute-start.26 = (f32[256,768]{1,0:T(8,128)}, f32[256,768]{1,0:T(8,128)}, u32[]{:S(2)}, u32[]{:S(2)}) collective-permute-start(f32[256,768]{1,0:T(8,128)} %get-tuple-element.120.refs_2_), channel_id=1, source_target_pairs={{0,2},{2,0},{4,6},{6,4},{8,10},{10,8},{12,14},{14,12},{16,18},{18,... | collective-permute-start | bytes 2359304 | tf_op jit(solution)/shard_map/ppermute | solution.py:74
  218.9 29.4 %collective-permute-start.28 = (f32[256,1024]{1,0:T(8,128)}, f32[256,1024]{1,0:T(8,128)}, u32[]{:S(2)}, u32[]{:S(2)}) collective-permute-start(f32[256,1024]{1,0:T(8,128)} %get-tuple-element.124.refs_3_), channel_id=1, source_target_pairs={{0,8},{2,10},{4,12},{6,14},{8,16},{10,18},{12,20},{14,22},{16,24},... | collective-permute-start | bytes 3145736 | tf_op jit(solution)/shard_map/ppermute | solution.py:74
  219.0 20.4 %collective-permute-start.29 = (f32[256,768]{1,0:T(8,128)}, f32[256,768]{1,0:T(8,128)}, u32[]{:S(2)}, u32[]{:S(2)}) collective-permute-start(f32[256,768]{1,0:T(8,128)} %get-tuple-element.119.refs_0_), channel_id=1, source_target_pairs={{0,2},{2,0},{4,6},{6,4},{8,10},{10,8},{12,14},{14,12},{16,18},{18,... | collective-permute-start | bytes 2359304 | tf_op jit(solution)/shard_map/ppermute | solution.py:74
  219.6 20.3 %collective-permute-start.31 = (f32[256,768]{1,0:T(8,128)}, f32[256,768]{1,0:T(8,128)}, u32[]{:S(2)}, u32[]{:S(2)}) collective-permute-start(f32[256,768]{1,0:T(8,128)} %get-tuple-element.120.refs_2_), channel_id=1, source_target_pairs={{0,4},{2,6},{4,0},{6,2},{8,12},{10,14},{12,8},{14,10},{16,20},{18,... | collective-permute-start | bytes 2359304 | tf_op jit(solution)/shard_map/ppermute | solution.py:74
  220.2 27.6 %collective-permute-start.30 = (f32[256,768]{1,0:T(8,128)}, f32[256,768]{1,0:T(8,128)}, u32[]{:S(2)}, u32[]{:S(2)}) collective-permute-start(f32[256,768]{1,0:T(8,128)} %get-tuple-element.122.refs_1_), channel_id=1, source_target_pairs={{0,2},{2,0},{4,6},{6,4},{8,10},{10,8},{12,14},{14,12},{16,18},{18,... | collective-permute-start | bytes 2359304 | tf_op jit(solution)/shard_map/ppermute | solution.py:74
  221.5 26.8 %collective-permute-start.32 = (f32[256,768]{1,0:T(8,128)}, f32[256,768]{1,0:T(8,128)}, u32[]{:S(2)}, u32[]{:S(2)}) collective-permute-start(f32[256,768]{1,0:T(8,128)} %get-tuple-element.123.refs_3_), channel_id=1, source_target_pairs={{0,4},{2,6},{4,0},{6,2},{8,12},{10,14},{12,8},{14,10},{16,20},{18,... | collective-permute-start | bytes 2359304 | tf_op jit(solution)/shard_map/ppermute | solution.py:74
  259.3 25.9 %collective-permute-start.35 = (f32[256,1024]{1,0:T(8,128)}, f32[256,1024]{1,0:T(8,128)}, u32[]{:S(2)}, u32[]{:S(2)}) collective-permute-start(f32[256,1024]{1,0:T(8,128)} %get-tuple-element.133.refs_0_), channel_id=1, source_target_pairs={{0,4},{2,6},{4,0},{6,2},{8,12},{10,14},{12,8},{14,10},{16,20},{18,... | collective-permute-start | bytes 3145736 | tf_op jit(solution)/shard_map/ppermute | solution.py:74
  259.8 25.6 %collective-permute-start.36 = (f32[256,1024]{1,0:T(8,128)}, f32[256,1024]{1,0:T(8,128)}, u32[]{:S(2)}, u32[]{:S(2)}) collective-permute-start(f32[256,1024]{1,0:T(8,128)} %get-tuple-element.134.refs_0_), channel_id=1, source_target_pairs={{0,2},{2,0},{4,6},{6,4},{8,10},{10,8},{12,14},{14,12},{16,18},{18,... | collective-permute-start | bytes 3145736 | tf_op jit(solution)/shard_map/ppermute | solution.py:74
  261.1 27.1 %collective-permute-start.34 = (f32[256,1024]{1,0:T(8,128)}, f32[256,1024]{1,0:T(8,128)}, u32[]{:S(2)}, u32[]{:S(2)}) collective-permute-start(f32[256,1024]{1,0:T(8,128)} %get-tuple-element.132.refs_2_), channel_id=1, source_target_pairs={{0,8},{2,10},{4,12},{6,14},{8,16},{10,18},{12,20},{14,22},{16,24},... | collective-permute-start | bytes 3145736 | tf_op jit(solution)/shard_map/ppermute | solution.py:74
  288.2 26.3 %collective-permute-start.37 = (f32[256,1024]{1,0:T(8,128)}, f32[256,1024]{1,0:T(8,128)}, u32[]{:S(2)}, u32[]{:S(2)}) collective-permute-start(f32[256,1024]{1,0:T(8,128)} %get-tuple-element.144.refs_3_), channel_id=1, source_target_pairs={{0,8},{2,10},{4,12},{6,14},{8,16},{10,18},{12,20},{14,22},{16,24},... | collective-permute-start | bytes 3145736 | tf_op jit(solution)/shard_map/ppermute | solution.py:74
  291.2 61.3 %collective-permute-start.41 = (f32[512,1024]{1,0:T(8,128)}, f32[512,1024]{1,0:T(8,128)}, u32[]{:S(2)}, u32[]{:S(2)}) collective-permute-start(f32[512,1024]{1,0:T(8,128)} %stack.39.refs_2_), channel_id=1, source_target_pairs={{0,2},{2,0},{4,6},{6,4},{8,10},{10,8},{12,14},{14,12},{16,18},{18,... | collective-permute-start | bytes 6291464 | tf_op jit(solution)/shard_map/ppermute | solution.py:74
  295.0 69.0 %collective-permute-start.40 = (f32[512,1024]{1,0:T(8,128)}, f32[512,1024]{1,0:T(8,128)}, u32[]{:S(2)}, u32[]{:S(2)}) collective-permute-start(f32[512,1024]{1,0:T(8,128)} %stack.38.refs_2_), channel_id=1, source_target_pairs={{0,4},{2,6},{4,0},{6,2},{8,12},{10,14},{12,8},{14,10},{16,20},{18,... | collective-permute-start | bytes 6291464 | tf_op jit(solution)/shard_map/ppermute | solution.py:74
  314.5 25.3 %collective-permute-start.38 = (f32[256,1024]{1,0:T(8,128)}, f32[256,1024]{1,0:T(8,128)}, u32[]{:S(2)}, u32[]{:S(2)}) collective-permute-start(f32[256,1024]{1,0:T(8,128)} %get-tuple-element.145.refs_6_), channel_id=1, source_target_pairs={{0,8},{2,10},{4,12},{6,14},{8,16},{10,18},{12,20},{14,22},{16,24},... | collective-permute-start | bytes 3145736 | tf_op jit(solution)/shard_map/ppermute | solution.py:74
  339.8 36.2 %collective-permute-start.39 = (f32[256,1024]{1,0:T(8,128)}, f32[256,1024]{1,0:T(8,128)}, u32[]{:S(2)}, u32[]{:S(2)}) collective-permute-start(f32[256,1024]{1,0:T(8,128)} %get-tuple-element.148.refs_5_), channel_id=1, source_target_pairs={{0,8},{2,10},{4,12},{6,14},{8,16},{10,18},{12,20},{14,22},{16,24},... | collective-permute-start | bytes 3145736 | tf_op jit(solution)/shard_map/ppermute | solution.py:74
  (19 other events, 161.2 us)
where the time goes:
time: 400 us; the launch traced here: 399 us
  waiting for transfers between devices  178 us (44%)
  Pallas kernels  165 us (41%)
  starting transfers between devices  32.2 us (8%)
  other arithmetic  14.2 us (4%)
  local copies, waits for them, and re-layouts  9.61 us (2%)
    ppermute x39, waiting for transfers between devices, move(): return lax.ppermute(value, 'tok', pairs)  169 us
    pallas_call x3, Pallas kernels, expand(): pl.pallas_call(functools.partial(expand_kernel, groups, len(pieces)), gri...  38 us
    pallas_call x3, Pallas kernels, reduce(): pl.pallas_call(functools.partial(reduce_kernel, groups, len(pieces), firs...  37.7 us
    ppermute x39, starting transfers between devices, move(): return lax.ppermute(value, 'tok', pairs)  31.5 us
    pallas_call x4, Pallas kernels, mix(): pl.pallas_call(mix_kernel, grid=(units // tile,), in_specs=picked * 2 + [...  25.6 us
    pallas_call x2, Pallas kernels, project(): pl.pallas_call(functools.partial(project_kernel, rows, places), grid=(wid...  21.1 us
    pallas_call x4, Pallas kernels, stack(): pl.pallas_call(functools.partial(stack_kernel, len(values), parts), grid=...  12.8 us
    pallas_call x1, Pallas kernels, norm_two(): pl.pallas_call(functools.partial(norm_two_kernel, grid, channels // grid....  9.81 us
  transfers between devices with their start and end apart: 43, of which 27 were waited for; matrix products, arithmetic and copies ran while one was open for 5% of the time, Pallas kernels for 33%

commit v1 on v0

--- a/solution.py
+++ b/solution.py
@@ -139,22 +139,39 @@
     )(place, gain, *sources)
 
 
-def mix_kernel(high_one, high_two, low_one, low_two, weight_ref, out_ref):
+def mix_kernel(steps, high_one, high_two, low_one, low_two, weight_ref, out_a, out_b):
     normed = join([high_one[...], high_two[...]]), join([low_one[...], low_two[...]])
-    out_ref[...] = three_pass(normed, halves(weight_ref[...].T))
-
-
-def mix(high, low, weight, part, quarters):
+    product = three_pass(normed, halves(weight_ref[...].T))
+    part = pl.program_id(0) // steps
+
+    @pl.when(part == 0)
+    def _():
+        out_a[...] = product
+
+    @pl.when(part == 1)
+    def _():
+        out_b[...] = product
+
+
+def mix(high, low, weight, kept):
     channels, height = high.shape
     units = weight.shape[0] // 2
     tile = tile_of(units)
-    picked = [pl.BlockSpec((channels // 4, height), lambda n, q=q: (q, 0)) for q in quarters]
-    return pl.pallas_call(
-        mix_kernel,
-        grid=(units // tile,),
-        in_specs=picked * 2 + [pl.BlockSpec((tile, height), lambda n: (n + part * (units // tile), 0))],
-        out_specs=pl.BlockSpec((channels // 2, tile), lambda n: (0, n)),
-        out_shape=jax.ShapeDtypeStruct((channels // 2, units), jnp.float32),
+    steps = units // tile
+    if kept:
+        quarters = lambda n: 0, lambda n: 2 - n // steps
+    else:
+        quarters = lambda n: 1 + n // steps, lambda n: 3
+    picked = [pl.BlockSpec((channels // 4, height), lambda n, q=q: (q(n), 0)) for q in quarters]
+    return pl.pallas_call(
+        functools.partial(mix_kernel, steps),
+        grid=(2 * steps,),
+        in_specs=picked * 2 + [pl.BlockSpec((tile, height), lambda n: (n, 0))],
+        out_specs=[
+            pl.BlockSpec((channels // 2, tile), lambda n: (0, jnp.minimum(n, steps - 1))),
+            pl.BlockSpec((channels // 2, tile), lambda n: (0, jnp.maximum(n - steps, 0))),
+        ],
+        out_shape=[jax.ShapeDtypeStruct((channels // 2, units), jnp.float32)] * 2,
         compiler_params=pltpu.CompilerParams(vmem_limit_bytes=grant),
         cost_estimate=light,
         name="mix",
@@ -185,6 +202,22 @@
     for kept, sent, (top, bottom) in ((kept_a, sent_a, outs[:2]), (kept_b, sent_b, outs[2:])):
         total = kept[...] + sent[...]
         top[...], bottom[...] = total[: total.shape[0] // 2], total[total.shape[0] // 2 :]
+
+
+def halve(values):
+    rows, units = values[0].shape
+    tile = tile_of(units)
+    column = lambda n: (0, n)
+    return pl.pallas_call(
+        halve_kernel,
+        grid=(units // tile,),
+        in_specs=[pl.BlockSpec((rows, tile), column)] * 4,
+        out_specs=[pl.BlockSpec((rows // 2, tile), column)] * 4,
+        out_shape=[jax.ShapeDtypeStruct((rows // 2, units), jnp.float32)] * 4,
+        compiler_params=pltpu.CompilerParams(vmem_limit_bytes=grant),
+        cost_estimate=light,
+        name="halve",
+    )(*values)
 
 
 def merge_kernel(kept_a, sent_a, kept_b, sent_b, *outs):
@@ -195,21 +228,24 @@
         out_ref[:, middle:] = kept_b[block, :] + sent_b[block, :]
 
 
-def sums(kernel, values, count, shape):
-    return pl.pallas_call(
-        kernel,
+def merge(values, deep):
+    rows, units = values[0].shape
+    shape = rows // deep, 2 * units
+    return pl.pallas_call(
+        merge_kernel,
         grid=(1,),
         in_specs=[pl.BlockSpec(value.shape, lambda n: (0, 0)) for value in values],
-        out_specs=[pl.BlockSpec(shape, lambda n: (0, 0))] * count,
-        out_shape=[jax.ShapeDtypeStruct(shape, jnp.float32)] * count,
-        compiler_params=pltpu.CompilerParams(vmem_limit_bytes=grant),
-        cost_estimate=light,
-        name="sums",
+        out_specs=[pl.BlockSpec(shape, lambda n: (0, 0))] * deep,
+        out_shape=[jax.ShapeDtypeStruct(shape, jnp.float32)] * deep,
+        compiler_params=pltpu.CompilerParams(vmem_limit_bytes=grant),
+        cost_estimate=light,
+        name="merge",
     )(*values)
 
 
 def project_kernel(rows, places, weight_ref, *refs):
-    pieces, earlier, (out_ref, active_high, active_low) = refs[:4], refs[4:-3], refs[-3:]
+    pieces, (out_ref, active_high, active_low) = refs[:-3], refs[-3:]
+    count = len(pieces) // 2
     middle = pieces[0].shape[1]
 
     @pl.when(pl.program_id(0) == 0)
@@ -220,57 +256,58 @@
     high, low = halves(weight_ref[...].T)
     sums = []
     for part in range(2):
-        taken, units = slice(part * 2 * rows, (part + 1) * 2 * rows), slice(part * middle, (part + 1) * middle)
+        taken = slice(part * count * rows, (part + 1) * count * rows)
+        units = slice(part * middle, (part + 1) * middle)
         product = three_pass((active_high[taken, :], active_low[taken, :]), (high[units, :], low[units, :]))
-        sums += [product[:rows], product[rows:]]
+        sums += [product[n * rows : (n + 1) * rows] for n in range(count)]
     for group in range(out_ref.shape[0] // rows):
         target = slice(group * rows, (group + 1) * rows)
         terms = [value for value, place in zip(sums, places) if place == group]
-        terms += [ref[target, :] for ref in earlier if group < ref.shape[0] // rows]
         out_ref[target, :] = functools.reduce(lambda a, b: a + b, terms)
 
 
-def project(weight, pieces, places, groups, earlier=()):
+def project(weight, pieces, places):
     width, units = weight.shape
     rows = pieces[0].shape[0]
+    groups = 1 + max(places)
     tile = tile_of(width)
     return pl.pallas_call(
         functools.partial(project_kernel, rows, places),
         grid=(width // tile,),
         in_specs=[pl.BlockSpec((tile, units), lambda n: (n, 0))]
-        + [pl.BlockSpec(piece.shape, lambda n: (0, 0)) for piece in pieces]
-        + [pl.BlockSpec((value.shape[0], tile), lambda n: (0, n)) for value in earlier],
+        + [pl.BlockSpec(piece.shape, lambda n: (0, 0)) for piece in pieces],
         out_specs=pl.BlockSpec((groups * rows, tile), lambda n: (0, n)),
         out_shape=jax.ShapeDtypeStruct((groups * rows, width), jnp.float32),
-        scratch_shapes=[pltpu.VMEM((4 * rows, units // 2), jnp.bfloat16)] * 2,
+        scratch_shapes=[pltpu.VMEM((len(pieces) * rows, units // 2), jnp.bfloat16)] * 2,
         compiler_params=pltpu.CompilerParams(vmem_limit_bytes=grant),
         cost_estimate=light,
         name="project",
-    )(weight, *pieces, *earlier)
-
-
-def norm_two_kernel(grid, rows, per_core, place_ref, gain_ref, fields_ref, *refs):
+    )(weight, *pieces)
+
+
+def norm_two_kernel(grid, rows, per_core, parts, place_ref, gain_ref, fields_ref, *refs):
     terms, (mixed_ref, high_ref, low_ref) = refs[:-3], refs[-3:]
     starts = block_starts(grid, place_ref, rows, per_core)
     gain = jnp.concatenate([gain_ref[pl.ds(start, rows), :] for start in starts], axis=0)
-    total = terms[0][...]
-    for ref in terms[1:]:
-        total = total + ref[...]
-    mixed = fields_ref[...] + total
+    total = [ref[...] for ref in terms[:parts]]
+    for n in range(parts, len(terms)):
+        total[n % parts] = total[n % parts] + terms[n][...]
+    mixed = fields_ref[...] + join(total)
     mixed_ref[...] = mixed
     high_ref[...], low_ref[...] = halves(column_norm(mixed, gain))
 
 
-def norm_two(grid, place, gain, fields, terms, per_core):
+def norm_two(grid, place, gain, fields, terms, parts, per_core):
     channels, width = fields.shape
     tile = tile_of(width)
     whole = pl.BlockSpec((channels, tile), lambda n, place: (0, n))
     return pl.pallas_call(
-        functools.partial(norm_two_kernel, grid, channels // grid.tok, per_core),
+        functools.partial(norm_two_kernel, grid, channels // grid.tok, per_core, parts),
         grid_spec=pltpu.PrefetchScalarGridSpec(
             num_scalar_prefetch=1,
             grid=(width // tile,),
-            in_specs=[pl.BlockSpec((channels, 1), lambda n, place: (0, 0))] + [whole] * (1 + len(terms)),
+            in_specs=[pl.BlockSpec((channels, 1), lambda n, place: (0, 0)), whole]
+            + [pl.BlockSpec((term.shape[0], tile), lambda n, place: (0, n)) for term in terms],
             out_specs=[whole] * 3,
         ),
         out_shape=[
@@ -444,8 +481,6 @@
     corner = {(b, a): [key for key in whole if key[1:] == (b, a)] for b in range(2) for a in range(2)}
     y_last = grid.segments([corner[0, 0], corner[0, 1], corner[1, 0], corner[1, 1]], rows)
     x_last = grid.segments([corner[0, 0], corner[1, 0], corner[0, 1], corner[1, 1]], rows)
-    y_last_pair = grid.segments([corner[0, 0] + corner[0, 1], corner[1, 0] + corner[1, 1]], rows)
-    x_last_pair = grid.segments([corner[0, 0] + corner[1, 0], corner[0, 1] + corner[1, 1]], rows)
     z_after_xy = grid.segments(lone("z", "yx"), rows)
     z_after_yx = grid.segments(lone("z", "xy"), rows)
 
@@ -468,25 +503,23 @@
 
     middle = tok_in_weight.shape[0] // 2
     quarter = deep * rows
-    sent_a = mix(high, low, tok_in_weight, 0, (1, 3))
-    sent_b = mix(high, low, tok_in_weight, 1, (2, 3))
-    sent_a, sent_b, ring[0] = fence(sent_a, sent_b, ring[0])
+    sent_a, sent_b = mix(high, low, tok_in_weight, False)
+    sent_a, sent_b, ring[0], in_step, out_step = fence(sent_a, sent_b, ring[0], in_step, out_step)
     sent_a, sent_b = move(sent_a, dx=1), move(sent_b, dy=1)
     ring.append(move(ring[0], dz=1))
-    kept_a = mix(high, low, tok_in_weight, 0, (0, 2))
-    kept_b = mix(high, low, tok_in_weight, 1, (0, 1))
+    kept_a, kept_b = mix(high, low, tok_in_weight, True)
     biases = [ch_in_bias[a:b, None] for a, b in spans]
-    sent_a, sent_b, kept_a, kept_b, in_step, out_step, ring[1], *biases = fence(
-        sent_a, sent_b, kept_a, kept_b, in_step, out_step, ring[1], *biases
+    in_last, out_last = join([in_last, in_step]), join([out_last, out_step])
+    sent_a, sent_b, kept_a, kept_b, in_last, out_last, ring[1], *biases = fence(
+        sent_a, sent_b, kept_a, kept_b, in_last, out_last, ring[1], *biases
     )
-    kept_a, sent_a, kept_b, sent_b = sums(halve_kernel, [kept_a, sent_a, kept_b, sent_b], 4, (quarter, middle))
+    kept_a, sent_a, kept_b, sent_b = halve([kept_a, sent_a, kept_b, sent_b])
     sent_a, sent_b = move(sent_a, dy=1), move(sent_b, dx=1)
-    in_last, out_last = join([in_last, in_step]), join([out_last, out_step])
     for _ in range(2, deep - 1):
         ring.append(move(ring[-1], dz=1))
-    sent_a, sent_b, in_last, out_last, ring[-1] = fence(sent_a, sent_b, in_last, out_last, ring[-1])
-
-    partial = sums(merge_kernel, [kept_a, sent_a, kept_b, sent_b], deep, (rows, 2 * middle))
+    sent_a, sent_b, ring[-1] = fence(sent_a, sent_b, ring[-1])
+
+    partial = merge([kept_a, sent_a, kept_b, sent_b], deep)
     total = partial[deep - 1]
     for step in range(2, deep + 1):
         total = move(total, dz=1) + partial[deep - step]
@@ -505,39 +538,41 @@
     first = [first[0] + first_step[:2], first[1] + first_step[2:]]
 
     active_a, active_b = stack(grid.line(activated, ring), [(0, rows, 0, middle), (0, rows, middle, 2 * middle)])
-    step_a, step_b = move(active_a, dy=1), move(active_b, dx=1)
+    arrived = [move(active_a, dy=1), move(active_a, dx=1), move(active_b, dx=1), move(active_b, dy=1)]
     in_ring = [move(in_last, dz=1)]
-    step_a, step_b, in_ring[0] = fence(step_a, step_b, in_ring[0])
-    arrived = [move(active_a, dx=1), move(step_a, dx=1), move(active_b, dy=1), move(step_b, dy=1)]
+    in_ring[0], *arrived = fence(in_ring[0], *arrived)
+    last_a, last_b = move(arrived[0], dx=1), move(arrived[2], dy=1)
     in_ring.append(move(in_ring[0], dz=1))
-    terms = project(tok_out_weight, [active_a, step_a, active_b, step_b], (0, 2, 0, 1), 3)
-    terms, in_ring[1], *arrived = fence(terms, in_ring[1], *arrived)
+    most = project(tok_out_weight, [active_a, *arrived[:2], active_b, *arrived[2:]], (0, 2, 1, 0, 1, 2))
+    last_a, last_b, in_ring[1], most = fence(last_a, last_b, in_ring[1], most)
 
     for _ in range(2, deep - 1):
         in_ring.append(move(in_ring[-1], dz=1))
     second_step = [move(second[0][0], dy=1), move(second[1][0], dx=1)]
-    terms = project(tok_out_weight, arrived, (1, 3, 2, 3), 4, [terms])
-    terms = [terms] + [grid.to_core(terms, step) for step in range(1, ch)]
-    mixed, high, low = norm_two(grid, place, gains[:, 1:], full, terms, per_core)
-
-    high, out_last, in_ring[-1], *second_step = fence(high, out_last, in_ring[-1], *second_step)
-    second = [stack([line[0], step], [(0, quarter, 0, step.shape[1])])[0] for line, step in zip(second, second_step)]
-    second_step = [move(second[0], dx=1), move(second[1], dy=1)]
+    most = [most] + [grid.to_core(most, step) for step in range(1, ch)]
+    least = project(tok_out_weight, [last_a, last_b], (0, 0))
+    least = [least] + [grid.to_core(least, step) for step in range(1, ch)]
+    terms = [part for pair in zip(most, least) for part in pair]
+    mixed, high, low = norm_two(grid, place, gains[:, 1:], full, terms, 2, per_core)
+
+    hidden = [expand(high, low, biases[0], first[0], y_last)]
+    hidden_high, out_last, in_ring[-1], *second_step = fence(hidden[0][0], out_last, in_ring[-1], *second_step)
+    hidden[0] = hidden_high, hidden[0][1]
+    second = [line + [step] for line, step in zip(second, second_step)]
+    second_step = [move(value, dx=1) for value in second[0]] + [move(value, dy=1) for value in second[1]]
     out_ring = [move(out_last, dz=1)]
-    hidden = [
-        expand(high, low, biases[0], first[0], y_last),
+    hidden += [
         expand(high, low, biases[1], first[1], x_last),
+        expand(high, low, biases[2], grid.line(in_last, in_ring), z_after_xy),
     ]
-    hidden_high, out_ring[0] = fence(hidden[1][0], out_ring[0])
-    hidden[1] = hidden_high, hidden[1][1]
-    out_ring.append(move(out_ring[0], dz=1))
-    hidden.append(expand(high, low, biases[2], grid.line(in_last, in_ring), z_after_xy))
-    hidden_high, out_ring[1] = fence(hidden[2][0], out_ring[1])
-    hidden[2] = hidden_high, hidden[2][1]
+    fenced = fence(hidden[1][0], hidden[2][0], out_ring[0])
+    hidden[1:] = [(fenced[0], hidden[1][1]), (fenced[1], hidden[2][1])]
+    out_ring = [fenced[2], move(fenced[2], dz=1)]
+    (result,) = reduce(*hidden[0], second[0] + second_step[:2], x_last, None)
+    result, out_ring[1], *second_step[2:] = fence(result, out_ring[1], *second_step[2:])
     for _ in range(2, deep - 1):
         out_ring.append(move(out_ring[-1], dz=1))
-    (result,) = reduce(*hidden[0], [second[0], second_step[0]], x_last_pair, None)
-    (result,) = reduce(*hidden[1], [second[1], second_step[1]], y_last_pair, result)
+    (result,) = reduce(*hidden[1], second[1] + second_step[2:], y_last, result)
     spread = grid, rows, per_core
     parts = reduce(*hidden[2], grid.line(out_last, out_ring), z_after_yx, result, spread, place, mixed)
     return finish([parts[0]] + [grid.to_core(part, step) for step, part in enumerate(parts) if step])

time: 400 us -> 384 us (0.960)
  waiting for transfers between devices: 178 us -> 159 us
  starting transfers between devices: 32.2 us -> 42 us
  Pallas kernels: 165 us -> 156 us
    ppermute x39 -> x41, waiting for transfers between devices: 169 us -> 155 us  [move(): return lax.ppermute(value, 'tok', pairs)]
    ppermute x39 -> x41, starting transfers between devices: 31.5 us -> 40.8 us  [move(): return lax.ppermute(value, 'tok', pairs)]
    pallas_call x4 -> x2, Pallas kernels: 12.8 us -> 6.83 us  [stack(): pl.pallas_call(functools.partial(stack_kernel, len(values), parts), grid=...]
    ppermute x4 -> x5, waiting for transfers between devices: 9.38 us -> 4.5 us  [to_core(): lax.ppermute(value, 'ch', [(core, (core + step) % self.ch) for core in ra...]
    pallas_call x6 -> x4, Pallas kernels: 33.2 us -> 29.9 us  [the longest x2 21.7 us: mix(): pl.pallas_call(functools.partial(mix_kernel, steps), grid=(2 * steps,), i...]
  transfers between devices with their start and end apart: 43 -> 46, of which waited for: 27 -> 23; matrix products, arithmetic and copies ran while one was open for 5% -> 6% of each run, Pallas kernels for 33% -> 35%
where the time goes in v1:
time: 384 us; the launch traced here: 383 us
  waiting for transfers between devices  159 us (41%)
  Pallas kernels  156 us (41%)
  starting transfers between devices  42 us (11%)
  other arithmetic  15 us (4%)
  local copies, waits for them, and re-layouts  10.5 us (3%)
    ppermute x41, waiting for transfers between devices, move(): return lax.ppermute(value, 'tok', pairs)  155 us
    ppermute x41, starting transfers between devices, move(): return lax.ppermute(value, 'tok', pairs)  40.8 us
    pallas_call x3, Pallas kernels, expand(): pl.pallas_call(functools.partial(expand_kernel, groups, len(pieces)), gri...  38 us
    pallas_call x3, Pallas kernels, reduce(): pl.pallas_call(functools.partial(reduce_kernel, groups, len(pieces), firs...  37.6 us
    pallas_call x2, Pallas kernels, mix(): pl.pallas_call(functools.partial(mix_kernel, steps), grid=(2 * steps,), i...  21.7 us
    pallas_call x2, Pallas kernels, project(): pl.pallas_call(functools.partial(project_kernel, rows, places), grid=(wid...  21 us
    pallas_call x1, Pallas kernels, norm_two(): pl.pallas_call(functools.partial(norm_two_kernel, grid, channels // grid....  9.92 us
    concatenate x5, other arithmetic, join(): return jnp.concatenate(list(values), axis=axis)  8.1 us
  transfers between devices with their start and end apart: 46, of which 23 were waited for; matrix products, arithmetic and copies ran while one was open for 6% of the time, Pallas kernels for 35%

profile of v1, /device:TPU:0, one launch (start us, length us, event | category | flops | bytes accessed | tf_op | source)
XLA Modules:
  0.0 382.7 jit_solution(1165321572977126756)
XLA Ops:
  14.9 8.0 %norm_one.1 = (f32[1024,1024]{1,0:T(8,128)}, bf16[1024,1024]{1,0:T(8,128)(2,1)}, bf16[1024,1024]{1,0:T(8,128)(2,1)}) custom-call(s32[4]{0:T(128)} %pad_add_fusion.place_ref.refs_0_, f32[1024,1]{1,0:T(8,128)} %get-tuple-element.175.gain_ref, f32[1024,512]{1,0:T(8,128)} %refs_0_.1, f32[1024,512]{1,0:T(8,128)} %collective-permute-done.1.refs_1_), custom_call_target="tpu_custom_call" | custom-call | tf_op jit(solution)/shard_map/norm_one/pallas_call | solution.py:123
  27.7 10.8 %mix.2 = (f32[512,768]{1,0:T(8,128)}, f32[512,768]{1,0:T(8,128)}) custom-call(bf16[1024,1024]{1,0:T(8,128)(2,1)} %get-tuple-element.92.high_one.high_two, bf16[1024,1024]{1,0:T(8,128)(2,1)} %get-tuple-element.92.high_one.high_two, bf16[1024,1024]{1,0:T(8,128)(2,1)} %get-tuple-element.93.low_one.low_two, ...), custom_call_target="tpu_custom_call" | custom-call | tf_op jit(solution)/shard_map/mix/pallas_call | solution.py:166
  47.1 10.8 %mix.3 = (f32[512,768]{1,0:T(8,128)}, f32[512,768]{1,0:T(8,128)}) custom-call(bf16[1024,1024]{1,0:T(8,128)(2,1)} %get-tuple-element.92.high_one.high_two, bf16[1024,1024]{1,0:T(8,128)(2,1)} %get-tuple-element.92.high_one.high_two, bf16[1024,1024]{1,0:T(8,128)(2,1)} %get-tuple-element.93.low_one.low_two, ...), custom_call_target="tpu_custom_call" | custom-call | tf_op jit(solution)/shard_map/mix/pallas_call | solution.py:166
  57.9 3.2 pad_maximum_fusion.1
  61.1 5.9 %collective-permute-done.9.refs_6_ = f32[128,2048]{1,0:T(8,128)} collective-permute-done((f32[128,2048]{1,0:T(8,128)}, f32[128,2048]{1,0:T(8,128)}, u32[]{:S(2)}, u32[]{:S(2)}) %collective-permute-start.9) | collective-permute-done | bytes 1048608 | tf_op jit(solution)/shard_map/ppermute | solution.py:74
  67.0 7.9 %collective-permute-done.7.refs_0_ = f32[512,768]{1,0:T(8,128)} collective-permute-done((f32[512,768]{1,0:T(8,128)}, f32[512,768]{1,0:T(8,128)}, u32[]{:S(2)}, u32[]{:S(2)}) %collective-permute-start.7) | collective-permute-done | bytes 1572896 | tf_op jit(solution)/shard_map/ppermute | solution.py:74
  76.8 5.2 %halve.1 = (f32[256,768]{1,0:T(8,128)}, f32[256,768]{1,0:T(8,128)}, f32[256,768]{1,0:T(8,128)}, f32[256,768]{1,0:T(8,128)}) custom-call(f32[512,768]{1,0:T(8,128)} %get-tuple-element.105.kept_a, f32[512,768]{1,0:T(8,128)} %get-tuple-element.106.sent_a, f32[512,768]{1,0:T(8,128)} %get-tuple-element.107.kept_b, f32[512,768]{1,0:T(8,128)} %get-tuple-element.108.sent_b), custom_call_target="tpu_custom_call" | custom-call | tf_op jit(solution)/shard_map/halve/pallas_call | solution.py:211
  84.9 13.3 %collective-permute-done.10.refs_0_ = f32[256,768]{1,0:T(8,128)} collective-permute-done((f32[256,768]{1,0:T(8,128)}, f32[256,768]{1,0:T(8,128)}, u32[]{:S(2)}, u32[]{:S(2)}) %collective-permute-start.10) | collective-permute-done | bytes 786464 | tf_op jit(solution)/shard_map/ppermute | solution.py:74
  99.5 3.1 merge.1
  104.1 8.2 %collective-permute-done.13 = f32[64,1536]{1,0:T(8,128)S(1)} collective-permute-done((f32[64,1536]{1,0:T(8,128)}, f32[64,1536]{1,0:T(8,128)S(1)}, u32[]{:S(2)}, u32[]{:S(2)}) %collective-permute-start.13) | collective-permute-done | bytes 393248 | tf_op jit(solution)/shard_map/ppermute | solution.py:74
  114.3 4.2 %stack.34 = (f32[256,1024]{1,0:T(8,128)}, f32[256,1024]{1,0:T(8,128)}, f32[256,1024]{1,0:T(8,128)}, f32[256,1024]{1,0:T(8,128)}) custom-call(f32[128,2048]{1,0:T(8,128)} %pad_maximum_fusion.refs_0_, f32[128,2048]{1,0:T(8,128)} %get-tuple-element.120.refs_1_, f32[128,2048]{1,0:T(8,128)} %get-tuple-element.112.refs_2_, f32[128,2048]{1,0:T(8,128)} %get-tuple-element.104.refs_3_), custom_call_target="tpu_custom_call" | custom-call | tf_op jit(solution)/shard_map/stack/pallas_call | solution.py:189
  121.1 3.9 %collective-permute-done.14 = f32[64,1536]{1,0:T(8,128)} collective-permute-done((f32[64,1536]{1,0:T(8,128)}, f32[64,1536]{1,0:T(8,128)}, u32[]{:S(2)}, u32[]{:S(2)}) %collective-permute-start.14) | collective-permute-done | bytes 393248 | tf_op jit(solution)/shard_map/ppermute | solution.py:74
  126.1 9.6 %collective-permute-done.15 = f32[64,1536]{1,0:T(8,128)S(1)} collective-permute-done((f32[64,1536]{1,0:T(8,128)S(1)}, f32[64,1536]{1,0:T(8,128)S(1)}, u32[]{:S(2)}, u32[]{:S(2)}) %collective-permute-start.15) | collective-permute-done | bytes 393248 | tf_op jit(solution)/shard_map/ppermute | solution.py:74
  139.2 3.8 %collective-permute-done.17.refs_4_ = f32[256,1024]{1,0:T(8,128)} collective-permute-done((f32[256,1024]{1,0:T(8,128)}, f32[256,1024]{1,0:T(8,128)}, u32[]{:S(2)}, u32[]{:S(2)}) %collective-permute-start.17) | collective-permute-done | bytes 1048608 | tf_op jit(solution)/shard_map/ppermute | solution.py:74
  147.1 7.6 %collective-permute-done.18.refs_3_ = f32[64,1536]{1,0:T(8,128)S(1)} collective-permute-done((f32[64,1536]{1,0:T(8,128)}, f32[64,1536]{1,0:T(8,128)S(1)}, u32[]{:S(2)}, u32[]{:S(2)}) %collective-permute-start.18) | collective-permute-done | bytes 393248 | tf_op jit(solution)/shard_map/ppermute | solution.py:74
  155.5 10.5 %collective-permute-done.19.refs_2_ = f32[64,1536]{1,0:T(8,128)S(1)} collective-permute-done((f32[64,1536]{1,0:T(8,128)S(1)}, f32[64,1536]{1,0:T(8,128)S(1)}, u32[]{:S(2)}, u32[]{:S(2)}) %collective-permute-start.19) | collective-permute-done | bytes 393248 | tf_op jit(solution)/shard_map/ppermute | solution.py:74
  169.5 16.7 %collective-permute-done.22.refs_3_ = f32[256,1024]{1,0:T(8,128)} collective-permute-done((f32[256,1024]{1,0:T(8,128)}, f32[256,1024]{1,0:T(8,128)}, u32[]{:S(2)}, u32[]{:S(2)}) %collective-permute-start.22) | collective-permute-done | bytes 1048608 | tf_op jit(solution)/shard_map/ppermute | solution.py:74
  192.9 16.7 %collective-permute-done.26.refs_1_ = f32[256,768]{1,0:T(8,128)} collective-permute-done((f32[256,768]{1,0:T(8,128)}, f32[256,768]{1,0:T(8,128)}, u32[]{:S(2)}, u32[]{:S(2)}) %collective-permute-start.26) | collective-permute-done | bytes 786464 | tf_op jit(solution)/shard_map/ppermute | solution.py:74
  209.6 12.9 %collective-permute-done.28.refs_3_ = f32[256,768]{1,0:T(8,128)} collective-permute-done((f32[256,768]{1,0:T(8,128)}, f32[256,768]{1,0:T(8,128)}, u32[]{:S(2)}, u32[]{:S(2)}) %collective-permute-start.28) | collective-permute-done | bytes 786464 | tf_op jit(solution)/shard_map/ppermute | solution.py:74
  224.9 13.2 %project.2.refs_3_ = f32[768,1024]{1,0:T(8,128)} custom-call(f32[1024,1536]{1,0:T(8,128)} %weight_ref.7, f32[256,768]{1,0:T(8,128)} %get-tuple-element.131.refs_0_, f32[256,768]{1,0:T(8,128)} %get-tuple-element.133.refs_1_, f32[256,768]{1,0:T(8,128)} %get-tuple-element.136.refs_2_, f32[256,768]{1,0:T(8,128)} %get-tuple-element.132.refs_3_, ...), custom_call_target="tpu_custom_call" | custom-call | tf_op jit(solution)/shard_map/project/pallas_call | solution.py:274
  239.9 7.8 %project.3.refs_1_ = f32[256,1024]{1,0:T(8,128)} custom-call(f32[1024,1536]{1,0:T(8,128)} %weight_ref.7, f32[256,768]{1,0:T(8,128)} %get-tuple-element.139.refs_0_, f32[256,768]{1,0:T(8,128)} %get-tuple-element.140.refs_1_), custom_call_target="tpu_custom_call" | custom-call | tf_op jit(solution)/shard_map/project/pallas_call | solution.py:274
  252.6 9.9 %norm_two.1 = (f32[1024,1024]{1,0:T(8,128)}, bf16[1024,1024]{1,0:T(8,128)(2,1)}, bf16[1024,1024]{1,0:T(8,128)(2,1)}) custom-call(s32[4]{0:T(128)} %pad_add_fusion.place_ref.refs_0_, f32[1024,1]{1,0:T(8,128)} %get-tuple-element.176.gain_ref, f32[1024,1024]{1,0:T(8,128)} %get-tuple-element.90.fields_ref, f32[768,1024]{1,0:T(8,128)} %get-tuple-element.138.refs_0_, ...), custom_call_target="tpu_custom_call" | custom-call | tf_op jit(solution)/shard_map/norm_two/pallas_call | solution.py:304
  262.5 12.7 %expand.4 = (bf16[1024,1024]{1,0:T(8,128)(2,1)}, bf16[1024,1024]{1,0:T(8,128)(2,1)}) custom-call(bf16[1024,1024]{1,0:T(8,128)(2,1)} %get-tuple-element.141.high_ref, bf16[1024,1024]{1,0:T(8,128)(2,1)} %get-tuple-element.142.low_ref, f32[1024,1]{1,0:T(8,128)} %get-tuple-element.148.bias_ref, f32[256,1024]{1,0:T(8,128)} %get-tuple-element.125.refs_0_, ...), custom_call_target="tpu_custom_call" | custom-call | tf_op jit(solution)/shard_map/expand/pallas_call | solution.py:344
  281.5 12.6 %expand.5 = (bf16[1024,1024]{1,0:T(8,128)(2,1)}, bf16[1024,1024]{1,0:T(8,128)(2,1)}) custom-call(bf16[1024,1024]{1,0:T(8,128)(2,1)} %get-tuple-element.141.high_ref, bf16[1024,1024]{1,0:T(8,128)(2,1)} %get-tuple-element.142.low_ref, f32[1024,1]{1,0:T(8,128)} %get-tuple-element.147.bias_ref, f32[256,1024]{1,0:T(8,128)} %get-tuple-element.129.refs_0_, ...), custom_call_target="tpu_custom_call" | custom-call | tf_op jit(solution)/shard_map/expand/pallas_call | solution.py:344
  294.1 12.7 %expand.3 = (bf16[1024,1024]{1,0:T(8,128)(2,1)}, bf16[1024,1024]{1,0:T(8,128)(2,1)}) custom-call(bf16[1024,1024]{1,0:T(8,128)(2,1)} %get-tuple-element.141.high_ref, bf16[1024,1024]{1,0:T(8,128)(2,1)} %get-tuple-element.142.low_ref, f32[1024,1]{1,0:T(8,128)} %get-tuple-element.143.bias_ref, f32[256,1024]{1,0:T(8,128)} %get-tuple-element.127.refs_0_, ...), custom_call_target="tpu_custom_call" | custom-call | tf_op jit(solution)/shard_map/expand/pallas_call | solution.py:344
  308.0 15.6 %collective-permute-done.40.refs_5_ = f32[256,1024]{1,0:T(8,128)} collective-permute-done((f32[256,1024]{1,0:T(8,128)}, f32[256,1024]{1,0:T(8,128)}, u32[]{:S(2)}, u32[]{:S(2)}) %collective-permute-start.40) | collective-permute-done | bytes 1048608 | tf_op jit(solution)/shard_map/ppermute | solution.py:74
  323.5 11.4 %reduce.3.refs_0_ = f32[1024,1024]{1,0:T(8,128)} custom-call(bf16[1024,1024]{1,0:T(8,128)(2,1)} %get-tuple-element.161.refs_0_, bf16[1024,1024]{1,0:T(8,128)(2,1)} %get-tuple-element.162.refs_1_, f32[256,1024]{1,0:T(8,128)} %get-tuple-element.154.refs_2_, f32[256,1024]{1,0:T(8,128)} %get-tuple-element.163.refs_3_, ...), custom_call_target="tpu_custom_call" | custom-call | tf_op jit(solution)/shard_map/reduce/pallas_call | solution.py:405
  335.9 12.0 %reduce.4.refs_7_ = f32[1024,1024]{1,0:T(8,128)} custom-call(bf16[1024,1024]{1,0:T(8,128)(2,1)} %get-tuple-element.167.refs_0_, bf16[1024,1024]{1,0:T(8,128)(2,1)} %get-tuple-element.168.refs_1_, f32[256,1024]{1,0:T(8,128)} %get-tuple-element.155.refs_2_, f32[256,1024]{1,0:T(8,128)} %get-tuple-element.165.refs_3_, f32[256,1024]{1,0:T(8,128)} %get-tuple-element.169.refs_4_, ...), custom_call_target="tpu_custom_call" | custom-call | tf_op jit(solution)/shard_map/reduce/pallas_call | solution.py:405
  347.9 11.6 %collective-permute-done.44.refs_4_ = f32[256,1024]{1,0:T(8,128)} collective-permute-done((f32[256,1024]{1,0:T(8,128)}, f32[256,1024]{1,0:T(8,128)}, u32[]{:S(2)}, u32[]{:S(2)}) %collective-permute-start.44) | collective-permute-done | bytes 1048608 | tf_op jit(solution)/shard_map/ppermute | solution.py:74
  359.5 14.2 %reduce.5 = (f32[512,1024]{1,0:T(8,128)}, f32[512,1024]{1,0:T(8,128)}) custom-call(s32[4]{0:T(128)} %pad_add_fusion.place_ref.refs_0_, bf16[1024,1024]{1,0:T(8,128)(2,1)} %get-tuple-element.159.refs_1_, bf16[1024,1024]{1,0:T(8,128)(2,1)} %get-tuple-element.160.refs_2_, f32[256,1024]{1,0:T(8,128)} %get-tuple-element.158.refs_3_, ...), custom_call_target="tpu_custom_call" | custom-call | tf_op jit(solution)/shard_map/reduce/pallas_call | solution.py:405
  373.7 4.5 %collective-permute-done.45.refs_1_ = f32[512,1024]{1,0:T(8,128)} collective-permute-done((f32[512,1024]{1,0:T(8,128)}, f32[512,1024]{1,0:T(8,128)}, u32[]{:S(2)}, u32[]{:S(2)}) %collective-permute-start.45) | collective-permute-done | bytes 2097184 | tf_op jit(solution)/shard_map/ppermute | solution.py:77
  378.2 4.5 %finish.1 = f32[1024,512]{1,0:T(8,128)} custom-call(f32[512,1024]{1,0:T(8,128)} %get-tuple-element.173.refs_0_, f32[512,1024]{1,0:T(8,128)} %collective-permute-done.45.refs_1_), custom_call_target="tpu_custom_call" | custom-call | tf_op jit(solution)/shard_map/finish/pallas_call | solution.py:433
  (121 shorter events, 77.7 us)
Async XLA Ops:
  3.0 19.9 %collective-permute-start.3 = (f32[64,1024]{1,0:T(8,128)}, f32[64,1024]{1,0:T(8,128)}, u32[]{:S(2)}, u32[]{:S(2)}) collective-permute-start(f32[64,1024]{1,0:T(8,128)} %slice.38), channel_id=1, source_target_pairs={{0,4},{2,6},{4,0},{6,2},{8,12},{10,14},{12,8},{14,10},{16,20},{18,... | collective-permute-start | bytes 786440 | tf_op jit(solution)/shard_map/ppermute | solution.py:74
  7.6 15.3 %collective-permute-start.2 = (f32[64,1024]{1,0:T(8,128)}, f32[64,1024]{1,0:T(8,128)}, u32[]{:S(2)}, u32[]{:S(2)}) collective-permute-start(f32[64,1024]{1,0:T(8,128)} %slice.29), channel_id=1, source_target_pairs={{0,2},{2,0},{4,6},{6,4},{8,10},{10,8},{12,14},{14,12},{16,18},{18,... | collective-permute-start | bytes 786440 | tf_op jit(solution)/shard_map/ppermute | solution.py:74
  11.3 27.3 %collective-permute-start.4 = (f32[128,2048]{1,0:T(8,128)}, f32[128,2048]{1,0:T(8,128)}, u32[]{:S(2)}, u32[]{:S(2)}) collective-permute-start(f32[128,2048]{1,0:T(8,128)} %pad_maximum_fusion.refs_0_), channel_id=1, source_target_pairs={{0,8},{2,10},{4,12},{6,14},{8,16},{10,18},{12,20},{14,22},{16,24},... | collective-permute-start | bytes 3145736 | tf_op jit(solution)/shard_map/ppermute | solution.py:74
  40.3 34.6 %collective-permute-start.7 = (f32[512,768]{1,0:T(8,128)}, f32[512,768]{1,0:T(8,128)}, u32[]{:S(2)}, u32[]{:S(2)}) collective-permute-start(f32[512,768]{1,0:T(8,128)} %get-tuple-element.98), channel_id=1, source_target_pairs={{0,2},{2,0},{4,6},{6,4},{8,10},{10,8},{12,14},{14,12},{16,18},{18,... | collective-permute-start | bytes 4718600 | tf_op jit(solution)/shard_map/ppermute | solution.py:74
  40.8 34.4 %collective-permute-start.8 = (f32[512,768]{1,0:T(8,128)}, f32[512,768]{1,0:T(8,128)}, u32[]{:S(2)}, u32[]{:S(2)}) collective-permute-start(f32[512,768]{1,0:T(8,128)} %get-tuple-element.99), channel_id=1, source_target_pairs={{0,4},{2,6},{4,0},{6,2},{8,12},{10,14},{12,8},{14,10},{16,20},{18,... | collective-permute-start | bytes 4718600 | tf_op jit(solution)/shard_map/ppermute | solution.py:74
  42.4 24.6 %collective-permute-start.9 = (f32[128,2048]{1,0:T(8,128)}, f32[128,2048]{1,0:T(8,128)}, u32[]{:S(2)}, u32[]{:S(2)}) collective-permute-start(f32[128,2048]{1,0:T(8,128)} %get-tuple-element.104.refs_3_), channel_id=1, source_target_pairs={{0,8},{2,10},{4,12},{6,14},{8,16},{10,18},{12,20},{14,22},{16,24},... | collective-permute-start | bytes 3145736 | tf_op jit(solution)/shard_map/ppermute | solution.py:74
  75.2 24.3 %collective-permute-start.12 = (f32[128,2048]{1,0:T(8,128)}, f32[128,2048]{1,0:T(8,128)}, u32[]{:S(2)}, u32[]{:S(2)}) collective-permute-start(f32[128,2048]{1,0:T(8,128)} %get-tuple-element.112.refs_2_), channel_id=1, source_target_pairs={{0,8},{2,10},{4,12},{6,14},{8,16},{10,18},{12,20},{14,22},{16,24},... | collective-permute-start | bytes 3145736 | tf_op jit(solution)/shard_map/ppermute | solution.py:74
  81.9 16.3 %collective-permute-start.10 = (f32[256,768]{1,0:T(8,128)}, f32[256,768]{1,0:T(8,128)}, u32[]{:S(2)}, u32[]{:S(2)}) collective-permute-start(f32[256,768]{1,0:T(8,128)} %get-tuple-element.110), channel_id=1, source_target_pairs={{0,4},{2,6},{4,0},{6,2},{8,12},{10,14},{12,8},{14,10},{16,20},{18,... | collective-permute-start | bytes 2359304 | tf_op jit(solution)/shard_map/ppermute | solution.py:74
  83.4 16.0 %collective-permute-start.11 = (f32[256,768]{1,0:T(8,128)}, f32[256,768]{1,0:T(8,128)}, u32[]{:S(2)}, u32[]{:S(2)}) collective-permute-start(f32[256,768]{1,0:T(8,128)} %get-tuple-element.111), channel_id=1, source_target_pairs={{0,2},{2,0},{4,6},{6,4},{8,10},{10,8},{12,14},{14,12},{16,18},{18,... | collective-permute-start | bytes 2359304 | tf_op jit(solution)/shard_map/ppermute | solution.py:74
  118.5 20.8 %collective-permute-start.16 = (f32[256,1024]{1,0:T(8,128)}, f32[256,1024]{1,0:T(8,128)}, u32[]{:S(2)}, u32[]{:S(2)}) collective-permute-start(f32[256,1024]{1,0:T(8,128)} %get-tuple-element.121.refs_1_), channel_id=1, source_target_pairs={{0,2},{2,0},{4,6},{6,4},{8,10},{10,8},{12,14},{14,12},{16,18},{18,... | collective-permute-start | bytes 3145736 | tf_op jit(solution)/shard_map/ppermute | solution.py:74
  119.9 23.1 %collective-permute-start.17 = (f32[256,1024]{1,0:T(8,128)}, f32[256,1024]{1,0:T(8,128)}, u32[]{:S(2)}, u32[]{:S(2)}) collective-permute-start(f32[256,1024]{1,0:T(8,128)} %get-tuple-element.122.refs_2_), channel_id=1, source_target_pairs={{0,4},{2,6},{4,0},{6,2},{8,12},{10,14},{12,8},{14,10},{16,20},{18,... | collective-permute-start | bytes 3145736 | tf_op jit(solution)/shard_map/ppermute | solution.py:74
  143.1 26.4 %collective-permute-start.21 = (f32[256,1024]{1,0:T(8,128)}, f32[256,1024]{1,0:T(8,128)}, u32[]{:S(2)}, u32[]{:S(2)}) collective-permute-start(f32[256,1024]{1,0:T(8,128)} %get-tuple-element.125.refs_0_), channel_id=1, source_target_pairs={{0,4},{2,6},{4,0},{6,2},{8,12},{10,14},{12,8},{14,10},{16,20},{18,... | collective-permute-start | bytes 3145736 | tf_op jit(solution)/shard_map/ppermute | solution.py:74
  144.4 41.8 %collective-permute-start.22 = (f32[256,1024]{1,0:T(8,128)}, f32[256,1024]{1,0:T(8,128)}, u32[]{:S(2)}, u32[]{:S(2)}) collective-permute-start(f32[256,1024]{1,0:T(8,128)} %get-tuple-element.126.refs_1_), channel_id=1, source_target_pairs={{0,4},{2,6},{4,0},{6,2},{8,12},{10,14},{12,8},{14,10},{16,20},{18,... | collective-permute-start | bytes 3145736 | tf_op jit(solution)/shard_map/ppermute | solution.py:74
  145.1 41.0 %collective-permute-start.23 = (f32[256,1024]{1,0:T(8,128)}, f32[256,1024]{1,0:T(8,128)}, u32[]{:S(2)}, u32[]{:S(2)}) collective-permute-start(f32[256,1024]{1,0:T(8,128)} %get-tuple-element.127.refs_0_), channel_id=1, source_target_pairs={{0,2},{2,0},{4,6},{6,4},{8,10},{10,8},{12,14},{14,12},{16,18},{18,... | collective-permute-start | bytes 3145736 | tf_op jit(solution)/shard_map/ppermute | solution.py:74
  145.7 40.5 %collective-permute-start.24 = (f32[256,1024]{1,0:T(8,128)}, f32[256,1024]{1,0:T(8,128)}, u32[]{:S(2)}, u32[]{:S(2)}) collective-permute-start(f32[256,1024]{1,0:T(8,128)} %get-tuple-element.128.refs_1_), channel_id=1, source_target_pairs={{0,2},{2,0},{4,6},{6,4},{8,10},{10,8},{12,14},{14,12},{16,18},{18,... | collective-permute-start | bytes 3145736 | tf_op jit(solution)/shard_map/ppermute | solution.py:74
  166.7 19.4 %collective-permute-start.20 = (f32[64,1536]{1,0:T(8,128)S(1)}, f32[64,1536]{1,0:T(8,128)}, u32[]{:S(2)}, u32[]{:S(2)}) collective-permute-start(f32[64,1536]{1,0:T(8,128)S(1)} %collective-permute-done.19.refs_2_), channel_id=1, source_target_pairs={{0,8},{2,10},{4,12},{6,14},{8,16},{10,18},{12,20},{14,22},{16,24},... | collective-permute-start | bytes 1179656 | tf_op jit(solution)/shard_map/ppermute | solution.py:74
  186.2 36.8 %collective-permute-start.25 = (f32[256,1024]{1,0:T(8,128)}, f32[256,1024]{1,0:T(8,128)}, u32[]{:S(2)}, u32[]{:S(2)}) collective-permute-start(f32[256,1024]{1,0:T(8,128)} %get-tuple-element.129.refs_0_), channel_id=1, source_target_pairs={{0,8},{2,10},{4,12},{6,14},{8,16},{10,18},{12,20},{14,22},{16,24},... | collective-permute-start | bytes 3145736 | tf_op jit(solution)/shard_map/ppermute | solution.py:74
  188.9 20.7 %collective-permute-start.26 = (f32[256,768]{1,0:T(8,128)}, f32[256,768]{1,0:T(8,128)}, u32[]{:S(2)}, u32[]{:S(2)}) collective-permute-start(f32[256,768]{1,0:T(8,128)} %get-tuple-element.131.refs_0_), channel_id=1, source_target_pairs={{0,4},{2,6},{4,0},{6,2},{8,12},{10,14},{12,8},{14,10},{16,20},{18,... | collective-permute-start | bytes 2359304 | tf_op jit(solution)/shard_map/ppermute | solution.py:74
  190.2 19.4 %collective-permute-start.27 = (f32[256,768]{1,0:T(8,128)}, f32[256,768]{1,0:T(8,128)}, u32[]{:S(2)}, u32[]{:S(2)}) collective-permute-start(f32[256,768]{1,0:T(8,128)} %get-tuple-element.131.refs_0_), channel_id=1, source_target_pairs={{0,2},{2,0},{4,6},{6,4},{8,10},{10,8},{12,14},{14,12},{16,18},{18,... | collective-permute-start | bytes 2359304 | tf_op jit(solution)/shard_map/ppermute | solution.py:74
  190.7 31.8 %collective-permute-start.28 = (f32[256,768]{1,0:T(8,128)}, f32[256,768]{1,0:T(8,128)}, u32[]{:S(2)}, u32[]{:S(2)}) collective-permute-start(f32[256,768]{1,0:T(8,128)} %get-tuple-element.132.refs_3_), channel_id=1, source_target_pairs={{0,2},{2,0},{4,6},{6,4},{8,10},{10,8},{12,14},{14,12},{16,18},{18,... | collective-permute-start | bytes 2359304 | tf_op jit(solution)/shard_map/ppermute | solution.py:74
  192.2 30.8 %collective-permute-start.29 = (f32[256,768]{1,0:T(8,128)}, f32[256,768]{1,0:T(8,128)}, u32[]{:S(2)}, u32[]{:S(2)}) collective-permute-start(f32[256,768]{1,0:T(8,128)} %get-tuple-element.132.refs_3_), channel_id=1, source_target_pairs={{0,4},{2,6},{4,0},{6,2},{8,12},{10,14},{12,8},{14,10},{16,20},{18,... | collective-permute-start | bytes 2359304 | tf_op jit(solution)/shard_map/ppermute | solution.py:74
  223.0 16.9 %collective-permute-start.32 = (f32[256,1024]{1,0:T(8,128)}, f32[256,1024]{1,0:T(8,128)}, u32[]{:S(2)}, u32[]{:S(2)}) collective-permute-start(f32[256,1024]{1,0:T(8,128)} %get-tuple-element.135.refs_3_), channel_id=1, source_target_pairs={{0,8},{2,10},{4,12},{6,14},{8,16},{10,18},{12,20},{14,22},{16,24},... | collective-permute-start | bytes 3145736 | tf_op jit(solution)/shard_map/ppermute | solution.py:74
  248.3 26.9 %collective-permute-start.36 = (f32[256,1024]{1,0:T(8,128)}, f32[256,1024]{1,0:T(8,128)}, u32[]{:S(2)}, u32[]{:S(2)}) collective-permute-start(f32[256,1024]{1,0:T(8,128)} %get-tuple-element.154.refs_2_), channel_id=1, source_target_pairs={{0,4},{2,6},{4,0},{6,2},{8,12},{10,14},{12,8},{14,10},{16,20},{18,... | collective-permute-start | bytes 3145736 | tf_op jit(solution)/shard_map/ppermute | solution.py:74
  249.6 25.6 %collective-permute-start.37 = (f32[256,1024]{1,0:T(8,128)}, f32[256,1024]{1,0:T(8,128)}, u32[]{:S(2)}, u32[]{:S(2)}) collective-permute-start(f32[256,1024]{1,0:T(8,128)} %get-tuple-element.155.refs_2_), channel_id=1, source_target_pairs={{0,2},{2,0},{4,6},{6,4},{8,10},{10,8},{12,14},{14,12},{16,18},{18,... | collective-permute-start | bytes 3145736 | tf_op jit(solution)/shard_map/ppermute | solution.py:74
  250.1 26.6 %collective-permute-start.35 = (f32[256,1024]{1,0:T(8,128)}, f32[256,1024]{1,0:T(8,128)}, u32[]{:S(2)}, u32[]{:S(2)}) collective-permute-start(f32[256,1024]{1,0:T(8,128)} %get-tuple-element.153.refs_2_), channel_id=1, source_target_pairs={{0,8},{2,10},{4,12},{6,14},{8,16},{10,18},{12,20},{14,22},{16,24},... | collective-permute-start | bytes 3145736 | tf_op jit(solution)/shard_map/ppermute | solution.py:74
  276.7 30.0 %collective-permute-start.38 = (f32[256,1024]{1,0:T(8,128)}, f32[256,1024]{1,0:T(8,128)}, u32[]{:S(2)}, u32[]{:S(2)}) collective-permute-start(f32[256,1024]{1,0:T(8,128)} %get-tuple-element.158.refs_3_), channel_id=1, source_target_pairs={{0,8},{2,10},{4,12},{6,14},{8,16},{10,18},{12,20},{14,22},{16,24},... | collective-permute-start | bytes 3145736 | tf_op jit(solution)/shard_map/ppermute | solution.py:74
  277.4 30.6 %collective-permute-start.39 = (f32[256,1024]{1,0:T(8,128)}, f32[256,1024]{1,0:T(8,128)}, u32[]{:S(2)}, u32[]{:S(2)}) collective-permute-start(f32[256,1024]{1,0:T(8,128)} %get-tuple-element.154.refs_2_), channel_id=1, source_target_pairs={{0,2},{2,0},{4,6},{6,4},{8,10},{10,8},{12,14},{14,12},{16,18},{18,... | collective-permute-start | bytes 3145736 | tf_op jit(solution)/shard_map/ppermute | solution.py:74
  278.2 56.6 %collective-permute-start.42 = (f32[256,1024]{1,0:T(8,128)}, f32[256,1024]{1,0:T(8,128)}, u32[]{:S(2)}, u32[]{:S(2)}) collective-permute-start(f32[256,1024]{1,0:T(8,128)} %get-tuple-element.155.refs_2_), channel_id=1, source_target_pairs={{0,4},{2,6},{4,0},{6,2},{8,12},{10,14},{12,8},{14,10},{16,20},{18,... | collective-permute-start | bytes 3145736 | tf_op jit(solution)/shard_map/ppermute | solution.py:74
  279.0 44.5 %collective-permute-start.40 = (f32[256,1024]{1,0:T(8,128)}, f32[256,1024]{1,0:T(8,128)}, u32[]{:S(2)}, u32[]{:S(2)}) collective-permute-start(f32[256,1024]{1,0:T(8,128)} %get-tuple-element.163.refs_3_), channel_id=1, source_target_pairs={{0,2},{2,0},{4,6},{6,4},{8,10},{10,8},{12,14},{14,12},{16,18},{18,... | collective-permute-start | bytes 3145736 | tf_op jit(solution)/shard_map/ppermute | solution.py:74
  279.8 55.1 %collective-permute-start.43 = (f32[256,1024]{1,0:T(8,128)}, f32[256,1024]{1,0:T(8,128)}, u32[]{:S(2)}, u32[]{:S(2)}) collective-permute-start(f32[256,1024]{1,0:T(8,128)} %get-tuple-element.165.refs_3_), channel_id=1, source_target_pairs={{0,4},{2,6},{4,0},{6,2},{8,12},{10,14},{12,8},{14,10},{16,20},{18,... | collective-permute-start | bytes 3145736 | tf_op jit(solution)/shard_map/ppermute | solution.py:74
  306.8 28.1 %collective-permute-start.41 = (f32[256,1024]{1,0:T(8,128)}, f32[256,1024]{1,0:T(8,128)}, u32[]{:S(2)}, u32[]{:S(2)}) collective-permute-start(f32[256,1024]{1,0:T(8,128)} %get-tuple-element.164.refs_6_), channel_id=1, source_target_pairs={{0,8},{2,10},{4,12},{6,14},{8,16},{10,18},{12,20},{14,22},{16,24},... | collective-permute-start | bytes 3145736 | tf_op jit(solution)/shard_map/ppermute | solution.py:74
  334.9 24.6 %collective-permute-start.44 = (f32[256,1024]{1,0:T(8,128)}, f32[256,1024]{1,0:T(8,128)}, u32[]{:S(2)}, u32[]{:S(2)}) collective-permute-start(f32[256,1024]{1,0:T(8,128)} %get-tuple-element.166.refs_5_), channel_id=1, source_target_pairs={{0,8},{2,10},{4,12},{6,14},{8,16},{10,18},{12,20},{14,22},{16,24},... | collective-permute-start | bytes 3145736 | tf_op jit(solution)/shard_map/ppermute | solution.py:74
  (21 other events, 206.5 us)

commit v2 on v1

--- a/solution.py
+++ b/solution.py
@@ -178,16 +178,21 @@
     )(high, high, low, low, weight)
 
 
-def stack_kernel(count, parts, *refs):
-    for out_ref, (top, bottom, left, right) in zip(refs[count:], parts):
-        for n, ref in enumerate(refs[:count]):
-            out_ref[n * (bottom - top) : (n + 1) * (bottom - top), :] = ref[top:bottom, left:right]
-
-
-def stack(values, parts):
-    shapes = [(len(values) * (bottom - top), right - left) for top, bottom, left, right in parts]
-    return pl.pallas_call(
-        functools.partial(stack_kernel, len(values), parts),
+def stack_kernel(count, outs, *refs):
+    for out_ref, parts in zip(refs[count:], outs):
+        row = 0
+        for top, bottom, left, right in parts:
+            for ref in refs[:count]:
+                out_ref[row : row + bottom - top, :] = ref[top:bottom, left:right]
+                row += bottom - top
+
+
+def stack(values, *outs):
+    shapes = [
+        (len(values) * sum(bottom - top for top, bottom, _, _ in parts), parts[0][3] - parts[0][2]) for parts in outs
+    ]
+    return pl.pallas_call(
+        functools.partial(stack_kernel, len(values), outs),
         grid=(1,),
         in_specs=[pl.BlockSpec(value.shape, lambda n: (0, 0)) for value in values],
         out_specs=[pl.BlockSpec(shape, lambda n: (0, 0)) for shape in shapes],
@@ -331,9 +336,14 @@
             weight_high[:, columns], weight_low[:, columns] = halves(value.T)
             column += value.shape[0]
 
-    total = three_pass((weight_high[...], weight_low[...]), (high_ref[...], low_ref[...])) + bias_ref[...]
-    active = 0.5 * total * (1.0 + lax.erf(total * 0.7071067811865476))
-    out_high[...], out_low[...] = halves(active)
+    units = out_high.shape[0]
+    tile = tile_of(units)
+    for row in range(0, units, tile):
+        taken = slice(row, row + tile)
+        total = three_pass((weight_high[taken, :], weight_low[taken, :]), (high_ref[...], low_ref[...]))
+        total = total + bias_ref[taken, :]
+        active = 0.5 * total * (1.0 + lax.erf(total * 0.7071067811865476))
+        out_high[taken, :], out_low[taken, :] = halves(active)
 
 
 def expand(high, low, bias, pieces, groups):
@@ -481,6 +491,8 @@
     corner = {(b, a): [key for key in whole if key[1:] == (b, a)] for b in range(2) for a in range(2)}
     y_last = grid.segments([corner[0, 0], corner[0, 1], corner[1, 0], corner[1, 1]], rows)
     x_last = grid.segments([corner[0, 0], corner[1, 0], corner[0, 1], corner[1, 1]], rows)
+    y_last_pair = grid.segments([corner[0, 0] + corner[0, 1], corner[1, 0] + corner[1, 1]], rows)
+    x_last_pair = grid.segments([corner[0, 0] + corner[1, 0], corner[0, 1] + corner[1, 1]], rows)
     z_after_xy = grid.segments(lone("z", "yx"), rows)
     z_after_yx = grid.segments(lone("z", "xy"), rows)
 
@@ -523,32 +535,35 @@
     total = partial[deep - 1]
     for step in range(2, deep + 1):
         total = move(total, dz=1) + partial[deep - step]
-    lines = stack(grid.line(own, ring), [(r, r + rows, a, b) for r in (0, rows) for a, b in spans[:2]])
-    first, second = [[line] for line in lines[:2]], [[line] for line in lines[2:]]
-    first_step = [move(first[0][0], dx=1), move(first[1][0], dy=1)]
+    (in_a, in_b), (out_a, out_b) = [[(top, top + rows, a, b) for a, b in spans[:2]] for top in (0, rows)]
+    pack_x, pack_y, line_a, line_b = stack(grid.line(own, ring), [in_a, out_b], [in_b, out_a], [in_a], [in_b])
+    got_x, got_y = move(pack_x, dx=1), move(pack_y, dy=1)
+    in_ring = [move(in_last, dz=1)]
     activated = jax.nn.gelu(total + tok_in_bias[None, :], approximate=False)
 
-    activated, *lines = fence(activated, first[0][0], first[1][0], *first_step)
-    first = [[lines[0], lines[2]], [lines[1], lines[3]]]
+    activated, line_a, line_b, got_x, got_y, in_ring[0] = fence(activated, line_a, line_b, got_x, got_y, in_ring[0])
     ring = []
     for step in range(1, deep):
         ring.append(move(ring[-1] if ring else activated, dz=1))
-    first_step = [move(value, dy=1) for value in first[0]] + [move(value, dx=1) for value in first[1]]
-    ring[-1], in_last, *first_step = fence(ring[-1], in_last, *first_step)
-    first = [first[0] + first_step[:2], first[1] + first_step[2:]]
-
-    active_a, active_b = stack(grid.line(activated, ring), [(0, rows, 0, middle), (0, rows, middle, 2 * middle)])
+    step_a, step_b = got_x[:quarter], got_y[:quarter]
+    first_step = [move(line_a, dy=1), move(step_a, dy=1), move(line_b, dx=1), move(step_b, dx=1)]
+    ring[-1], *first_step = fence(ring[-1], *first_step)
+    first = [[line_a, step_a, *first_step[:2]], [line_b, step_b, *first_step[2:]]]
+
+    active_a, active_b = stack(grid.line(activated, ring), [(0, rows, 0, middle)], [(0, rows, middle, 2 * middle)])
+    lower = quarter, 2 * quarter, 0, ends[1]
+    second = [stack([pack_y, got_y], [lower])[0], stack([pack_x, got_x], [lower])[0]]
     arrived = [move(active_a, dy=1), move(active_a, dx=1), move(active_b, dx=1), move(active_b, dy=1)]
-    in_ring = [move(in_last, dz=1)]
-    in_ring[0], *arrived = fence(in_ring[0], *arrived)
+    in_ring.append(move(in_ring[0], dz=1))
+    in_ring[1], second[0], second[1], *arrived = fence(in_ring[1], *second, *arrived)
     last_a, last_b = move(arrived[0], dx=1), move(arrived[2], dy=1)
-    in_ring.append(move(in_ring[0], dz=1))
-    most = project(tok_out_weight, [active_a, *arrived[:2], active_b, *arrived[2:]], (0, 2, 1, 0, 1, 2))
-    last_a, last_b, in_ring[1], most = fence(last_a, last_b, in_ring[1], most)
-
     for _ in range(2, deep - 1):
         in_ring.append(move(in_ring[-1], dz=1))
-    second_step = [move(second[0][0], dy=1), move(second[1][0], dx=1)]
+    most = project(tok_out_weight, [active_a, *arrived[:2], active_b, *arrived[2:]], (0, 2, 1, 0, 1, 2))
+    last_a, last_b, in_ring[-1], most = fence(last_a, last_b, in_ring[-1], most)
+
+    second_step = [move(second[0], dx=1), move(second[1], dy=1)]
+    out_ring = [move(out_last, dz=1)]
     most = [most] + [grid.to_core(most, step) for step in range(1, ch)]
     least = project(tok_out_weight, [last_a, last_b], (0, 0))
     least = [least] + [grid.to_core(least, step) for step in range(1, ch)]
@@ -556,23 +571,20 @@
     mixed, high, low = norm_two(grid, place, gains[:, 1:], full, terms, 2, per_core)
 
     hidden = [expand(high, low, biases[0], first[0], y_last)]
-    hidden_high, out_last, in_ring[-1], *second_step = fence(hidden[0][0], out_last, in_ring[-1], *second_step)
+    hidden_high, out_ring[0] = fence(hidden[0][0], out_ring[0])
     hidden[0] = hidden_high, hidden[0][1]
-    second = [line + [step] for line, step in zip(second, second_step)]
-    second_step = [move(value, dx=1) for value in second[0]] + [move(value, dy=1) for value in second[1]]
-    out_ring = [move(out_last, dz=1)]
+    out_ring.append(move(out_ring[0], dz=1))
     hidden += [
         expand(high, low, biases[1], first[1], x_last),
         expand(high, low, biases[2], grid.line(in_last, in_ring), z_after_xy),
     ]
-    fenced = fence(hidden[1][0], hidden[2][0], out_ring[0])
+    fenced = fence(hidden[1][0], hidden[2][0], out_ring[1], *second_step)
     hidden[1:] = [(fenced[0], hidden[1][1]), (fenced[1], hidden[2][1])]
-    out_ring = [fenced[2], move(fenced[2], dz=1)]
-    (result,) = reduce(*hidden[0], second[0] + second_step[:2], x_last, None)
-    result, out_ring[1], *second_step[2:] = fence(result, out_ring[1], *second_step[2:])
+    out_ring[1], *second_step = fenced[2:]
     for _ in range(2, deep - 1):
         out_ring.append(move(out_ring[-1], dz=1))
-    (result,) = reduce(*hidden[1], second[1] + second_step[2:], y_last, result)
+    (result,) = reduce(*hidden[0], [second[0], second_step[0]], x_last_pair, None)
+    (result,) = reduce(*hidden[1], [second[1], second_step[1]], y_last_pair, result)
     spread = grid, rows, per_core
     parts = reduce(*hidden[2], grid.line(out_last, out_ring), z_after_yx, result, spread, place, mixed)
     return finish([parts[0]] + [grid.to_core(part, step) for step, part in enumerate(parts) if step])

time: 384 us -> 377 us (0.982)
  Pallas kernels: 156 us -> 166 us
  waiting for transfers between devices: 159 us -> 150 us
  starting transfers between devices: 42 us -> 33.6 us
    ppermute x41 -> x37, waiting for transfers between devices: 155 us -> 144 us  [move(): return lax.ppermute(value, 'tok', pairs)]
    ppermute x41 -> x37, starting transfers between devices: 40.8 us -> 32.4 us  [move(): return lax.ppermute(value, 'tok', pairs)]
    pallas_call x2 -> x4, Pallas kernels: 6.83 us -> 14.9 us  [stack(): pl.pallas_call(functools.partial(stack_kernel, len(values), outs), grid=(...]
  transfers between devices with their start and end apart: 46 -> 42, of which waited for: 23 -> 22; matrix products, arithmetic and copies ran while one was open for 6% -> 6% of each run, Pallas kernels for 35% -> 38%
where the time goes in v2:
time: 377 us; the launch traced here: 376 us
  Pallas kernels  166 us (44%)
  waiting for transfers between devices  150 us (40%)
  starting transfers between devices  33.6 us (9%)
  local copies, waits for them, and re-layouts  13.7 us (4%)
  other arithmetic  12.9 us (3%)
    ppermute x37, waiting for transfers between devices, move(): return lax.ppermute(value, 'tok', pairs)  144 us
    pallas_call x3, Pallas kernels, expand(): pl.pallas_call(functools.partial(expand_kernel, groups, len(pieces)), gri...  39.6 us
    pallas_call x3, Pallas kernels, reduce(): pl.pallas_call(functools.partial(reduce_kernel, groups, len(pieces), firs...  37.7 us
    ppermute x37, starting transfers between devices, move(): return lax.ppermute(value, 'tok', pairs)  32.4 us
    pallas_call x2, Pallas kernels, mix(): pl.pallas_call(functools.partial(mix_kernel, steps), grid=(2 * steps,), i...  21.7 us
    pallas_call x2, Pallas kernels, project(): pl.pallas_call(functools.partial(project_kernel, rows, places), grid=(wid...  21 us
    pallas_call x4, Pallas kernels, stack(): pl.pallas_call(functools.partial(stack_kernel, len(values), outs), grid=(...  14.9 us
    pallas_call x1, Pallas kernels, norm_two(): pl.pallas_call(functools.partial(norm_two_kernel, grid, channels // grid....  10 us
  transfers between devices with their start and end apart: 42, of which 22 were waited for; matrix products, arithmetic and copies ran while one was open for 6% of the time, Pallas kernels for 38%

profile of v2, /device:TPU:0, one launch (start us, length us, event | category | flops | bytes accessed | tf_op | source)
XLA Modules:
  0.0 376.2 jit_solution(15294245799592142450)
XLA Ops:
  3.0 2.9 collective-permute-start.3
  14.8 8.0 %norm_one.1 = (f32[1024,1024]{1,0:T(8,128)}, bf16[1024,1024]{1,0:T(8,128)(2,1)}, bf16[1024,1024]{1,0:T(8,128)(2,1)}) custom-call(s32[4]{0:T(128)} %pad_add_fusion.place_ref.refs_0_, f32[1024,1]{1,0:T(8,128)} %get-tuple-element.169.gain_ref, f32[1024,512]{1,0:T(8,128)} %refs_0_.1, f32[1024,512]{1,0:T(8,128)} %collective-permute-done.1.refs_1_), custom_call_target="tpu_custom_call" | custom-call | tf_op jit(solution)/shard_map/norm_one/pallas_call | solution.py:123
  27.6 10.8 %mix.2 = (f32[512,768]{1,0:T(8,128)}, f32[512,768]{1,0:T(8,128)}) custom-call(bf16[1024,1024]{1,0:T(8,128)(2,1)} %get-tuple-element.89.high_one.high_two, bf16[1024,1024]{1,0:T(8,128)(2,1)} %get-tuple-element.89.high_one.high_two, bf16[1024,1024]{1,0:T(8,128)(2,1)} %get-tuple-element.90.low_one.low_two, ...), custom_call_target="tpu_custom_call" | custom-call | tf_op jit(solution)/shard_map/mix/pallas_call | solution.py:166
  46.9 10.9 %mix.3 = (f32[512,768]{1,0:T(8,128)}, f32[512,768]{1,0:T(8,128)}) custom-call(bf16[1024,1024]{1,0:T(8,128)(2,1)} %get-tuple-element.89.high_one.high_two, bf16[1024,1024]{1,0:T(8,128)(2,1)} %get-tuple-element.89.high_one.high_two, bf16[1024,1024]{1,0:T(8,128)(2,1)} %get-tuple-element.90.low_one.low_two, ...), custom_call_target="tpu_custom_call" | custom-call | tf_op jit(solution)/shard_map/mix/pallas_call | solution.py:166
  57.8 3.1 pad_maximum_fusion.1
  60.8 6.1 %collective-permute-done.9.refs_6_ = f32[128,2048]{1,0:T(8,128)} collective-permute-done((f32[128,2048]{1,0:T(8,128)}, f32[128,2048]{1,0:T(8,128)}, u32[]{:S(2)}, u32[]{:S(2)}) %collective-permute-start.9) | collective-permute-done | bytes 1048608 | tf_op jit(solution)/shard_map/ppermute | solution.py:74
  66.9 7.9 %collective-permute-done.7.refs_0_ = f32[512,768]{1,0:T(8,128)} collective-permute-done((f32[512,768]{1,0:T(8,128)}, f32[512,768]{1,0:T(8,128)}, u32[]{:S(2)}, u32[]{:S(2)}) %collective-permute-start.7) | collective-permute-done | bytes 1572896 | tf_op jit(solution)/shard_map/ppermute | solution.py:74
  76.7 5.2 %halve.1 = (f32[256,768]{1,0:T(8,128)}, f32[256,768]{1,0:T(8,128)}, f32[256,768]{1,0:T(8,128)}, f32[256,768]{1,0:T(8,128)}) custom-call(f32[512,768]{1,0:T(8,128)} %get-tuple-element.102.kept_a, f32[512,768]{1,0:T(8,128)} %get-tuple-element.103.sent_a, f32[512,768]{1,0:T(8,128)} %get-tuple-element.104.kept_b, f32[512,768]{1,0:T(8,128)} %get-tuple-element.105.sent_b), custom_call_target="tpu_custom_call" | custom-call | tf_op jit(solution)/shard_map/halve/pallas_call | solution.py:216
  84.8 13.3 %collective-permute-done.10.refs_0_ = f32[256,768]{1,0:T(8,128)} collective-permute-done((f32[256,768]{1,0:T(8,128)}, f32[256,768]{1,0:T(8,128)}, u32[]{:S(2)}, u32[]{:S(2)}) %collective-permute-start.10) | collective-permute-done | bytes 786464 | tf_op jit(solution)/shard_map/ppermute | solution.py:74
  99.4 5.0 %stack.36 = (f32[512,1024]{1,0:T(8,128)}, f32[512,1024]{1,0:T(8,128)}, f32[256,1024]{1,0:T(8,128)}, f32[256,1024]{1,0:T(8,128)}) custom-call(f32[128,2048]{1,0:T(8,128)} %pad_maximum_fusion.refs_0_, f32[128,2048]{1,0:T(8,128)} %get-tuple-element.117.refs_1_, f32[128,2048]{1,0:T(8,128)} %get-tuple-element.109.refs_2_, f32[128,2048]{1,0:T(8,128)} %get-tuple-element.101.refs_3_), custom_call_target="tpu_custom_call" | custom-call | tf_op jit(solution)/shard_map/stack/pallas_call | solution.py:194
  107.1 3.0 merge.1
  111.0 9.2 %collective-permute-done.13 = f32[64,1536]{1,0:T(8,128)S(1)} collective-permute-done((f32[64,1536]{1,0:T(8,128)}, f32[64,1536]{1,0:T(8,128)S(1)}, u32[]{:S(2)}, u32[]{:S(2)}) %collective-permute-start.13) | collective-permute-done | bytes 393248 | tf_op jit(solution)/shard_map/ppermute | solution.py:74
  122.2 12.9 %collective-permute-done.14 = f32[64,1536]{1,0:T(8,128)S(1)} collective-permute-done((f32[64,1536]{1,0:T(8,128)S(1)}, f32[64,1536]{1,0:T(8,128)S(1)}, u32[]{:S(2)}, u32[]{:S(2)}) %collective-permute-start.14) | collective-permute-done | bytes 393248 | tf_op jit(solution)/shard_map/ppermute | solution.py:74
  136.2 23.0 %collective-permute-done.15 = f32[64,1536]{1,0:T(8,128)S(1)} collective-permute-done((f32[64,1536]{1,0:T(8,128)S(1)}, f32[64,1536]{1,0:T(8,128)S(1)}, u32[]{:S(2)}, u32[]{:S(2)}) %collective-permute-start.15) | collective-permute-done | bytes 393248 | tf_op jit(solution)/shard_map/ppermute | solution.py:74
  168.9 7.9 %collective-permute-done.20.refs_3_ = f32[64,1536]{1,0:T(8,128)S(1)} collective-permute-done((f32[64,1536]{1,0:T(8,128)S(1)}, f32[64,1536]{1,0:T(8,128)S(1)}, u32[]{:S(2)}, u32[]{:S(2)}) %collective-permute-start.20) | collective-permute-done | bytes 393248 | tf_op jit(solution)/shard_map/ppermute | solution.py:74
  176.8 13.8 %collective-permute-done.21.refs_2_ = f32[64,1536]{1,0:T(8,128)S(1)} collective-permute-done((f32[64,1536]{1,0:T(8,128)S(1)}, f32[64,1536]{1,0:T(8,128)S(1)}, u32[]{:S(2)}, u32[]{:S(2)}) %collective-permute-start.21) | collective-permute-done | bytes 393248 | tf_op jit(solution)/shard_map/ppermute | solution.py:74
  191.7 11.7 %collective-permute-done.23.refs_1_ = f32[256,1024]{1,0:T(8,128)S(1)} collective-permute-done((f32[256,1024]{1,0:T(8,128)S(1)}, f32[256,1024]{1,0:T(8,128)S(1)}, u32[]{:S(2)}, u32[]{:S(2)}) %collective-permute-start.23) | collective-permute-done | bytes 1048608 | tf_op jit(solution)/shard_map/ppermute | solution.py:74
  214.3 3.7 stack.38.refs_2_
  218.0 3.7 stack.37.refs_1_
  221.6 8.4 %collective-permute-done.27.refs_3_ = f32[256,768]{1,0:T(8,128)} collective-permute-done((f32[256,768]{1,0:T(8,128)}, f32[256,768]{1,0:T(8,128)}, u32[]{:S(2)}, u32[]{:S(2)}) %collective-permute-start.27) | collective-permute-done | bytes 786464 | tf_op jit(solution)/shard_map/ppermute | solution.py:74
  231.5 14.7 %collective-permute-done.29.refs_5_ = f32[256,768]{1,0:T(8,128)} collective-permute-done((f32[256,768]{1,0:T(8,128)}, f32[256,768]{1,0:T(8,128)}, u32[]{:S(2)}, u32[]{:S(2)}) %collective-permute-start.29) | collective-permute-done | bytes 786464 | tf_op jit(solution)/shard_map/ppermute | solution.py:74
  247.4 13.1 %project.2.refs_3_ = f32[768,1024]{1,0:T(8,128)} custom-call(f32[1024,1536]{1,0:T(8,128)} %weight_ref.7, f32[256,768]{1,0:T(8,128)} %get-tuple-element.130.refs_0_, f32[256,768]{1,0:T(8,128)} %get-tuple-element.132.refs_1_, f32[256,768]{1,0:T(8,128)} %get-tuple-element.135.refs_2_, f32[256,768]{1,0:T(8,128)} %get-tuple-element.131.refs_3_, ...), custom_call_target="tpu_custom_call" | custom-call | tf_op jit(solution)/shard_map/project/pallas_call | solution.py:279
  263.3 7.8 %project.3.refs_1_ = f32[256,1024]{1,0:T(8,128)} custom-call(f32[1024,1536]{1,0:T(8,128)} %weight_ref.7, f32[256,768]{1,0:T(8,128)} %get-tuple-element.138.refs_0_, f32[256,768]{1,0:T(8,128)} %get-tuple-element.139.refs_1_), custom_call_target="tpu_custom_call" | custom-call | tf_op jit(solution)/shard_map/project/pallas_call | solution.py:279
  274.2 10.0 %norm_two.1 = (f32[1024,1024]{1,0:T(8,128)}, bf16[1024,1024]{1,0:T(8,128)(2,1)}, bf16[1024,1024]{1,0:T(8,128)(2,1)}) custom-call(s32[4]{0:T(128)} %pad_add_fusion.place_ref.refs_0_, f32[1024,1]{1,0:T(8,128)} %get-tuple-element.170.gain_ref, f32[1024,1024]{1,0:T(8,128)} %get-tuple-element.87.fields_ref, f32[768,1024]{1,0:T(8,128)} %get-tuple-element.137.refs_0_, ...), custom_call_target="tpu_custom_call" | custom-call | tf_op jit(solution)/shard_map/norm_two/pallas_call | solution.py:309
  284.2 13.2 %expand.5 = (bf16[1024,1024]{1,0:T(8,128)(2,1)}, bf16[1024,1024]{1,0:T(8,128)(2,1)}) custom-call(bf16[1024,1024]{1,0:T(8,128)(2,1)} %get-tuple-element.140.high_ref, bf16[1024,1024]{1,0:T(8,128)(2,1)} %get-tuple-element.141.low_ref, f32[1024,1]{1,0:T(8,128)} %get-tuple-element.149.bias_ref, f32[256,1024]{1,0:T(8,128)} %get-tuple-element.127.refs_0_, ...), custom_call_target="tpu_custom_call" | custom-call | tf_op jit(solution)/shard_map/expand/pallas_call | solution.py:354
  300.4 13.1 %expand.4 = (bf16[1024,1024]{1,0:T(8,128)(2,1)}, bf16[1024,1024]{1,0:T(8,128)(2,1)}) custom-call(bf16[1024,1024]{1,0:T(8,128)(2,1)} %get-tuple-element.140.high_ref, bf16[1024,1024]{1,0:T(8,128)(2,1)} %get-tuple-element.141.low_ref, f32[1024,1]{1,0:T(8,128)} %get-tuple-element.146.bias_ref, f32[256,1024]{1,0:T(8,128)} %get-tuple-element.122.refs_0_, ...), custom_call_target="tpu_custom_call" | custom-call | tf_op jit(solution)/shard_map/expand/pallas_call | solution.py:354
  313.6 13.2 %expand.3 = (bf16[1024,1024]{1,0:T(8,128)(2,1)}, bf16[1024,1024]{1,0:T(8,128)(2,1)}) custom-call(bf16[1024,1024]{1,0:T(8,128)(2,1)} %get-tuple-element.140.high_ref, bf16[1024,1024]{1,0:T(8,128)(2,1)} %get-tuple-element.141.low_ref, f32[1024,1]{1,0:T(8,128)} %get-tuple-element.142.bias_ref, f32[256,1024]{1,0:T(8,128)} %get-tuple-element.128.refs_0_, ...), custom_call_target="tpu_custom_call" | custom-call | tf_op jit(solution)/shard_map/expand/pallas_call | solution.py:354
  327.0 11.4 %reduce.3.refs_4_ = f32[1024,1024]{1,0:T(8,128)} custom-call(bf16[1024,1024]{1,0:T(8,128)(2,1)} %get-tuple-element.163.refs_0_, bf16[1024,1024]{1,0:T(8,128)(2,1)} %get-tuple-element.164.refs_1_, f32[512,1024]{1,0:T(8,128)} %get-tuple-element.155.refs_2_, f32[512,1024]{1,0:T(8,128)} %get-tuple-element.165.refs_3_), custom_call_target="tpu_custom_call" | custom-call | tf_op jit(solution)/shard_map/reduce/pallas_call | solution.py:415
  338.4 12.1 %reduce.4.refs_7_ = f32[1024,1024]{1,0:T(8,128)} custom-call(bf16[1024,1024]{1,0:T(8,128)(2,1)} %get-tuple-element.160.refs_0_, bf16[1024,1024]{1,0:T(8,128)(2,1)} %get-tuple-element.161.refs_1_, f32[512,1024]{1,0:T(8,128)} %get-tuple-element.156.refs_2_, f32[512,1024]{1,0:T(8,128)} %get-tuple-element.162.refs_3_, f32[1024,1024]{1,0:T(8,128)} %reduce.3.refs_4_), custom_call_target="tpu_custom_call" | custom-call | tf_op jit(solution)/shard_map/reduce/pallas_call | solution.py:415
  353.0 14.2 %reduce.5 = (f32[512,1024]{1,0:T(8,128)}, f32[512,1024]{1,0:T(8,128)}) custom-call(s32[4]{0:T(128)} %pad_add_fusion.place_ref.refs_0_, bf16[1024,1024]{1,0:T(8,128)(2,1)} %get-tuple-element.157.refs_1_, bf16[1024,1024]{1,0:T(8,128)(2,1)} %get-tuple-element.158.refs_2_, f32[256,1024]{1,0:T(8,128)} %get-tuple-element.153.refs_3_, ...), custom_call_target="tpu_custom_call" | custom-call | tf_op jit(solution)/shard_map/reduce/pallas_call | solution.py:415
  367.2 4.5 %collective-permute-done.41.refs_1_ = f32[512,1024]{1,0:T(8,128)} collective-permute-done((f32[512,1024]{1,0:T(8,128)}, f32[512,1024]{1,0:T(8,128)}, u32[]{:S(2)}, u32[]{:S(2)}) %collective-permute-start.41) | collective-permute-done | bytes 2097184 | tf_op jit(solution)/shard_map/ppermute | solution.py:77
  371.7 4.5 %finish.1 = f32[1024,512]{1,0:T(8,128)} custom-call(f32[512,1024]{1,0:T(8,128)} %get-tuple-element.167.refs_0_, f32[512,1024]{1,0:T(8,128)} %collective-permute-done.41.refs_1_), custom_call_target="tpu_custom_call" | custom-call | tf_op jit(solution)/shard_map/finish/pallas_call | solution.py:443
  (136 shorter events, 73.6 us)
Async XLA Ops:
  0.0 14.8 %collective-permute-start.1 = (f32[1024,512]{1,0:T(8,128)}, f32[1024,512]{1,0:T(8,128)}, u32[]{:S(2)}, u32[]{:S(2)}) collective-permute-start(f32[1024,512]{1,0:T(8,128)} %refs_0_.1), channel_id=1, source_target_pairs={{0,1},{1,0},{2,3},{3,2},{4,5},{5,4},{6,7},{7,6},{8,9},{9,8},{10,11... | collective-permute-start | bytes 6291464 | tf_op jit(solution)/shard_map/ppermute | solution.py:77
  3.0 19.8 %collective-permute-start.3 = (f32[64,1024]{1,0:T(8,128)}, f32[64,1024]{1,0:T(8,128)}, u32[]{:S(2)}, u32[]{:S(2)}) collective-permute-start(f32[64,1024]{1,0:T(8,128)} %slice.46), channel_id=1, source_target_pairs={{0,4},{2,6},{4,0},{6,2},{8,12},{10,14},{12,8},{14,10},{16,20},{18,... | collective-permute-start | bytes 786440 | tf_op jit(solution)/shard_map/ppermute | solution.py:74
  7.6 15.2 %collective-permute-start.2 = (f32[64,1024]{1,0:T(8,128)}, f32[64,1024]{1,0:T(8,128)}, u32[]{:S(2)}, u32[]{:S(2)}) collective-permute-start(f32[64,1024]{1,0:T(8,128)} %slice.35), channel_id=1, source_target_pairs={{0,2},{2,0},{4,6},{6,4},{8,10},{10,8},{12,14},{14,12},{16,18},{18,... | collective-permute-start | bytes 786440 | tf_op jit(solution)/shard_map/ppermute | solution.py:74
  11.2 27.3 %collective-permute-start.4 = (f32[128,2048]{1,0:T(8,128)}, f32[128,2048]{1,0:T(8,128)}, u32[]{:S(2)}, u32[]{:S(2)}) collective-permute-start(f32[128,2048]{1,0:T(8,128)} %pad_maximum_fusion.refs_0_), channel_id=1, source_target_pairs={{0,8},{2,10},{4,12},{6,14},{8,16},{10,18},{12,20},{14,22},{16,24},... | collective-permute-start | bytes 3145736 | tf_op jit(solution)/shard_map/ppermute | solution.py:74
  40.2 34.6 %collective-permute-start.7 = (f32[512,768]{1,0:T(8,128)}, f32[512,768]{1,0:T(8,128)}, u32[]{:S(2)}, u32[]{:S(2)}) collective-permute-start(f32[512,768]{1,0:T(8,128)} %get-tuple-element.95), channel_id=1, source_target_pairs={{0,2},{2,0},{4,6},{6,4},{8,10},{10,8},{12,14},{14,12},{16,18},{18,... | collective-permute-start | bytes 4718600 | tf_op jit(solution)/shard_map/ppermute | solution.py:74
  40.7 34.4 %collective-permute-start.8 = (f32[512,768]{1,0:T(8,128)}, f32[512,768]{1,0:T(8,128)}, u32[]{:S(2)}, u32[]{:S(2)}) collective-permute-start(f32[512,768]{1,0:T(8,128)} %get-tuple-element.96), channel_id=1, source_target_pairs={{0,4},{2,6},{4,0},{6,2},{8,12},{10,14},{12,8},{14,10},{16,20},{18,... | collective-permute-start | bytes 4718600 | tf_op jit(solution)/shard_map/ppermute | solution.py:74
  42.3 24.6 %collective-permute-start.9 = (f32[128,2048]{1,0:T(8,128)}, f32[128,2048]{1,0:T(8,128)}, u32[]{:S(2)}, u32[]{:S(2)}) collective-permute-start(f32[128,2048]{1,0:T(8,128)} %get-tuple-element.101.refs_3_), channel_id=1, source_target_pairs={{0,8},{2,10},{4,12},{6,14},{8,16},{10,18},{12,20},{14,22},{16,24},... | collective-permute-start | bytes 3145736 | tf_op jit(solution)/shard_map/ppermute | solution.py:74
  75.1 24.3 %collective-permute-start.12 = (f32[128,2048]{1,0:T(8,128)}, f32[128,2048]{1,0:T(8,128)}, u32[]{:S(2)}, u32[]{:S(2)}) collective-permute-start(f32[128,2048]{1,0:T(8,128)} %get-tuple-element.109.refs_2_), channel_id=1, source_target_pairs={{0,8},{2,10},{4,12},{6,14},{8,16},{10,18},{12,20},{14,22},{16,24},... | collective-permute-start | bytes 3145736 | tf_op jit(solution)/shard_map/ppermute | solution.py:74
  81.8 16.3 %collective-permute-start.10 = (f32[256,768]{1,0:T(8,128)}, f32[256,768]{1,0:T(8,128)}, u32[]{:S(2)}, u32[]{:S(2)}) collective-permute-start(f32[256,768]{1,0:T(8,128)} %get-tuple-element.107), channel_id=1, source_target_pairs={{0,4},{2,6},{4,0},{6,2},{8,12},{10,14},{12,8},{14,10},{16,20},{18,... | collective-permute-start | bytes 2359304 | tf_op jit(solution)/shard_map/ppermute | solution.py:74
  83.4 16.0 %collective-permute-start.11 = (f32[256,768]{1,0:T(8,128)}, f32[256,768]{1,0:T(8,128)}, u32[]{:S(2)}, u32[]{:S(2)}) collective-permute-start(f32[256,768]{1,0:T(8,128)} %get-tuple-element.108), channel_id=1, source_target_pairs={{0,2},{2,0},{4,6},{6,4},{8,10},{10,8},{12,14},{14,12},{16,18},{18,... | collective-permute-start | bytes 2359304 | tf_op jit(solution)/shard_map/ppermute | solution.py:74
  104.4 56.5 %collective-permute-start.16 = (f32[512,1024]{1,0:T(8,128)}, f32[512,1024]{1,0:T(8,128)}, u32[]{:S(2)}, u32[]{:S(2)}) collective-permute-start(f32[512,1024]{1,0:T(8,128)} %get-tuple-element.120.refs_0_), channel_id=1, source_target_pairs={{0,2},{2,0},{4,6},{6,4},{8,10},{10,8},{12,14},{14,12},{16,18},{18,... | collective-permute-start | bytes 6291464 | tf_op jit(solution)/shard_map/ppermute | solution.py:74
  105.9 55.0 %collective-permute-start.17 = (f32[512,1024]{1,0:T(8,128)}, f32[512,1024]{1,0:T(8,128)}, u32[]{:S(2)}, u32[]{:S(2)}) collective-permute-start(f32[512,1024]{1,0:T(8,128)} %get-tuple-element.121.refs_0_), channel_id=1, source_target_pairs={{0,4},{2,6},{4,0},{6,2},{8,12},{10,14},{12,8},{14,10},{16,20},{18,... | collective-permute-start | bytes 6291464 | tf_op jit(solution)/shard_map/ppermute | solution.py:74
  121.2 13.9 %collective-permute-start.14 = (f32[64,1536]{1,0:T(8,128)S(1)}, f32[64,1536]{1,0:T(8,128)S(1)}, u32[]{:S(2)}, u32[]{:S(2)}) collective-permute-start(f32[64,1536]{1,0:T(8,128)S(1)} %add.28), channel_id=1, source_target_pairs={{0,8},{2,10},{4,12},{6,14},{8,16},{10,18},{12,20},{14,22},{16,24},... | collective-permute-start | bytes 1179656 | tf_op jit(solution)/shard_map/ppermute | solution.py:74
  121.3 39.6 %collective-permute-start.18 = (f32[256,1024]{1,0:T(8,128)}, f32[256,1024]{1,0:T(8,128)}, u32[]{:S(2)}, u32[]{:S(2)}) collective-permute-start(f32[256,1024]{1,0:T(8,128)} %get-tuple-element.122.refs_0_), channel_id=1, source_target_pairs={{0,8},{2,10},{4,12},{6,14},{8,16},{10,18},{12,20},{14,22},{16,24},... | collective-permute-start | bytes 3145736 | tf_op jit(solution)/shard_map/ppermute | solution.py:74
  136.2 23.1 %collective-permute-start.15 = (f32[64,1536]{1,0:T(8,128)S(1)}, f32[64,1536]{1,0:T(8,128)S(1)}, u32[]{:S(2)}, u32[]{:S(2)}) collective-permute-start(f32[64,1536]{1,0:T(8,128)S(1)} %add.29), channel_id=1, source_target_pairs={{0,8},{2,10},{4,12},{6,14},{8,16},{10,18},{12,20},{14,22},{16,24},... | collective-permute-start | bytes 1179656 | tf_op jit(solution)/shard_map/ppermute | solution.py:74
  162.4 28.1 %collective-permute-start.24 = (f32[256,1024]{1,0:T(8,128)S(1)}, f32[256,1024]{1,0:T(8,128)S(1)}, u32[]{:S(2)}, u32[]{:S(2)}) collective-permute-start(f32[256,1024]{1,0:T(8,128)S(1)} %slice.42.refs_1_), channel_id=1, source_target_pairs={{0,4},{2,6},{4,0},{6,2},{8,12},{10,14},{12,8},{14,10},{16,20},{18,... | collective-permute-start | bytes 3145736 | tf_op jit(solution)/shard_map/ppermute | solution.py:74
  165.6 26.1 %collective-permute-start.26 = (f32[256,1024]{1,0:T(8,128)S(1)}, f32[256,1024]{1,0:T(8,128)S(1)}, u32[]{:S(2)}, u32[]{:S(2)}) collective-permute-start(f32[256,1024]{1,0:T(8,128)S(1)} %slice.43.refs_1_), channel_id=1, source_target_pairs={{0,2},{2,0},{4,6},{6,4},{8,10},{10,8},{12,14},{14,12},{16,18},{18,... | collective-permute-start | bytes 3145736 | tf_op jit(solution)/shard_map/ppermute | solution.py:74
  166.2 37.3 %collective-permute-start.23 = (f32[256,1024]{1,0:T(8,128)S(1)}, f32[256,1024]{1,0:T(8,128)S(1)}, u32[]{:S(2)}, u32[]{:S(2)}) collective-permute-start(f32[256,1024]{1,0:T(8,128)S(1)} %copy-done.6), channel_id=1, source_target_pairs={{0,4},{2,6},{4,0},{6,2},{8,12},{10,14},{12,8},{14,10},{16,20},{18,... | collective-permute-start | bytes 3145736 | tf_op jit(solution)/shard_map/ppermute | solution.py:74
  167.4 38.7 %collective-permute-start.25 = (f32[256,1024]{1,0:T(8,128)S(1)}, f32[256,1024]{1,0:T(8,128)S(1)}, u32[]{:S(2)}, u32[]{:S(2)}) collective-permute-start(f32[256,1024]{1,0:T(8,128)S(1)} %copy-done.7), channel_id=1, source_target_pairs={{0,2},{2,0},{4,6},{6,4},{8,10},{10,8},{12,14},{14,12},{16,18},{18,... | collective-permute-start | bytes 3145736 | tf_op jit(solution)/shard_map/ppermute | solution.py:74
  190.5 16.6 %collective-permute-start.22 = (f32[64,1536]{1,0:T(8,128)S(1)}, f32[64,1536]{1,0:T(8,128)}, u32[]{:S(2)}, u32[]{:S(2)}) collective-permute-start(f32[64,1536]{1,0:T(8,128)S(1)} %collective-permute-done.21.refs_2_), channel_id=1, source_target_pairs={{0,8},{2,10},{4,12},{6,14},{8,16},{10,18},{12,20},{14,22},{16,24},... | collective-permute-start | bytes 1179656 | tf_op jit(solution)/shard_map/ppermute | solution.py:74
  190.5 31.1 %collective-permute-start.19 = (f32[256,1024]{1,0:T(8,128)}, f32[256,1024]{1,0:T(8,128)}, u32[]{:S(2)}, u32[]{:S(2)}) collective-permute-start(f32[256,1024]{1,0:T(8,128)} %get-tuple-element.123.refs_3_), channel_id=1, source_target_pairs={{0,8},{2,10},{4,12},{6,14},{8,16},{10,18},{12,20},{14,22},{16,24},... | collective-permute-start | bytes 3145736 | tf_op jit(solution)/shard_map/ppermute | solution.py:74
  209.7 20.3 %collective-permute-start.27 = (f32[256,768]{1,0:T(8,128)}, f32[256,768]{1,0:T(8,128)}, u32[]{:S(2)}, u32[]{:S(2)}) collective-permute-start(f32[256,768]{1,0:T(8,128)} %get-tuple-element.130.refs_0_), channel_id=1, source_target_pairs={{0,4},{2,6},{4,0},{6,2},{8,12},{10,14},{12,8},{14,10},{16,20},{18,... | collective-permute-start | bytes 2359304 | tf_op jit(solution)/shard_map/ppermute | solution.py:74
  212.3 19.2 %collective-permute-start.28 = (f32[256,768]{1,0:T(8,128)}, f32[256,768]{1,0:T(8,128)}, u32[]{:S(2)}, u32[]{:S(2)}) collective-permute-start(f32[256,768]{1,0:T(8,128)} %get-tuple-element.130.refs_0_), channel_id=1, source_target_pairs={{0,2},{2,0},{4,6},{6,4},{8,10},{10,8},{12,14},{14,12},{16,18},{18,... | collective-permute-start | bytes 2359304 | tf_op jit(solution)/shard_map/ppermute | solution.py:74
  212.8 33.4 %collective-permute-start.29 = (f32[256,768]{1,0:T(8,128)}, f32[256,768]{1,0:T(8,128)}, u32[]{:S(2)}, u32[]{:S(2)}) collective-permute-start(f32[256,768]{1,0:T(8,128)} %get-tuple-element.131.refs_3_), channel_id=1, source_target_pairs={{0,2},{2,0},{4,6},{6,4},{8,10},{10,8},{12,14},{14,12},{16,18},{18,... | collective-permute-start | bytes 2359304 | tf_op jit(solution)/shard_map/ppermute | solution.py:74
  214.3 31.9 %collective-permute-start.30 = (f32[256,768]{1,0:T(8,128)}, f32[256,768]{1,0:T(8,128)}, u32[]{:S(2)}, u32[]{:S(2)}) collective-permute-start(f32[256,768]{1,0:T(8,128)} %get-tuple-element.131.refs_3_), channel_id=1, source_target_pairs={{0,4},{2,6},{4,0},{6,2},{8,12},{10,14},{12,8},{14,10},{16,20},{18,... | collective-permute-start | bytes 2359304 | tf_op jit(solution)/shard_map/ppermute | solution.py:74
  246.2 17.1 %collective-permute-start.33 = (f32[256,1024]{1,0:T(8,128)}, f32[256,1024]{1,0:T(8,128)}, u32[]{:S(2)}, u32[]{:S(2)}) collective-permute-start(f32[256,1024]{1,0:T(8,128)} %get-tuple-element.134.refs_2_), channel_id=1, source_target_pairs={{0,8},{2,10},{4,12},{6,14},{8,16},{10,18},{12,20},{14,22},{16,24},... | collective-permute-start | bytes 3145736 | tf_op jit(solution)/shard_map/ppermute | solution.py:74
  246.2 14.3 %collective-permute-start.31 = (f32[256,768]{1,0:T(8,128)}, f32[256,768]{1,0:T(8,128)}, u32[]{:S(2)}, u32[]{:S(2)}) collective-permute-start(f32[256,768]{1,0:T(8,128)} %get-tuple-element.132.refs_1_), channel_id=1, source_target_pairs={{0,2},{2,0},{4,6},{6,4},{8,10},{10,8},{12,14},{14,12},{16,18},{18,... | collective-permute-start | bytes 2359304 | tf_op jit(solution)/shard_map/ppermute | solution.py:74
  271.6 27.2 %collective-permute-start.36 = (f32[256,1024]{1,0:T(8,128)}, f32[256,1024]{1,0:T(8,128)}, u32[]{:S(2)}, u32[]{:S(2)}) collective-permute-start(f32[256,1024]{1,0:T(8,128)} %get-tuple-element.153.refs_3_), channel_id=1, source_target_pairs={{0,8},{2,10},{4,12},{6,14},{8,16},{10,18},{12,20},{14,22},{16,24},... | collective-permute-start | bytes 3145736 | tf_op jit(solution)/shard_map/ppermute | solution.py:74
  271.6 55.2 %collective-permute-start.38 = (f32[512,1024]{1,0:T(8,128)}, f32[512,1024]{1,0:T(8,128)}, u32[]{:S(2)}, u32[]{:S(2)}) collective-permute-start(f32[512,1024]{1,0:T(8,128)} %get-tuple-element.155.refs_2_), channel_id=1, source_target_pairs={{0,2},{2,0},{4,6},{6,4},{8,10},{10,8},{12,14},{14,12},{16,18},{18,... | collective-permute-start | bytes 6291464 | tf_op jit(solution)/shard_map/ppermute | solution.py:74
  272.2 54.7 %collective-permute-start.39 = (f32[512,1024]{1,0:T(8,128)}, f32[512,1024]{1,0:T(8,128)}, u32[]{:S(2)}, u32[]{:S(2)}) collective-permute-start(f32[512,1024]{1,0:T(8,128)} %get-tuple-element.156.refs_2_), channel_id=1, source_target_pairs={{0,4},{2,6},{4,0},{6,2},{8,12},{10,14},{12,8},{14,10},{16,20},{18,... | collective-permute-start | bytes 6291464 | tf_op jit(solution)/shard_map/ppermute | solution.py:74
  298.8 28.0 %collective-permute-start.37 = (f32[256,1024]{1,0:T(8,128)}, f32[256,1024]{1,0:T(8,128)}, u32[]{:S(2)}, u32[]{:S(2)}) collective-permute-start(f32[256,1024]{1,0:T(8,128)} %get-tuple-element.154.refs_6_), channel_id=1, source_target_pairs={{0,8},{2,10},{4,12},{6,14},{8,16},{10,18},{12,20},{14,22},{16,24},... | collective-permute-start | bytes 3145736 | tf_op jit(solution)/shard_map/ppermute | solution.py:74
  326.9 26.1 %collective-permute-start.40 = (f32[256,1024]{1,0:T(8,128)}, f32[256,1024]{1,0:T(8,128)}, u32[]{:S(2)}, u32[]{:S(2)}) collective-permute-start(f32[256,1024]{1,0:T(8,128)} %get-tuple-element.159.refs_5_), channel_id=1, source_target_pairs={{0,8},{2,10},{4,12},{6,14},{8,16},{10,18},{12,20},{14,22},{16,24},... | collective-permute-start | bytes 3145736 | tf_op jit(solution)/shard_map/ppermute | solution.py:74
  (27 other events, 355.6 us)

commit v3 on v2

--- a/solution.py
+++ b/solution.py
@@ -203,43 +203,42 @@
     )(*values)
 
 
-def halve_kernel(kept_a, sent_a, kept_b, sent_b, *outs):
-    for kept, sent, (top, bottom) in ((kept_a, sent_a, outs[:2]), (kept_b, sent_b, outs[2:])):
-        total = kept[...] + sent[...]
-        top[...], bottom[...] = total[: total.shape[0] // 2], total[total.shape[0] // 2 :]
+def halve_kernel(kept_a, sent_a, kept_b, sent_b, out_a, out_b):
+    out_a[...] = kept_a[...] + sent_a[...]
+    out_b[...] = kept_b[...] + sent_b[...]
 
 
 def halve(values):
     rows, units = values[0].shape
     tile = tile_of(units)
-    column = lambda n: (0, n)
     return pl.pallas_call(
         halve_kernel,
         grid=(units // tile,),
-        in_specs=[pl.BlockSpec((rows, tile), column)] * 4,
-        out_specs=[pl.BlockSpec((rows // 2, tile), column)] * 4,
-        out_shape=[jax.ShapeDtypeStruct((rows // 2, units), jnp.float32)] * 4,
+        in_specs=[pl.BlockSpec((rows // 2, tile), lambda n: (1, n))] * 4,
+        out_specs=[pl.BlockSpec((rows // 2, tile), lambda n: (0, n))] * 2,
+        out_shape=[jax.ShapeDtypeStruct((rows // 2, units), jnp.float32)] * 2,
         compiler_params=pltpu.CompilerParams(vmem_limit_bytes=grant),
         cost_estimate=light,
         name="halve",
     )(*values)
 
 
-def merge_kernel(kept_a, sent_a, kept_b, sent_b, *outs):
+def merge_kernel(*refs):
+    (kept_a, sent_a, last_a, kept_b, sent_b, last_b), outs = refs[:6], refs[6:]
     middle = kept_a.shape[1]
     for n, out_ref in enumerate(outs):
         block = slice(n * out_ref.shape[0], (n + 1) * out_ref.shape[0])
-        out_ref[:, :middle] = kept_a[block, :] + sent_a[block, :]
-        out_ref[:, middle:] = kept_b[block, :] + sent_b[block, :]
+        out_ref[:, :middle] = kept_a[block, :] + sent_a[block, :] + last_a[block, :]
+        out_ref[:, middle:] = kept_b[block, :] + sent_b[block, :] + last_b[block, :]
 
 
 def merge(values, deep):
-    rows, units = values[0].shape
+    rows, units = values[2].shape
     shape = rows // deep, 2 * units
     return pl.pallas_call(
         merge_kernel,
         grid=(1,),
-        in_specs=[pl.BlockSpec(value.shape, lambda n: (0, 0)) for value in values],
+        in_specs=[pl.BlockSpec((rows, units), lambda n: (0, 0))] * 6,
         out_specs=[pl.BlockSpec(shape, lambda n: (0, 0))] * deep,
         out_shape=[jax.ShapeDtypeStruct(shape, jnp.float32)] * deep,
         compiler_params=pltpu.CompilerParams(vmem_limit_bytes=grant),
@@ -248,7 +247,7 @@
     )(*values)
 
 
-def project_kernel(rows, places, weight_ref, *refs):
+def project_kernel(rows, places, high, low, *refs):
     pieces, (out_ref, active_high, active_low) = refs[:-3], refs[-3:]
     count = len(pieces) // 2
     middle = pieces[0].shape[1]
@@ -258,7 +257,6 @@
         for n, piece in enumerate(pieces):
             active_high[n * rows : (n + 1) * rows, :], active_low[n * rows : (n + 1) * rows, :] = halves(piece[...])
 
-    high, low = halves(weight_ref[...].T)
     sums = []
     for part in range(2):
         taken = slice(part * count * rows, (part + 1) * count * rows)
@@ -271,15 +269,15 @@
         out_ref[target, :] = functools.reduce(lambda a, b: a + b, terms)
 
 
-def project(weight, pieces, places):
-    width, units = weight.shape
+def project(high, low, pieces, places):
+    units, width = high.shape
     rows = pieces[0].shape[0]
     groups = 1 + max(places)
     tile = tile_of(width)
     return pl.pallas_call(
         functools.partial(project_kernel, rows, places),
         grid=(width // tile,),
-        in_specs=[pl.BlockSpec((tile, units), lambda n: (n, 0))]
+        in_specs=[pl.BlockSpec((units, tile), lambda n: (0, n))] * 2
         + [pl.BlockSpec(piece.shape, lambda n: (0, 0)) for piece in pieces],
         out_specs=pl.BlockSpec((groups * rows, tile), lambda n: (0, n)),
         out_shape=jax.ShapeDtypeStruct((groups * rows, width), jnp.float32),
@@ -287,7 +285,7 @@
         compiler_params=pltpu.CompilerParams(vmem_limit_bytes=grant),
         cost_estimate=light,
         name="project",
-    )(weight, *pieces)
+    )(high, low, *pieces)
 
 
 def norm_two_kernel(grid, rows, per_core, parts, place_ref, gain_ref, fields_ref, *refs):
@@ -324,31 +322,48 @@
     )(place, gain, fields, *terms)
 
 
+def prepare_kernel(groups, count, *refs):
+    pieces, (high_ref, low_ref) = refs[:count], refs[count:]
+    column = 0
+    for group in groups:
+        value = join([pieces[n][start : start + rows, :] for n, start, rows in group])
+        columns = slice(column, column + value.shape[0])
+        high_ref[:, columns], low_ref[:, columns] = halves(value.T)
+        column += value.shape[0]
+
+
+def prepare(pieces, groups):
+    shape = pieces[0].shape[1], sum(piece.shape[0] for piece in pieces)
+    return pl.pallas_call(
+        functools.partial(prepare_kernel, groups, len(pieces)),
+        grid=(1,),
+        in_specs=[pl.BlockSpec(piece.shape, lambda n: (0, 0)) for piece in pieces],
+        out_specs=[pl.BlockSpec(shape, lambda n: (0, 0))] * 2,
+        out_shape=[jax.ShapeDtypeStruct(shape, jnp.bfloat16)] * 2,
+        compiler_params=pltpu.CompilerParams(vmem_limit_bytes=grant),
+        cost_estimate=light,
+        name="prepare",
+    )(*pieces)
+
+
 def expand_kernel(groups, count, high_ref, low_ref, bias_ref, *refs):
-    pieces, (out_high, out_low, weight_high, weight_low) = refs[:count], refs[count:]
-
-    @pl.when(pl.program_id(0) == 0)
-    def _():
-        column = 0
-        for group in groups:
-            value = jnp.concatenate([pieces[n][start : start + rows, :] for n, start, rows in group], axis=0)
-            columns = slice(column, column + value.shape[0])
-            weight_high[:, columns], weight_low[:, columns] = halves(value.T)
-            column += value.shape[0]
-
-    units = out_high.shape[0]
-    tile = tile_of(units)
-    for row in range(0, units, tile):
-        taken = slice(row, row + tile)
-        total = three_pass((weight_high[taken, :], weight_low[taken, :]), (high_ref[...], low_ref[...]))
-        total = total + bias_ref[taken, :]
-        active = 0.5 * total * (1.0 + lax.erf(total * 0.7071067811865476))
-        out_high[taken, :], out_low[taken, :] = halves(active)
-
-
-def expand(high, low, bias, pieces, groups):
+    pieces, outs, weights = refs[:count], refs[count : count + 2], refs[count + 2 :]
+    if weights:
+
+        @pl.when(pl.program_id(0) == 0)
+        def _():
+            prepare_kernel(groups, count, *pieces, *weights)
+
+    else:
+        weights = pieces
+    total = three_pass((weights[0][...], weights[1][...]), (high_ref[...], low_ref[...])) + bias_ref[...]
+    active = 0.5 * total * (1.0 + lax.erf(total * 0.7071067811865476))
+    outs[0][...], outs[1][...] = halves(active)
+
+
+def expand(high, low, bias, pieces, groups=None):
     depth, width = high.shape
-    units = pieces[0].shape[1]
+    units = bias.shape[0]
     tile = tile_of(width)
     normed = pl.BlockSpec((depth, tile), lambda n: (0, n))
     return pl.pallas_call(
@@ -358,34 +373,43 @@
         + [pl.BlockSpec(piece.shape, lambda n: (0, 0)) for piece in pieces],
         out_specs=[pl.BlockSpec((units, tile), lambda n: (0, n))] * 2,
         out_shape=[jax.ShapeDtypeStruct((units, width), jnp.bfloat16)] * 2,
-        scratch_shapes=[pltpu.VMEM((units, depth), jnp.bfloat16)] * 2,
+        scratch_shapes=[pltpu.VMEM((units, depth), jnp.bfloat16)] * (2 if groups else 0),
         compiler_params=pltpu.CompilerParams(vmem_limit_bytes=grant),
         cost_estimate=light,
         name="expand",
     )(high, low, bias, *pieces)
 
 
-def reduce_kernel(groups, count, first, spread, *refs):
+def reduce_kernel(orders, counts, first, spread, *refs):
     if spread:
         place_ref, refs = refs[0], refs[1:]
-    (high_ref, low_ref), pieces, refs = refs[:2], refs[2 : 2 + count], refs[2 + count :]
+    hidden, refs = refs[: 2 * len(counts)], refs[2 * len(counts) :]
+    pieces, refs = refs[: sum(counts)], refs[sum(counts) :]
     if not first:
         start_ref, refs = refs[0], refs[1:]
     if spread:
         mixed_ref, refs = refs[0], refs[1:]
     outs, (weight_high, weight_low) = refs[:-2], refs[-2:]
+    width = pieces[0].shape[1]
 
     @pl.when(pl.program_id(0) == 0)
     def _():
-        row = 0
-        for group in groups:
-            for piece, start, rows in group:
-                high, low = halves(pieces[piece][start : start + rows, :])
-                weight_high[row : row + rows, :] = high
-                weight_low[row : row + rows, :] = low
-                row += rows
-
-    total = three_pass((weight_high[...], weight_low[...]), (high_ref[...], low_ref[...]))
+        for chunk, groups in enumerate(orders):
+            offset, row = sum(counts[:chunk]), 0
+            columns = slice(chunk * width, (chunk + 1) * width)
+            for group in groups:
+                for piece, start, rows in group:
+                    high, low = halves(pieces[offset + piece][start : start + rows, :])
+                    weight_high[row : row + rows, columns] = high
+                    weight_low[row : row + rows, columns] = low
+                    row += rows
+
+    total = None
+    for chunk in range(len(counts)):
+        columns = slice(chunk * width, (chunk + 1) * width)
+        high_ref, low_ref = hidden[2 * chunk : 2 * chunk + 2]
+        term = three_pass((weight_high[:, columns], weight_low[:, columns]), (high_ref[...], low_ref[...]))
+        total = term if total is None else total + term
     if not first:
         total = start_ref[...] + total
     if not spread:
@@ -404,30 +428,33 @@
                 out_ref[pl.ds(row, rows), :] = value
 
 
-def reduce(high, low, pieces, groups, start, spread=None, place=None, mixed=None):
-    units, width = high.shape
-    rows = sum(piece.shape[0] for piece in pieces)
+def reduce(chunks, start=None, spread=None, place=None, mixed=None):
+    hidden = [half for chunk in chunks for half in chunk[0]]
+    pieces = [piece for chunk in chunks for piece in chunk[1]]
+    units, width = hidden[0].shape
+    rows = sum(piece.shape[0] for piece in chunks[0][1])
     tile = tile_of(width)
-    hidden = pl.BlockSpec((units, tile), lambda n, *_: (0, n))
     total = pl.BlockSpec((rows, tile), lambda n, *_: (0, n))
     first = start is None
     outs = spread[0].ch if spread else 1
     return pl.pallas_call(
-        functools.partial(reduce_kernel, groups, len(pieces), first, spread),
+        functools.partial(
+            reduce_kernel, [chunk[2] for chunk in chunks], [len(chunk[1]) for chunk in chunks], first, spread
+        ),
         grid_spec=pltpu.PrefetchScalarGridSpec(
             num_scalar_prefetch=1 if spread else 0,
             grid=(width // tile,),
-            in_specs=[hidden, hidden]
+            in_specs=[pl.BlockSpec((units, tile), lambda n, *_: (0, n))] * len(hidden)
             + [pl.BlockSpec(piece.shape, lambda n, *_: (0, 0)) for piece in pieces]
             + [total] * ((not first) + (mixed is not None)),
             out_specs=[pl.BlockSpec((rows // outs, tile), lambda n, *_: (0, n))] * outs,
-            scratch_shapes=[pltpu.VMEM((rows, units), jnp.bfloat16)] * 2,
+            scratch_shapes=[pltpu.VMEM((rows, len(chunks) * units), jnp.bfloat16)] * 2,
         ),
         out_shape=[jax.ShapeDtypeStruct((rows // outs, width), jnp.float32)] * outs,
         compiler_params=pltpu.CompilerParams(vmem_limit_bytes=grant),
         cost_estimate=light,
         name="reduce",
-    )(*([place] if spread else []), high, low, *pieces, *([] if first else [start]), *([mixed] if spread else []))
+    )(*([place] if spread else []), *hidden, *pieces, *([] if first else [start]), *([mixed] if spread else []))
 
 
 def finish_kernel(*refs):
@@ -450,6 +477,28 @@
         cost_estimate=light,
         name="finish",
     )(*values)
+
+
+def cut_kernel(in_ref, out_ref, own_ref, in_last, out_last):
+    rows, units = in_ref.shape[0], own_ref.shape[1]
+    own_ref[:rows, :], own_ref[rows:, :] = in_ref[:, :units], out_ref[:, :units]
+    in_last[...], out_last[...] = in_ref[:, units:], out_ref[:, units:]
+
+
+def cut(in_rows, out_rows, units):
+    rows, total = in_rows.shape
+    whole = pl.BlockSpec((rows, total), lambda n: (0, 0))
+    shapes = [(2 * rows, units)] + [(rows, total - units)] * 2
+    return pl.pallas_call(
+        cut_kernel,
+        grid=(1,),
+        in_specs=[whole, whole],
+        out_specs=[pl.BlockSpec(shape, lambda n: (0, 0)) for shape in shapes],
+        out_shape=[jax.ShapeDtypeStruct(shape, jnp.float32) for shape in shapes],
+        compiler_params=pltpu.CompilerParams(vmem_limit_bytes=grant),
+        cost_estimate=light,
+        name="cut",
+    )(in_rows, out_rows)
 
 
 def join(values, axis=0):
@@ -504,8 +553,7 @@
     others = [grid.to_core(fields, ch - step) for step in range(1, ch)]
     pair_gain = jnp.stack([gain_one, gain_two])
     gains = join([pair_gain] + [grid.to_core(pair_gain, ch - step) for step in range(1, ch)], 1).T
-    own = join([ch_in_weight[:, : ends[2]], out_rows[:, : ends[2]]])
-    in_last, out_last = ch_in_weight[:, ends[2] :], out_rows[:, ends[2] :]
+    own, in_last, out_last = cut(ch_in_weight, out_rows, ends[2])
     ring = [move(own, dz=1)]
     in_step, out_step = move(in_last, dx=1), move(out_last, dy=1)
     full, high, low = norm_one(grid, place, gains[:, :1], [fields] + others, per_core)
@@ -525,13 +573,13 @@
     sent_a, sent_b, kept_a, kept_b, in_last, out_last, ring[1], *biases = fence(
         sent_a, sent_b, kept_a, kept_b, in_last, out_last, ring[1], *biases
     )
-    kept_a, sent_a, kept_b, sent_b = halve([kept_a, sent_a, kept_b, sent_b])
-    sent_a, sent_b = move(sent_a, dy=1), move(sent_b, dx=1)
+    last_a, last_b = halve([kept_a, sent_a, kept_b, sent_b])
+    last_a, last_b = move(last_a, dy=1), move(last_b, dx=1)
     for _ in range(2, deep - 1):
         ring.append(move(ring[-1], dz=1))
-    sent_a, sent_b, ring[-1] = fence(sent_a, sent_b, ring[-1])
-
-    partial = merge([kept_a, sent_a, kept_b, sent_b], deep)
+    last_a, last_b, ring[-1] = fence(last_a, last_b, ring[-1])
+
+    partial = merge([kept_a, sent_a, last_a, kept_b, sent_b, last_b], deep)
     total = partial[deep - 1]
     for step in range(2, deep + 1):
         total = move(total, dz=1) + partial[deep - step]
@@ -547,35 +595,41 @@
         ring.append(move(ring[-1] if ring else activated, dz=1))
     step_a, step_b = got_x[:quarter], got_y[:quarter]
     first_step = [move(line_a, dy=1), move(step_a, dy=1), move(line_b, dx=1), move(step_b, dx=1)]
-    ring[-1], *first_step = fence(ring[-1], *first_step)
-    first = [[line_a, step_a, *first_step[:2]], [line_b, step_b, *first_step[2:]]]
+    span = tok_out_weight.shape[0]
+    out_high, out_low = prepare([tok_out_weight], [[(0, 0, span)]])
+    ring[-1], out_high, out_low, *first_step = fence(ring[-1], out_high, out_low, *first_step)
+    first = [
+        *prepare([line_a, step_a, *first_step[:2]], y_last),
+        *prepare([line_b, step_b, *first_step[2:]], x_last),
+    ]
 
     active_a, active_b = stack(grid.line(activated, ring), [(0, rows, 0, middle)], [(0, rows, middle, 2 * middle)])
     lower = quarter, 2 * quarter, 0, ends[1]
     second = [stack([pack_y, got_y], [lower])[0], stack([pack_x, got_x], [lower])[0]]
     arrived = [move(active_a, dy=1), move(active_a, dx=1), move(active_b, dx=1), move(active_b, dy=1)]
     in_ring.append(move(in_ring[0], dz=1))
-    in_ring[1], second[0], second[1], *arrived = fence(in_ring[1], *second, *arrived)
+    in_ring[1], *fenced = fence(in_ring[1], *second, *first, *arrived)
+    second, first, arrived = fenced[:2], (fenced[2:4], fenced[4:6]), fenced[6:]
     last_a, last_b = move(arrived[0], dx=1), move(arrived[2], dy=1)
     for _ in range(2, deep - 1):
         in_ring.append(move(in_ring[-1], dz=1))
-    most = project(tok_out_weight, [active_a, *arrived[:2], active_b, *arrived[2:]], (0, 2, 1, 0, 1, 2))
+    most = project(out_high, out_low, [active_a, *arrived[:2], active_b, *arrived[2:]], (0, 2, 1, 0, 1, 2))
     last_a, last_b, in_ring[-1], most = fence(last_a, last_b, in_ring[-1], most)
 
     second_step = [move(second[0], dx=1), move(second[1], dy=1)]
     out_ring = [move(out_last, dz=1)]
     most = [most] + [grid.to_core(most, step) for step in range(1, ch)]
-    least = project(tok_out_weight, [last_a, last_b], (0, 0))
+    least = project(out_high, out_low, [last_a, last_b], (0, 0))
     least = [least] + [grid.to_core(least, step) for step in range(1, ch)]
     terms = [part for pair in zip(most, least) for part in pair]
     mixed, high, low = norm_two(grid, place, gains[:, 1:], full, terms, 2, per_core)
 
-    hidden = [expand(high, low, biases[0], first[0], y_last)]
+    hidden = [expand(high, low, biases[0], first[0])]
     hidden_high, out_ring[0] = fence(hidden[0][0], out_ring[0])
     hidden[0] = hidden_high, hidden[0][1]
     out_ring.append(move(out_ring[0], dz=1))
     hidden += [
-        expand(high, low, biases[1], first[1], x_last),
+        expand(high, low, biases[1], first[1]),
         expand(high, low, biases[2], grid.line(in_last, in_ring), z_after_xy),
     ]
     fenced = fence(hidden[1][0], hidden[2][0], out_ring[1], *second_step)
@@ -583,10 +637,14 @@
     out_ring[1], *second_step = fenced[2:]
     for _ in range(2, deep - 1):
         out_ring.append(move(out_ring[-1], dz=1))
-    (result,) = reduce(*hidden[0], [second[0], second_step[0]], x_last_pair, None)
-    (result,) = reduce(*hidden[1], [second[1], second_step[1]], y_last_pair, result)
+    (result,) = reduce(
+        [
+            (hidden[0], [second[0], second_step[0]], x_last_pair),
+            (hidden[1], [second[1], second_step[1]], y_last_pair),
+        ]
+    )
     spread = grid, rows, per_core
-    parts = reduce(*hidden[2], grid.line(out_last, out_ring), z_after_yx, result, spread, place, mixed)
+    parts = reduce([(hidden[2], grid.line(out_last, out_ring), z_after_yx)], result, spread, place, mixed)
     return finish([parts[0]] + [grid.to_core(part, step) for step, part in enumerate(parts) if step])
 
 

time: 377 us -> 371 us (0.984)
  waiting for transfers between devices: 150 us -> 137 us
  Pallas kernels: 166 us -> 177 us
  local copies, waits for them, and re-layouts: 13.7 us -> 9.92 us
    pallas_call x4 -> x7, Pallas kernels: 40.7 us -> 58.8 us  [the longest x2 34.4 us: reduce(): pl.pallas_call(functools.partial(reduce_kernel, [chunk[2] for chunk in ch...]
    ppermute x37, waiting for transfers between devices: 144 us -> 132 us  [move(): return lax.ppermute(value, 'tok', pairs)]
    slice x5 -> x0, local copies, waits for them, and re-layouts: 4.4 us -> none  [the longest x2 3.32 us: shards(): in_last, out_last = (ch_in_weight[:, ends[2]:], out_rows[:, ends[2]:])]
    pallas_call x3, Pallas kernels: 39.6 us -> 35.4 us  [expand(): pl.pallas_call(functools.partial(expand_kernel, groups, len(pieces)), gri...]
    concatenate x5 -> x4, other arithmetic: 7.93 us -> 7.67 us  [join(): return jnp.concatenate(list(values), axis=axis)]
  transfers between devices with their start and end apart: 42 -> 42, of which waited for: 22 -> 20; matrix products, arithmetic and copies ran while one was open for 6% -> 6% of each run, Pallas kernels for 38% -> 41%
where the time goes in v3:
time: 371 us; the launch traced here: 370 us
  Pallas kernels  177 us (48%)
  waiting for transfers between devices  137 us (37%)
  starting transfers between devices  33.9 us (9%)
  other arithmetic  12.7 us (3%)
  local copies, waits for them, and re-layouts  9.92 us (3%)
    ppermute x37, waiting for transfers between devices, move(): return lax.ppermute(value, 'tok', pairs)  132 us
    pallas_call x3, Pallas kernels, expand(): pl.pallas_call(functools.partial(expand_kernel, groups, len(pieces)), gri...  35.4 us
    pallas_call x2, Pallas kernels, reduce(): pl.pallas_call(functools.partial(reduce_kernel, [chunk[2] for chunk in ch...  34.4 us
    ppermute x37, starting transfers between devices, move(): return lax.ppermute(value, 'tok', pairs)  32.9 us
    pallas_call x2, Pallas kernels, mix(): pl.pallas_call(functools.partial(mix_kernel, steps), grid=(2 * steps,), i...  21.8 us
    pallas_call x2, Pallas kernels, project(): pl.pallas_call(functools.partial(project_kernel, rows, places), grid=(wid...  19.4 us
    pallas_call x3, Pallas kernels, prepare(): pl.pallas_call(functools.partial(prepare_kernel, groups, len(pieces)), gr...  18.3 us
    pallas_call x4, Pallas kernels, stack(): pl.pallas_call(functools.partial(stack_kernel, len(values), outs), grid=(...  15 us
  transfers between devices with their start and end apart: 42, of which 20 were waited for; matrix products, arithmetic and copies ran while one was open for 6% of the time, Pallas kernels for 41%

profile of v3, /device:TPU:0, one launch (start us, length us, event | category | flops | bytes accessed | tf_op | source)
XLA Modules:
  0.0 369.9 jit_solution(11597614255505728767)
XLA Ops:
  12.5 8.0 %norm_one.1 = (f32[1024,1024]{1,0:T(8,128)}, bf16[1024,1024]{1,0:T(8,128)(2,1)}, bf16[1024,1024]{1,0:T(8,128)(2,1)}) custom-call(s32[4]{0:T(128)} %pad_add_fusion.place_ref.refs_0_, f32[1024,1]{1,0:T(8,128)} %get-tuple-element.195.gain_ref, f32[1024,512]{1,0:T(8,128)} %refs_0_.2, f32[1024,512]{1,0:T(8,128)} %collective-permute-done.1.refs_1_), custom_call_target="tpu_custom_call" | custom-call | tf_op jit(solution)/shard_map/norm_one/pallas_call | solution.py:123
  25.4 10.9 %mix.2 = (f32[512,768]{1,0:T(8,128)}, f32[512,768]{1,0:T(8,128)}) custom-call(bf16[1024,1024]{1,0:T(8,128)(2,1)} %get-tuple-element.104.high_one.high_two, bf16[1024,1024]{1,0:T(8,128)(2,1)} %get-tuple-element.104.high_one.high_two, bf16[1024,1024]{1,0:T(8,128)(2,1)} %get-tuple-element.105.low_one.low_two, ...), custom_call_target="tpu_custom_call" | custom-call | tf_op jit(solution)/shard_map/mix/pallas_call | solution.py:166
  44.6 10.8 %mix.3 = (f32[512,768]{1,0:T(8,128)}, f32[512,768]{1,0:T(8,128)}) custom-call(bf16[1024,1024]{1,0:T(8,128)(2,1)} %get-tuple-element.104.high_one.high_two, bf16[1024,1024]{1,0:T(8,128)(2,1)} %get-tuple-element.104.high_one.high_two, bf16[1024,1024]{1,0:T(8,128)(2,1)} %get-tuple-element.105.low_one.low_two, ...), custom_call_target="tpu_custom_call" | custom-call | tf_op jit(solution)/shard_map/mix/pallas_call | solution.py:166
  58.7 6.0 %collective-permute-done.9.refs_6_ = f32[128,2048]{1,0:T(8,128)} collective-permute-done((f32[128,2048]{1,0:T(8,128)}, f32[128,2048]{1,0:T(8,128)}, u32[]{:S(2)}, u32[]{:S(2)}) %collective-permute-start.9) | collective-permute-done | bytes 1048608 | tf_op jit(solution)/shard_map/ppermute | solution.py:74
  64.7 7.8 %collective-permute-done.7.refs_0_ = f32[512,768]{1,0:T(8,128)} collective-permute-done((f32[512,768]{1,0:T(8,128)}, f32[512,768]{1,0:T(8,128)}, u32[]{:S(2)}, u32[]{:S(2)}) %collective-permute-start.7) | collective-permute-done | bytes 1572896 | tf_op jit(solution)/shard_map/ppermute | solution.py:74
  74.4 3.8 %halve.1 = (f32[256,768]{1,0:T(8,128)}, f32[256,768]{1,0:T(8,128)}) custom-call(f32[512,768]{1,0:T(8,128)} %get-tuple-element.118.kept_a.refs_0_, f32[512,768]{1,0:T(8,128)} %get-tuple-element.119.sent_a.refs_1_, f32[512,768]{1,0:T(8,128)} %get-tuple-element.120.kept_b.refs_3_, f32[512,768]{1,0:T(8,128)} %get-tuple-element.121.sent_b.refs_4_), custom_call_target="tpu_custom_call" | custom-call | tf_op jit(solution)/shard_map/halve/pallas_call | solution.py:214
  81.1 13.5 %collective-permute-done.10.refs_0_ = f32[256,768]{1,0:T(8,128)} collective-permute-done((f32[256,768]{1,0:T(8,128)}, f32[256,768]{1,0:T(8,128)}, u32[]{:S(2)}, u32[]{:S(2)}) %collective-permute-start.10) | collective-permute-done | bytes 786464 | tf_op jit(solution)/shard_map/ppermute | solution.py:74
  96.9 5.0 %stack.36 = (f32[512,1024]{1,0:T(8,128)}, f32[512,1024]{1,0:T(8,128)}, f32[256,1024]{1,0:T(8,128)}, f32[256,1024]{1,0:T(8,128)}) custom-call(f32[128,2048]{1,0:T(8,128)} %get-tuple-element.108.refs_0_, f32[128,2048]{1,0:T(8,128)} %get-tuple-element.131.refs_1_, f32[128,2048]{1,0:T(8,128)} %get-tuple-element.124.refs_2_, f32[128,2048]{1,0:T(8,128)} %get-tuple-element.117.refs_3_), custom_call_target="tpu_custom_call" | custom-call | tf_op jit(solution)/shard_map/stack/pallas_call | solution.py:194
  108.2 10.1 %collective-permute-done.13 = f32[64,1536]{1,0:T(8,128)S(1)} collective-permute-done((f32[64,1536]{1,0:T(8,128)}, f32[64,1536]{1,0:T(8,128)S(1)}, u32[]{:S(2)}, u32[]{:S(2)}) %collective-permute-start.13) | collective-permute-done | bytes 393248 | tf_op jit(solution)/shard_map/ppermute | solution.py:74
  120.3 12.9 %collective-permute-done.14 = f32[64,1536]{1,0:T(8,128)S(1)} collective-permute-done((f32[64,1536]{1,0:T(8,128)S(1)}, f32[64,1536]{1,0:T(8,128)S(1)}, u32[]{:S(2)}, u32[]{:S(2)}) %collective-permute-start.14) | collective-permute-done | bytes 393248 | tf_op jit(solution)/shard_map/ppermute | solution.py:74
  134.4 22.9 %collective-permute-done.15 = f32[64,1536]{1,0:T(8,128)S(1)} collective-permute-done((f32[64,1536]{1,0:T(8,128)S(1)}, f32[64,1536]{1,0:T(8,128)S(1)}, u32[]{:S(2)}, u32[]{:S(2)}) %collective-permute-start.15) | collective-permute-done | bytes 393248 | tf_op jit(solution)/shard_map/ppermute | solution.py:74
  167.8 4.4 %collective-permute-done.20.refs_3_ = f32[64,1536]{1,0:T(8,128)S(1)} collective-permute-done((f32[64,1536]{1,0:T(8,128)}, f32[64,1536]{1,0:T(8,128)S(1)}, u32[]{:S(2)}, u32[]{:S(2)}) %collective-permute-start.20) | collective-permute-done | bytes 393248 | tf_op jit(solution)/shard_map/ppermute | solution.py:74
  172.9 13.9 %collective-permute-done.21.refs_2_ = f32[64,1536]{1,0:T(8,128)} collective-permute-done((f32[64,1536]{1,0:T(8,128)S(1)}, f32[64,1536]{1,0:T(8,128)}, u32[]{:S(2)}, u32[]{:S(2)}) %collective-permute-start.21) | collective-permute-done | bytes 393248 | tf_op jit(solution)/shard_map/ppermute | solution.py:74
  186.8 7.3 %prepare.3 = (bf16[1536,1024]{1,0:T(8,128)(2,1)}, bf16[1536,1024]{1,0:T(8,128)(2,1)}) custom-call(f32[1024,1536]{1,0:T(8,128)} %refs_0_.3), custom_call_target="tpu_custom_call" | custom-call | tf_op jit(solution)/shard_map/prepare/pallas_call | solution.py:337
  194.1 6.1 %collective-permute-done.24.refs_4_ = f32[256,1024]{1,0:T(8,128)} collective-permute-done((f32[256,1024]{1,0:T(8,128)}, f32[256,1024]{1,0:T(8,128)}, u32[]{:S(2)}, u32[]{:S(2)}) %collective-permute-start.24) | collective-permute-done | bytes 1048608 | tf_op jit(solution)/shard_map/ppermute | solution.py:74
  200.3 6.1 %collective-permute-done.26.refs_6_ = f32[256,1024]{1,0:T(8,128)} collective-permute-done((f32[256,1024]{1,0:T(8,128)}, f32[256,1024]{1,0:T(8,128)}, u32[]{:S(2)}, u32[]{:S(2)}) %collective-permute-start.26) | collective-permute-done | bytes 1048608 | tf_op jit(solution)/shard_map/ppermute | solution.py:74
  213.0 3.8 %stack.37.refs_1_ = f32[512,1024]{1,0:T(8,128)} custom-call(f32[512,1024]{1,0:T(8,128)} %get-tuple-element.135.refs_0_, f32[512,1024]{1,0:T(8,128)} %get-tuple-element.138.refs_1_), custom_call_target="tpu_custom_call" | custom-call | tf_op jit(solution)/shard_map/stack/pallas_call | solution.py:194
  216.8 3.6 stack.38.refs_2_
  220.5 5.5 %prepare.4 = (bf16[1024,1024]{1,0:T(8,128)(2,1)}, bf16[1024,1024]{1,0:T(8,128)(2,1)}) custom-call(f32[256,1024]{1,0:T(8,128)} %get-tuple-element.140.refs_0_, f32[256,1024]{1,0:T(8,128)} %slice.26.refs_1_, f32[256,1024]{1,0:T(8,128)} %get-tuple-element.145.refs_2_, f32[256,1024]{1,0:T(8,128)} %get-tuple-element.146.refs_3_), custom_call_target="tpu_custom_call" | custom-call | tf_op jit(solution)/shard_map/prepare/pallas_call | solution.py:337
  225.9 5.5 %prepare.5 = (bf16[1024,1024]{1,0:T(8,128)(2,1)}, bf16[1024,1024]{1,0:T(8,128)(2,1)}) custom-call(f32[256,1024]{1,0:T(8,128)} %get-tuple-element.144.refs_0_, f32[256,1024]{1,0:T(8,128)} %slice.27.refs_1_, f32[256,1024]{1,0:T(8,128)} %get-tuple-element.149.refs_2_, f32[256,1024]{1,0:T(8,128)} %get-tuple-element.150.refs_3_), custom_call_target="tpu_custom_call" | custom-call | tf_op jit(solution)/shard_map/prepare/pallas_call | solution.py:337
  231.5 12.0 %collective-permute-done.29.refs_9_ = f32[256,768]{1,0:T(8,128)} collective-permute-done((f32[256,768]{1,0:T(8,128)}, f32[256,768]{1,0:T(8,128)}, u32[]{:S(2)}, u32[]{:S(2)}) %collective-permute-start.29) | collective-permute-done | bytes 786464 | tf_op jit(solution)/shard_map/ppermute | solution.py:74
  246.3 12.5 %project.2.refs_3_ = f32[768,1024]{1,0:T(8,128)} custom-call(bf16[1536,1024]{1,0:T(8,128)(2,1)} %get-tuple-element.159.high, bf16[1536,1024]{1,0:T(8,128)(2,1)} %get-tuple-element.160.low, f32[256,768]{1,0:T(8,128)} %get-tuple-element.154.refs_0_, f32[256,768]{1,0:T(8,128)} %get-tuple-element.156.refs_1_, f32[256,768]{1,0:T(8,128)} %get-tuple-element.161.refs_2_, ...), custom_call_target="tpu_custom_call" | custom-call | tf_op jit(solution)/shard_map/project/pallas_call | solution.py:277
  260.4 6.9 %project.3.refs_1_ = f32[256,1024]{1,0:T(8,128)} custom-call(bf16[1536,1024]{1,0:T(8,128)(2,1)} %get-tuple-element.159.high, bf16[1536,1024]{1,0:T(8,128)(2,1)} %get-tuple-element.160.low, f32[256,768]{1,0:T(8,128)} %get-tuple-element.164.refs_0_, f32[256,768]{1,0:T(8,128)} %get-tuple-element.165.refs_1_), custom_call_target="tpu_custom_call" | custom-call | tf_op jit(solution)/shard_map/project/pallas_call | solution.py:277
  270.6 10.0 %norm_two.1 = (f32[1024,1024]{1,0:T(8,128)}, bf16[1024,1024]{1,0:T(8,128)(2,1)}, bf16[1024,1024]{1,0:T(8,128)(2,1)}) custom-call(s32[4]{0:T(128)} %pad_add_fusion.place_ref.refs_0_, f32[1024,1]{1,0:T(8,128)} %get-tuple-element.196.gain_ref, f32[1024,1024]{1,0:T(8,128)} %get-tuple-element.100.fields_ref, f32[768,1024]{1,0:T(8,128)} %get-tuple-element.163.refs_0_, ...), custom_call_target="tpu_custom_call" | custom-call | tf_op jit(solution)/shard_map/norm_two/pallas_call | solution.py:307
  280.5 11.4 %expand.5 = (bf16[1024,1024]{1,0:T(8,128)(2,1)}, bf16[1024,1024]{1,0:T(8,128)(2,1)}) custom-call(bf16[1024,1024]{1,0:T(8,128)(2,1)} %get-tuple-element.166.high_ref, bf16[1024,1024]{1,0:T(8,128)(2,1)} %get-tuple-element.167.low_ref, f32[1024,1]{1,0:T(8,128)} %get-tuple-element.175.bias_ref, bf16[1024,1024]{1,0:T(8,128)(2,1)} %get-tuple-element.176.refs_0_, ...), custom_call_target="tpu_custom_call" | custom-call | tf_op jit(solution)/shard_map/expand/pallas_call | solution.py:369
  294.9 12.7 %expand.4 = (bf16[1024,1024]{1,0:T(8,128)(2,1)}, bf16[1024,1024]{1,0:T(8,128)(2,1)}) custom-call(bf16[1024,1024]{1,0:T(8,128)(2,1)} %get-tuple-element.166.high_ref, bf16[1024,1024]{1,0:T(8,128)(2,1)} %get-tuple-element.167.low_ref, f32[1024,1]{1,0:T(8,128)} %get-tuple-element.172.bias_ref, f32[256,1024]{1,0:T(8,128)} %get-tuple-element.136.refs_0_, ...), custom_call_target="tpu_custom_call" | custom-call | tf_op jit(solution)/shard_map/expand/pallas_call | solution.py:369
  307.6 11.3 %expand.3 = (bf16[1024,1024]{1,0:T(8,128)(2,1)}, bf16[1024,1024]{1,0:T(8,128)(2,1)}) custom-call(bf16[1024,1024]{1,0:T(8,128)(2,1)} %get-tuple-element.166.high_ref, bf16[1024,1024]{1,0:T(8,128)(2,1)} %get-tuple-element.167.low_ref, f32[1024,1]{1,0:T(8,128)} %get-tuple-element.168.bias_ref, bf16[1024,1024]{1,0:T(8,128)(2,1)} %get-tuple-element.169.refs_0_, ...), custom_call_target="tpu_custom_call" | custom-call | tf_op jit(solution)/shard_map/expand/pallas_call | solution.py:369
  321.3 20.2 %reduce.2.refs_7_ = f32[1024,1024]{1,0:T(8,128)} custom-call(bf16[1024,1024]{1,0:T(8,128)(2,1)} %get-tuple-element.186.refs_0_, bf16[1024,1024]{1,0:T(8,128)(2,1)} %get-tuple-element.187.refs_1_, bf16[1024,1024]{1,0:T(8,128)(2,1)} %get-tuple-element.188.refs_2_, bf16[1024,1024]{1,0:T(8,128)(2,1)} %get-tuple-element.189.refs_3_, ...), custom_call_target="tpu_custom_call" | custom-call | tf_op jit(solution)/shard_map/reduce/pallas_call | solution.py:440
  341.5 5.2 %collective-permute-done.40.refs_4_ = f32[256,1024]{1,0:T(8,128)} collective-permute-done((f32[256,1024]{1,0:T(8,128)}, f32[256,1024]{1,0:T(8,128)}, u32[]{:S(2)}, u32[]{:S(2)}) %collective-permute-start.40) | collective-permute-done | bytes 1048608 | tf_op jit(solution)/shard_map/ppermute | solution.py:74
  346.7 14.2 %reduce.3 = (f32[512,1024]{1,0:T(8,128)}, f32[512,1024]{1,0:T(8,128)}) custom-call(s32[4]{0:T(128)} %pad_add_fusion.place_ref.refs_0_, bf16[1024,1024]{1,0:T(8,128)(2,1)} %get-tuple-element.183.refs_1_, bf16[1024,1024]{1,0:T(8,128)(2,1)} %get-tuple-element.184.refs_2_, f32[256,1024]{1,0:T(8,128)} %get-tuple-element.179.refs_3_, ...), custom_call_target="tpu_custom_call" | custom-call | tf_op jit(solution)/shard_map/reduce/pallas_call | solution.py:440
  361.0 4.5 %collective-permute-done.41.refs_1_ = f32[512,1024]{1,0:T(8,128)} collective-permute-done((f32[512,1024]{1,0:T(8,128)}, f32[512,1024]{1,0:T(8,128)}, u32[]{:S(2)}, u32[]{:S(2)}) %collective-permute-start.41) | collective-permute-done | bytes 2097184 | tf_op jit(solution)/shard_map/ppermute | solution.py:77
  365.4 4.5 %finish.1 = f32[1024,512]{1,0:T(8,128)} custom-call(f32[512,1024]{1,0:T(8,128)} %get-tuple-element.193.refs_0_, f32[512,1024]{1,0:T(8,128)} %collective-permute-done.41.refs_1_), custom_call_target="tpu_custom_call" | custom-call | tf_op jit(solution)/shard_map/finish/pallas_call | solution.py:470
  (109 shorter events, 76.5 us)
Async XLA Ops:
  3.8 16.7 %collective-permute-start.2 = (f32[64,1024]{1,0:T(8,128)}, f32[64,1024]{1,0:T(8,128)}, u32[]{:S(2)}, u32[]{:S(2)}) collective-permute-start(f32[64,1024]{1,0:T(8,128)} %get-tuple-element.102), channel_id=1, source_target_pairs={{0,2},{2,0},{4,6},{6,4},{8,10},{10,8},{12,14},{14,12},{16,18},{18,... | collective-permute-start | bytes 786440 | tf_op jit(solution)/shard_map/ppermute | solution.py:74
  8.3 28.0 %collective-permute-start.4 = (f32[128,2048]{1,0:T(8,128)}, f32[128,2048]{1,0:T(8,128)}, u32[]{:S(2)}, u32[]{:S(2)}) collective-permute-start(f32[128,2048]{1,0:T(8,128)} %get-tuple-element.108.refs_0_), channel_id=1, source_target_pairs={{0,8},{2,10},{4,12},{6,14},{8,16},{10,18},{12,20},{14,22},{16,24},... | collective-permute-start | bytes 3145736 | tf_op jit(solution)/shard_map/ppermute | solution.py:74
  37.9 34.6 %collective-permute-start.7 = (f32[512,768]{1,0:T(8,128)}, f32[512,768]{1,0:T(8,128)}, u32[]{:S(2)}, u32[]{:S(2)}) collective-permute-start(f32[512,768]{1,0:T(8,128)} %get-tuple-element.111), channel_id=1, source_target_pairs={{0,2},{2,0},{4,6},{6,4},{8,10},{10,8},{12,14},{14,12},{16,18},{18,... | collective-permute-start | bytes 4718600 | tf_op jit(solution)/shard_map/ppermute | solution.py:74
  38.4 34.4 %collective-permute-start.8 = (f32[512,768]{1,0:T(8,128)}, f32[512,768]{1,0:T(8,128)}, u32[]{:S(2)}, u32[]{:S(2)}) collective-permute-start(f32[512,768]{1,0:T(8,128)} %get-tuple-element.112), channel_id=1, source_target_pairs={{0,4},{2,6},{4,0},{6,2},{8,12},{10,14},{12,8},{14,10},{16,20},{18,... | collective-permute-start | bytes 4718600 | tf_op jit(solution)/shard_map/ppermute | solution.py:74
  39.9 24.7 %collective-permute-start.9 = (f32[128,2048]{1,0:T(8,128)}, f32[128,2048]{1,0:T(8,128)}, u32[]{:S(2)}, u32[]{:S(2)}) collective-permute-start(f32[128,2048]{1,0:T(8,128)} %get-tuple-element.117.refs_3_), channel_id=1, source_target_pairs={{0,8},{2,10},{4,12},{6,14},{8,16},{10,18},{12,20},{14,22},{16,24},... | collective-permute-start | bytes 3145736 | tf_op jit(solution)/shard_map/ppermute | solution.py:74
  72.9 24.1 %collective-permute-start.12 = (f32[128,2048]{1,0:T(8,128)}, f32[128,2048]{1,0:T(8,128)}, u32[]{:S(2)}, u32[]{:S(2)}) collective-permute-start(f32[128,2048]{1,0:T(8,128)} %get-tuple-element.124.refs_2_), channel_id=1, source_target_pairs={{0,8},{2,10},{4,12},{6,14},{8,16},{10,18},{12,20},{14,22},{16,24},... | collective-permute-start | bytes 3145736 | tf_op jit(solution)/shard_map/ppermute | solution.py:74
  78.2 16.4 %collective-permute-start.10 = (f32[256,768]{1,0:T(8,128)}, f32[256,768]{1,0:T(8,128)}, u32[]{:S(2)}, u32[]{:S(2)}) collective-permute-start(f32[256,768]{1,0:T(8,128)} %get-tuple-element.122), channel_id=1, source_target_pairs={{0,4},{2,6},{4,0},{6,2},{8,12},{10,14},{12,8},{14,10},{16,20},{18,... | collective-permute-start | bytes 2359304 | tf_op jit(solution)/shard_map/ppermute | solution.py:74
  79.7 16.1 %collective-permute-start.11 = (f32[256,768]{1,0:T(8,128)}, f32[256,768]{1,0:T(8,128)}, u32[]{:S(2)}, u32[]{:S(2)}) collective-permute-start(f32[256,768]{1,0:T(8,128)} %get-tuple-element.123), channel_id=1, source_target_pairs={{0,2},{2,0},{4,6},{6,4},{8,10},{10,8},{12,14},{14,12},{16,18},{18,... | collective-permute-start | bytes 2359304 | tf_op jit(solution)/shard_map/ppermute | solution.py:74
  101.9 57.1 %collective-permute-start.16 = (f32[512,1024]{1,0:T(8,128)}, f32[512,1024]{1,0:T(8,128)}, u32[]{:S(2)}, u32[]{:S(2)}) collective-permute-start(f32[512,1024]{1,0:T(8,128)} %get-tuple-element.134.refs_0_), channel_id=1, source_target_pairs={{0,2},{2,0},{4,6},{6,4},{8,10},{10,8},{12,14},{14,12},{16,18},{18,... | collective-permute-start | bytes 6291464 | tf_op jit(solution)/shard_map/ppermute | solution.py:74
  103.1 55.8 %collective-permute-start.17 = (f32[512,1024]{1,0:T(8,128)}, f32[512,1024]{1,0:T(8,128)}, u32[]{:S(2)}, u32[]{:S(2)}) collective-permute-start(f32[512,1024]{1,0:T(8,128)} %get-tuple-element.135.refs_0_), channel_id=1, source_target_pairs={{0,4},{2,6},{4,0},{6,2},{8,12},{10,14},{12,8},{14,10},{16,20},{18,... | collective-permute-start | bytes 6291464 | tf_op jit(solution)/shard_map/ppermute | solution.py:74
  119.3 13.9 %collective-permute-start.14 = (f32[64,1536]{1,0:T(8,128)S(1)}, f32[64,1536]{1,0:T(8,128)S(1)}, u32[]{:S(2)}, u32[]{:S(2)}) collective-permute-start(f32[64,1536]{1,0:T(8,128)S(1)} %add.28), channel_id=1, source_target_pairs={{0,8},{2,10},{4,12},{6,14},{8,16},{10,18},{12,20},{14,22},{16,24},... | collective-permute-start | bytes 1179656 | tf_op jit(solution)/shard_map/ppermute | solution.py:74
  119.4 39.6 %collective-permute-start.18 = (f32[256,1024]{1,0:T(8,128)}, f32[256,1024]{1,0:T(8,128)}, u32[]{:S(2)}, u32[]{:S(2)}) collective-permute-start(f32[256,1024]{1,0:T(8,128)} %get-tuple-element.136.refs_0_), channel_id=1, source_target_pairs={{0,8},{2,10},{4,12},{6,14},{8,16},{10,18},{12,20},{14,22},{16,24},... | collective-permute-start | bytes 3145736 | tf_op jit(solution)/shard_map/ppermute | solution.py:74
  134.3 23.0 %collective-permute-start.15 = (f32[64,1536]{1,0:T(8,128)S(1)}, f32[64,1536]{1,0:T(8,128)S(1)}, u32[]{:S(2)}, u32[]{:S(2)}) collective-permute-start(f32[64,1536]{1,0:T(8,128)S(1)} %add.29), channel_id=1, source_target_pairs={{0,8},{2,10},{4,12},{6,14},{8,16},{10,18},{12,20},{14,22},{16,24},... | collective-permute-start | bytes 1179656 | tf_op jit(solution)/shard_map/ppermute | solution.py:74
  159.0 27.8 %collective-permute-start.23 = (f32[256,1024]{1,0:T(8,128)}, f32[256,1024]{1,0:T(8,128)}, u32[]{:S(2)}, u32[]{:S(2)}) collective-permute-start(f32[256,1024]{1,0:T(8,128)} %get-tuple-element.140.refs_0_), channel_id=1, source_target_pairs={{0,4},{2,6},{4,0},{6,2},{8,12},{10,14},{12,8},{14,10},{16,20},{18,... | collective-permute-start | bytes 3145736 | tf_op jit(solution)/shard_map/ppermute | solution.py:74
  161.9 38.4 %collective-permute-start.24 = (f32[256,1024]{1,0:T(8,128)}, f32[256,1024]{1,0:T(8,128)}, u32[]{:S(2)}, u32[]{:S(2)}) collective-permute-start(f32[256,1024]{1,0:T(8,128)} %slice.26.refs_1_), channel_id=1, source_target_pairs={{0,4},{2,6},{4,0},{6,2},{8,12},{10,14},{12,8},{14,10},{16,20},{18,... | collective-permute-start | bytes 3145736 | tf_op jit(solution)/shard_map/ppermute | solution.py:74
  163.4 36.9 %collective-permute-start.25 = (f32[256,1024]{1,0:T(8,128)}, f32[256,1024]{1,0:T(8,128)}, u32[]{:S(2)}, u32[]{:S(2)}) collective-permute-start(f32[256,1024]{1,0:T(8,128)} %get-tuple-element.144.refs_0_), channel_id=1, source_target_pairs={{0,2},{2,0},{4,6},{6,4},{8,10},{10,8},{12,14},{14,12},{16,18},{18,... | collective-permute-start | bytes 3145736 | tf_op jit(solution)/shard_map/ppermute | solution.py:74
  166.5 39.9 %collective-permute-start.26 = (f32[256,1024]{1,0:T(8,128)}, f32[256,1024]{1,0:T(8,128)}, u32[]{:S(2)}, u32[]{:S(2)}) collective-permute-start(f32[256,1024]{1,0:T(8,128)} %slice.27.refs_1_), channel_id=1, source_target_pairs={{0,2},{2,0},{4,6},{6,4},{8,10},{10,8},{12,14},{14,12},{16,18},{18,... | collective-permute-start | bytes 3145736 | tf_op jit(solution)/shard_map/ppermute | solution.py:74
  172.9 13.9 %collective-permute-start.21 = (f32[64,1536]{1,0:T(8,128)S(1)}, f32[64,1536]{1,0:T(8,128)}, u32[]{:S(2)}, u32[]{:S(2)}) collective-permute-start(f32[64,1536]{1,0:T(8,128)S(1)} %collective-permute-done.20.refs_3_), channel_id=1, source_target_pairs={{0,8},{2,10},{4,12},{6,14},{8,16},{10,18},{12,20},{14,22},{16,24},... | collective-permute-start | bytes 1179656 | tf_op jit(solution)/shard_map/ppermute | solution.py:74
  186.8 19.6 %collective-permute-start.22 = (f32[64,1536]{1,0:T(8,128)}, f32[64,1536]{1,0:T(8,128)}, u32[]{:S(2)}, u32[]{:S(2)}) collective-permute-start(f32[64,1536]{1,0:T(8,128)} %collective-permute-done.21.refs_2_), channel_id=1, source_target_pairs={{0,8},{2,10},{4,12},{6,14},{8,16},{10,18},{12,20},{14,22},{16,24},... | collective-permute-start | bytes 1179656 | tf_op jit(solution)/shard_map/ppermute | solution.py:74
  186.8 44.7 %collective-permute-start.19 = (f32[256,1024]{1,0:T(8,128)}, f32[256,1024]{1,0:T(8,128)}, u32[]{:S(2)}, u32[]{:S(2)}) collective-permute-start(f32[256,1024]{1,0:T(8,128)} %get-tuple-element.137.refs_3_), channel_id=1, source_target_pairs={{0,8},{2,10},{4,12},{6,14},{8,16},{10,18},{12,20},{14,22},{16,24},... | collective-permute-start | bytes 3145736 | tf_op jit(solution)/shard_map/ppermute | solution.py:74
  209.0 22.5 %collective-permute-start.27 = (f32[256,768]{1,0:T(8,128)}, f32[256,768]{1,0:T(8,128)}, u32[]{:S(2)}, u32[]{:S(2)}) collective-permute-start(f32[256,768]{1,0:T(8,128)} %get-tuple-element.154.refs_0_), channel_id=1, source_target_pairs={{0,4},{2,6},{4,0},{6,2},{8,12},{10,14},{12,8},{14,10},{16,20},{18,... | collective-permute-start | bytes 2359304 | tf_op jit(solution)/shard_map/ppermute | solution.py:74
  209.0 22.5 %collective-permute-start.28 = (f32[256,768]{1,0:T(8,128)}, f32[256,768]{1,0:T(8,128)}, u32[]{:S(2)}, u32[]{:S(2)}) collective-permute-start(f32[256,768]{1,0:T(8,128)} %get-tuple-element.154.refs_0_), channel_id=1, source_target_pairs={{0,2},{2,0},{4,6},{6,4},{8,10},{10,8},{12,14},{14,12},{16,18},{18,... | collective-permute-start | bytes 2359304 | tf_op jit(solution)/shard_map/ppermute | solution.py:74
  209.8 33.7 %collective-permute-start.29 = (f32[256,768]{1,0:T(8,128)}, f32[256,768]{1,0:T(8,128)}, u32[]{:S(2)}, u32[]{:S(2)}) collective-permute-start(f32[256,768]{1,0:T(8,128)} %get-tuple-element.155.refs_3_), channel_id=1, source_target_pairs={{0,2},{2,0},{4,6},{6,4},{8,10},{10,8},{12,14},{14,12},{16,18},{18,... | collective-permute-start | bytes 2359304 | tf_op jit(solution)/shard_map/ppermute | solution.py:74
  211.0 32.5 %collective-permute-start.30 = (f32[256,768]{1,0:T(8,128)}, f32[256,768]{1,0:T(8,128)}, u32[]{:S(2)}, u32[]{:S(2)}) collective-permute-start(f32[256,768]{1,0:T(8,128)} %get-tuple-element.155.refs_3_), channel_id=1, source_target_pairs={{0,4},{2,6},{4,0},{6,2},{8,12},{10,14},{12,8},{14,10},{16,20},{18,... | collective-permute-start | bytes 2359304 | tf_op jit(solution)/shard_map/ppermute | solution.py:74
  243.5 16.9 %collective-permute-start.33 = (f32[256,1024]{1,0:T(8,128)}, f32[256,1024]{1,0:T(8,128)}, u32[]{:S(2)}, u32[]{:S(2)}) collective-permute-start(f32[256,1024]{1,0:T(8,128)} %get-tuple-element.158.refs_2_), channel_id=1, source_target_pairs={{0,8},{2,10},{4,12},{6,14},{8,16},{10,18},{12,20},{14,22},{16,24},... | collective-permute-start | bytes 3145736 | tf_op jit(solution)/shard_map/ppermute | solution.py:74
  243.5 15.4 %collective-permute-start.31 = (f32[256,768]{1,0:T(8,128)}, f32[256,768]{1,0:T(8,128)}, u32[]{:S(2)}, u32[]{:S(2)}) collective-permute-start(f32[256,768]{1,0:T(8,128)} %get-tuple-element.156.refs_1_), channel_id=1, source_target_pairs={{0,2},{2,0},{4,6},{6,4},{8,10},{10,8},{12,14},{14,12},{16,18},{18,... | collective-permute-start | bytes 2359304 | tf_op jit(solution)/shard_map/ppermute | solution.py:74
  244.6 14.2 %collective-permute-start.32 = (f32[256,768]{1,0:T(8,128)}, f32[256,768]{1,0:T(8,128)}, u32[]{:S(2)}, u32[]{:S(2)}) collective-permute-start(f32[256,768]{1,0:T(8,128)} %get-tuple-element.157.refs_4_), channel_id=1, source_target_pairs={{0,4},{2,6},{4,0},{6,2},{8,12},{10,14},{12,8},{14,10},{16,20},{18,... | collective-permute-start | bytes 2359304 | tf_op jit(solution)/shard_map/ppermute | solution.py:74
  267.7 27.2 %collective-permute-start.36 = (f32[256,1024]{1,0:T(8,128)}, f32[256,1024]{1,0:T(8,128)}, u32[]{:S(2)}, u32[]{:S(2)}) collective-permute-start(f32[256,1024]{1,0:T(8,128)} %get-tuple-element.179.refs_3_), channel_id=1, source_target_pairs={{0,8},{2,10},{4,12},{6,14},{8,16},{10,18},{12,20},{14,22},{16,24},... | collective-permute-start | bytes 3145736 | tf_op jit(solution)/shard_map/ppermute | solution.py:74
  267.7 51.2 %collective-permute-start.38 = (f32[512,1024]{1,0:T(8,128)}, f32[512,1024]{1,0:T(8,128)}, u32[]{:S(2)}, u32[]{:S(2)}) collective-permute-start(f32[512,1024]{1,0:T(8,128)} %get-tuple-element.181.refs_4_), channel_id=1, source_target_pairs={{0,2},{2,0},{4,6},{6,4},{8,10},{10,8},{12,14},{14,12},{16,18},{18,... | collective-permute-start | bytes 6291464 | tf_op jit(solution)/shard_map/ppermute | solution.py:74
  268.5 50.4 %collective-permute-start.39 = (f32[512,1024]{1,0:T(8,128)}, f32[512,1024]{1,0:T(8,128)}, u32[]{:S(2)}, u32[]{:S(2)}) collective-permute-start(f32[512,1024]{1,0:T(8,128)} %get-tuple-element.182.refs_6_), channel_id=1, source_target_pairs={{0,4},{2,6},{4,0},{6,2},{8,12},{10,14},{12,8},{14,10},{16,20},{18,... | collective-permute-start | bytes 6291464 | tf_op jit(solution)/shard_map/ppermute | solution.py:74
  294.9 26.4 %collective-permute-start.37 = (f32[256,1024]{1,0:T(8,128)}, f32[256,1024]{1,0:T(8,128)}, u32[]{:S(2)}, u32[]{:S(2)}) collective-permute-start(f32[256,1024]{1,0:T(8,128)} %get-tuple-element.180.refs_6_), channel_id=1, source_target_pairs={{0,8},{2,10},{4,12},{6,14},{8,16},{10,18},{12,20},{14,22},{16,24},... | collective-permute-start | bytes 3145736 | tf_op jit(solution)/shard_map/ppermute | solution.py:74
  321.3 25.4 %collective-permute-start.40 = (f32[256,1024]{1,0:T(8,128)}, f32[256,1024]{1,0:T(8,128)}, u32[]{:S(2)}, u32[]{:S(2)}) collective-permute-start(f32[256,1024]{1,0:T(8,128)} %get-tuple-element.185.refs_5_), channel_id=1, source_target_pairs={{0,8},{2,10},{4,12},{6,14},{8,16},{10,18},{12,20},{14,22},{16,24},... | collective-permute-start | bytes 3145736 | tf_op jit(solution)/shard_map/ppermute | solution.py:74
  (14 other events, 205.8 us)

commit v4 on v3

--- a/solution.py
+++ b/solution.py
@@ -200,6 +200,27 @@
         compiler_params=pltpu.CompilerParams(vmem_limit_bytes=grant),
         cost_estimate=light,
         name="stack",
+    )(*values)
+
+
+def rows_kernel(*refs):
+    for ref, out_ref in zip(refs[: len(refs) // 2], refs[len(refs) // 2 :]):
+        out_ref[...] = ref[...]
+
+
+def cut_rows(values, rows):
+    units = values[0].shape[1]
+    tile = tile_of(units)
+    block = pl.BlockSpec((rows, tile), lambda n: (0, n))
+    return pl.pallas_call(
+        rows_kernel,
+        grid=(units // tile,),
+        in_specs=[block] * len(values),
+        out_specs=[block] * len(values),
+        out_shape=[jax.ShapeDtypeStruct((rows, units), jnp.float32)] * len(values),
+        compiler_params=pltpu.CompilerParams(vmem_limit_bytes=grant),
+        cost_estimate=light,
+        name="cut_rows",
     )(*values)
 
 
@@ -593,7 +614,7 @@
     ring = []
     for step in range(1, deep):
         ring.append(move(ring[-1] if ring else activated, dz=1))
-    step_a, step_b = got_x[:quarter], got_y[:quarter]
+    step_a, step_b = cut_rows([got_x, got_y], quarter)
     first_step = [move(line_a, dy=1), move(step_a, dy=1), move(line_b, dx=1), move(step_b, dx=1)]
     span = tok_out_weight.shape[0]
     out_high, out_low = prepare([tok_out_weight], [[(0, 0, span)]])

time: 371 us -> 373 us (level)
  local copies, waits for them, and re-layouts: 9.92 us -> 4.5 us
    slice x2 -> x0, local copies, waits for them, and re-layouts: 4.67 us -> none  [shards(): step_a, step_b = (got_x[:quarter], got_y[:quarter])]
    pallas_call x0 -> x1, Pallas kernels: none -> 3.81 us  [cut_rows(): pl.pallas_call(rows_kernel, grid=(units // tile,), in_specs=[block] * len...]
  transfers between devices with their start and end apart: 42 -> 42, of which waited for: 20 -> 20; matrix products, arithmetic and copies ran while one was open for 6% -> 5% of each run, Pallas kernels for 41% -> 42%
where the time goes in v4:
time: 373 us; the launch traced here: 371 us
  Pallas kernels  180 us (48%)
  waiting for transfers between devices  140 us (38%)
  starting transfers between devices  33.9 us (9%)
  other arithmetic  12.7 us (3%)
  local copies, waits for them, and re-layouts  4.5 us (1%)
    ppermute x37, waiting for transfers between devices, move(): return lax.ppermute(value, 'tok', pairs)  135 us
    pallas_call x3, Pallas kernels, expand(): pl.pallas_call(functools.partial(expand_kernel, groups, len(pieces)), gri...  35.4 us
    pallas_call x2, Pallas kernels, reduce(): pl.pallas_call(functools.partial(reduce_kernel, [chunk[2] for chunk in ch...  34.4 us
    ppermute x37, starting transfers between devices, move(): return lax.ppermute(value, 'tok', pairs)  32.9 us
    pallas_call x2, Pallas kernels, mix(): pl.pallas_call(functools.partial(mix_kernel, steps), grid=(2 * steps,), i...  21.8 us
    pallas_call x2, Pallas kernels, project(): pl.pallas_call(functools.partial(project_kernel, rows, places), grid=(wid...  19.4 us
    pallas_call x3, Pallas kernels, prepare(): pl.pallas_call(functools.partial(prepare_kernel, groups, len(pieces)), gr...  18.3 us
    pallas_call x4, Pallas kernels, stack(): pl.pallas_call(functools.partial(stack_kernel, len(values), outs), grid=(...  15 us
  transfers between devices with their start and end apart: 42, of which 20 were waited for; matrix products, arithmetic and copies ran while one was open for 5% of the time, Pallas kernels for 42%

profile of v4, /device:TPU:0, one launch (start us, length us, event | category | flops | bytes accessed | tf_op | source)
XLA Modules:
  0.0 371.4 jit_solution(12998364706167847855)
XLA Ops:
  12.5 8.0 %norm_one.1 = (f32[1024,1024]{1,0:T(8,128)}, bf16[1024,1024]{1,0:T(8,128)(2,1)}, bf16[1024,1024]{1,0:T(8,128)(2,1)}) custom-call(s32[4]{0:T(128)} %pad_add_fusion.place_ref.refs_0_, f32[1024,1]{1,0:T(8,128)} %get-tuple-element.199.gain_ref, f32[1024,512]{1,0:T(8,128)} %refs_0_.2, f32[1024,512]{1,0:T(8,128)} %collective-permute-done.1.refs_1_), custom_call_target="tpu_custom_call" | custom-call | tf_op jit(solution)/shard_map/norm_one/pallas_call | solution.py:123
  25.4 10.9 %mix.2 = (f32[512,768]{1,0:T(8,128)}, f32[512,768]{1,0:T(8,128)}) custom-call(bf16[1024,1024]{1,0:T(8,128)(2,1)} %get-tuple-element.106.high_one.high_two, bf16[1024,1024]{1,0:T(8,128)(2,1)} %get-tuple-element.106.high_one.high_two, bf16[1024,1024]{1,0:T(8,128)(2,1)} %get-tuple-element.107.low_one.low_two, ...), custom_call_target="tpu_custom_call" | custom-call | tf_op jit(solution)/shard_map/mix/pallas_call | solution.py:166
  44.6 10.8 %mix.3 = (f32[512,768]{1,0:T(8,128)}, f32[512,768]{1,0:T(8,128)}) custom-call(bf16[1024,1024]{1,0:T(8,128)(2,1)} %get-tuple-element.106.high_one.high_two, bf16[1024,1024]{1,0:T(8,128)(2,1)} %get-tuple-element.106.high_one.high_two, bf16[1024,1024]{1,0:T(8,128)(2,1)} %get-tuple-element.107.low_one.low_two, ...), custom_call_target="tpu_custom_call" | custom-call | tf_op jit(solution)/shard_map/mix/pallas_call | solution.py:166
  58.7 6.0 %collective-permute-done.9.refs_6_ = f32[128,2048]{1,0:T(8,128)} collective-permute-done((f32[128,2048]{1,0:T(8,128)}, f32[128,2048]{1,0:T(8,128)}, u32[]{:S(2)}, u32[]{:S(2)}) %collective-permute-start.9) | collective-permute-done | bytes 1048608 | tf_op jit(solution)/shard_map/ppermute | solution.py:74
  64.7 7.8 %collective-permute-done.7.refs_0_ = f32[512,768]{1,0:T(8,128)} collective-permute-done((f32[512,768]{1,0:T(8,128)}, f32[512,768]{1,0:T(8,128)}, u32[]{:S(2)}, u32[]{:S(2)}) %collective-permute-start.7) | collective-permute-done | bytes 1572896 | tf_op jit(solution)/shard_map/ppermute | solution.py:74
  74.4 3.8 %halve.1 = (f32[256,768]{1,0:T(8,128)}, f32[256,768]{1,0:T(8,128)}) custom-call(f32[512,768]{1,0:T(8,128)} %get-tuple-element.120.kept_a.refs_0_, f32[512,768]{1,0:T(8,128)} %get-tuple-element.121.sent_a.refs_1_, f32[512,768]{1,0:T(8,128)} %get-tuple-element.122.kept_b.refs_3_, f32[512,768]{1,0:T(8,128)} %get-tuple-element.123.sent_b.refs_4_), custom_call_target="tpu_custom_call" | custom-call | tf_op jit(solution)/shard_map/halve/pallas_call | solution.py:235
  81.1 13.5 %collective-permute-done.10.refs_0_ = f32[256,768]{1,0:T(8,128)} collective-permute-done((f32[256,768]{1,0:T(8,128)}, f32[256,768]{1,0:T(8,128)}, u32[]{:S(2)}, u32[]{:S(2)}) %collective-permute-start.10) | collective-permute-done | bytes 786464 | tf_op jit(solution)/shard_map/ppermute | solution.py:74
  96.9 5.0 %stack.36 = (f32[512,1024]{1,0:T(8,128)}, f32[512,1024]{1,0:T(8,128)}, f32[256,1024]{1,0:T(8,128)}, f32[256,1024]{1,0:T(8,128)}) custom-call(f32[128,2048]{1,0:T(8,128)} %get-tuple-element.110.refs_0_, f32[128,2048]{1,0:T(8,128)} %get-tuple-element.133.refs_1_, f32[128,2048]{1,0:T(8,128)} %get-tuple-element.126.refs_2_, f32[128,2048]{1,0:T(8,128)} %get-tuple-element.119.refs_3_), custom_call_target="tpu_custom_call" | custom-call | tf_op jit(solution)/shard_map/stack/pallas_call | solution.py:194
  108.2 10.1 %collective-permute-done.13 = f32[64,1536]{1,0:T(8,128)S(1)} collective-permute-done((f32[64,1536]{1,0:T(8,128)}, f32[64,1536]{1,0:T(8,128)S(1)}, u32[]{:S(2)}, u32[]{:S(2)}) %collective-permute-start.13) | collective-permute-done | bytes 393248 | tf_op jit(solution)/shard_map/ppermute | solution.py:74
  120.3 12.9 %collective-permute-done.14 = f32[64,1536]{1,0:T(8,128)S(1)} collective-permute-done((f32[64,1536]{1,0:T(8,128)S(1)}, f32[64,1536]{1,0:T(8,128)S(1)}, u32[]{:S(2)}, u32[]{:S(2)}) %collective-permute-start.14) | collective-permute-done | bytes 393248 | tf_op jit(solution)/shard_map/ppermute | solution.py:74
  134.4 22.9 %collective-permute-done.15 = f32[64,1536]{1,0:T(8,128)S(1)} collective-permute-done((f32[64,1536]{1,0:T(8,128)S(1)}, f32[64,1536]{1,0:T(8,128)S(1)}, u32[]{:S(2)}, u32[]{:S(2)}) %collective-permute-start.15) | collective-permute-done | bytes 393248 | tf_op jit(solution)/shard_map/ppermute | solution.py:74
  159.6 3.8 %cut_rows.1 = (f32[256,1024]{1,0:T(8,128)}, f32[256,1024]{1,0:T(8,128)}) custom-call(f32[512,1024]{1,0:T(8,128)} %get-tuple-element.141.refs_1_.refs_0_, f32[512,1024]{1,0:T(8,128)} %get-tuple-element.140.refs_1_), custom_call_target="tpu_custom_call" | custom-call | tf_op jit(solution)/shard_map/cut_rows/pallas_call | solution.py:215
  166.9 5.8 %collective-permute-done.20.refs_3_ = f32[64,1536]{1,0:T(8,128)} collective-permute-done((f32[64,1536]{1,0:T(8,128)}, f32[64,1536]{1,0:T(8,128)}, u32[]{:S(2)}, u32[]{:S(2)}) %collective-permute-start.20) | collective-permute-done | bytes 393248 | tf_op jit(solution)/shard_map/ppermute | solution.py:74
  172.7 14.1 %collective-permute-done.21.refs_2_ = f32[64,1536]{1,0:T(8,128)} collective-permute-done((f32[64,1536]{1,0:T(8,128)}, f32[64,1536]{1,0:T(8,128)}, u32[]{:S(2)}, u32[]{:S(2)}) %collective-permute-start.21) | collective-permute-done | bytes 393248 | tf_op jit(solution)/shard_map/ppermute | solution.py:74
  186.9 7.3 %prepare.3 = (bf16[1536,1024]{1,0:T(8,128)(2,1)}, bf16[1536,1024]{1,0:T(8,128)(2,1)}) custom-call(f32[1024,1536]{1,0:T(8,128)} %refs_0_.3), custom_call_target="tpu_custom_call" | custom-call | tf_op jit(solution)/shard_map/prepare/pallas_call | solution.py:358
  194.2 6.1 %collective-permute-done.24.refs_4_ = f32[256,1024]{1,0:T(8,128)} collective-permute-done((f32[256,1024]{1,0:T(8,128)}, f32[256,1024]{1,0:T(8,128)}, u32[]{:S(2)}, u32[]{:S(2)}) %collective-permute-start.24) | collective-permute-done | bytes 1048608 | tf_op jit(solution)/shard_map/ppermute | solution.py:74
  200.3 7.6 %collective-permute-done.26.refs_6_ = f32[256,1024]{1,0:T(8,128)} collective-permute-done((f32[256,1024]{1,0:T(8,128)}, f32[256,1024]{1,0:T(8,128)}, u32[]{:S(2)}, u32[]{:S(2)}) %collective-permute-start.26) | collective-permute-done | bytes 1048608 | tf_op jit(solution)/shard_map/ppermute | solution.py:74
  214.5 3.8 %stack.37.refs_1_ = f32[512,1024]{1,0:T(8,128)} custom-call(f32[512,1024]{1,0:T(8,128)} %get-tuple-element.137.refs_0_, f32[512,1024]{1,0:T(8,128)} %get-tuple-element.140.refs_1_), custom_call_target="tpu_custom_call" | custom-call | tf_op jit(solution)/shard_map/stack/pallas_call | solution.py:194
  221.9 5.5 %prepare.4 = (bf16[1024,1024]{1,0:T(8,128)(2,1)}, bf16[1024,1024]{1,0:T(8,128)(2,1)}) custom-call(f32[256,1024]{1,0:T(8,128)} %get-tuple-element.142.refs_0_, f32[256,1024]{1,0:T(8,128)} %get-tuple-element.143.refs_1_, f32[256,1024]{1,0:T(8,128)} %get-tuple-element.149.refs_2_, f32[256,1024]{1,0:T(8,128)} %get-tuple-element.150.refs_3_), custom_call_target="tpu_custom_call" | custom-call | tf_op jit(solution)/shard_map/prepare/pallas_call | solution.py:358
  227.4 5.5 %prepare.5 = (bf16[1024,1024]{1,0:T(8,128)(2,1)}, bf16[1024,1024]{1,0:T(8,128)(2,1)}) custom-call(f32[256,1024]{1,0:T(8,128)} %get-tuple-element.147.refs_0_, f32[256,1024]{1,0:T(8,128)} %get-tuple-element.148.refs_1_, f32[256,1024]{1,0:T(8,128)} %get-tuple-element.153.refs_2_, f32[256,1024]{1,0:T(8,128)} %get-tuple-element.154.refs_3_), custom_call_target="tpu_custom_call" | custom-call | tf_op jit(solution)/shard_map/prepare/pallas_call | solution.py:358
  232.9 12.0 %collective-permute-done.29.refs_9_ = f32[256,768]{1,0:T(8,128)} collective-permute-done((f32[256,768]{1,0:T(8,128)}, f32[256,768]{1,0:T(8,128)}, u32[]{:S(2)}, u32[]{:S(2)}) %collective-permute-start.29) | collective-permute-done | bytes 786464 | tf_op jit(solution)/shard_map/ppermute | solution.py:74
  247.8 12.5 %project.2.refs_3_ = f32[768,1024]{1,0:T(8,128)} custom-call(bf16[1536,1024]{1,0:T(8,128)(2,1)} %get-tuple-element.163.high, bf16[1536,1024]{1,0:T(8,128)(2,1)} %get-tuple-element.164.low, f32[256,768]{1,0:T(8,128)} %get-tuple-element.158.refs_0_, f32[256,768]{1,0:T(8,128)} %get-tuple-element.160.refs_1_, f32[256,768]{1,0:T(8,128)} %get-tuple-element.165.refs_2_, ...), custom_call_target="tpu_custom_call" | custom-call | tf_op jit(solution)/shard_map/project/pallas_call | solution.py:298
  261.9 6.9 %project.3.refs_1_ = f32[256,1024]{1,0:T(8,128)} custom-call(bf16[1536,1024]{1,0:T(8,128)(2,1)} %get-tuple-element.163.high, bf16[1536,1024]{1,0:T(8,128)(2,1)} %get-tuple-element.164.low, f32[256,768]{1,0:T(8,128)} %get-tuple-element.168.refs_0_, f32[256,768]{1,0:T(8,128)} %get-tuple-element.169.refs_1_), custom_call_target="tpu_custom_call" | custom-call | tf_op jit(solution)/shard_map/project/pallas_call | solution.py:298
  272.0 10.0 %norm_two.1 = (f32[1024,1024]{1,0:T(8,128)}, bf16[1024,1024]{1,0:T(8,128)(2,1)}, bf16[1024,1024]{1,0:T(8,128)(2,1)}) custom-call(s32[4]{0:T(128)} %pad_add_fusion.place_ref.refs_0_, f32[1024,1]{1,0:T(8,128)} %get-tuple-element.200.gain_ref, f32[1024,1024]{1,0:T(8,128)} %get-tuple-element.102.fields_ref, f32[768,1024]{1,0:T(8,128)} %get-tuple-element.167.refs_0_, ...), custom_call_target="tpu_custom_call" | custom-call | tf_op jit(solution)/shard_map/norm_two/pallas_call | solution.py:328
  282.0 11.4 %expand.5 = (bf16[1024,1024]{1,0:T(8,128)(2,1)}, bf16[1024,1024]{1,0:T(8,128)(2,1)}) custom-call(bf16[1024,1024]{1,0:T(8,128)(2,1)} %get-tuple-element.170.high_ref, bf16[1024,1024]{1,0:T(8,128)(2,1)} %get-tuple-element.171.low_ref, f32[1024,1]{1,0:T(8,128)} %get-tuple-element.179.bias_ref, bf16[1024,1024]{1,0:T(8,128)(2,1)} %get-tuple-element.180.refs_0_, ...), custom_call_target="tpu_custom_call" | custom-call | tf_op jit(solution)/shard_map/expand/pallas_call | solution.py:390
  296.4 12.7 %expand.4 = (bf16[1024,1024]{1,0:T(8,128)(2,1)}, bf16[1024,1024]{1,0:T(8,128)(2,1)}) custom-call(bf16[1024,1024]{1,0:T(8,128)(2,1)} %get-tuple-element.170.high_ref, bf16[1024,1024]{1,0:T(8,128)(2,1)} %get-tuple-element.171.low_ref, f32[1024,1]{1,0:T(8,128)} %get-tuple-element.176.bias_ref, f32[256,1024]{1,0:T(8,128)} %get-tuple-element.138.refs_0_, ...), custom_call_target="tpu_custom_call" | custom-call | tf_op jit(solution)/shard_map/expand/pallas_call | solution.py:390
  309.1 11.3 %expand.3 = (bf16[1024,1024]{1,0:T(8,128)(2,1)}, bf16[1024,1024]{1,0:T(8,128)(2,1)}) custom-call(bf16[1024,1024]{1,0:T(8,128)(2,1)} %get-tuple-element.170.high_ref, bf16[1024,1024]{1,0:T(8,128)(2,1)} %get-tuple-element.171.low_ref, f32[1024,1]{1,0:T(8,128)} %get-tuple-element.172.bias_ref, bf16[1024,1024]{1,0:T(8,128)(2,1)} %get-tuple-element.173.refs_0_, ...), custom_call_target="tpu_custom_call" | custom-call | tf_op jit(solution)/shard_map/expand/pallas_call | solution.py:390
  322.8 20.2 %reduce.2.refs_7_ = f32[1024,1024]{1,0:T(8,128)} custom-call(bf16[1024,1024]{1,0:T(8,128)(2,1)} %get-tuple-element.190.refs_0_, bf16[1024,1024]{1,0:T(8,128)(2,1)} %get-tuple-element.191.refs_1_, bf16[1024,1024]{1,0:T(8,128)(2,1)} %get-tuple-element.192.refs_2_, bf16[1024,1024]{1,0:T(8,128)(2,1)} %get-tuple-element.193.refs_3_, ...), custom_call_target="tpu_custom_call" | custom-call | tf_op jit(solution)/shard_map/reduce/pallas_call | solution.py:461
  343.0 5.2 %collective-permute-done.40.refs_4_ = f32[256,1024]{1,0:T(8,128)} collective-permute-done((f32[256,1024]{1,0:T(8,128)}, f32[256,1024]{1,0:T(8,128)}, u32[]{:S(2)}, u32[]{:S(2)}) %collective-permute-start.40) | collective-permute-done | bytes 1048608 | tf_op jit(solution)/shard_map/ppermute | solution.py:74
  348.2 14.2 %reduce.3 = (f32[512,1024]{1,0:T(8,128)}, f32[512,1024]{1,0:T(8,128)}) custom-call(s32[4]{0:T(128)} %pad_add_fusion.place_ref.refs_0_, bf16[1024,1024]{1,0:T(8,128)(2,1)} %get-tuple-element.187.refs_1_, bf16[1024,1024]{1,0:T(8,128)(2,1)} %get-tuple-element.188.refs_2_, f32[256,1024]{1,0:T(8,128)} %get-tuple-element.183.refs_3_, ...), custom_call_target="tpu_custom_call" | custom-call | tf_op jit(solution)/shard_map/reduce/pallas_call | solution.py:461
  362.4 4.5 %collective-permute-done.41.refs_1_ = f32[512,1024]{1,0:T(8,128)} collective-permute-done((f32[512,1024]{1,0:T(8,128)}, f32[512,1024]{1,0:T(8,128)}, u32[]{:S(2)}, u32[]{:S(2)}) %collective-permute-start.41) | collective-permute-done | bytes 2097184 | tf_op jit(solution)/shard_map/ppermute | solution.py:77
  366.9 4.5 %finish.1 = f32[1024,512]{1,0:T(8,128)} custom-call(f32[512,1024]{1,0:T(8,128)} %get-tuple-element.197.refs_0_, f32[512,1024]{1,0:T(8,128)} %collective-permute-done.41.refs_1_), custom_call_target="tpu_custom_call" | custom-call | tf_op jit(solution)/shard_map/finish/pallas_call | solution.py:491
  (106 shorter events, 74.7 us)
Async XLA Ops:
  3.8 16.7 %collective-permute-start.2 = (f32[64,1024]{1,0:T(8,128)}, f32[64,1024]{1,0:T(8,128)}, u32[]{:S(2)}, u32[]{:S(2)}) collective-permute-start(f32[64,1024]{1,0:T(8,128)} %get-tuple-element.104), channel_id=1, source_target_pairs={{0,2},{2,0},{4,6},{6,4},{8,10},{10,8},{12,14},{14,12},{16,18},{18,... | collective-permute-start | bytes 786440 | tf_op jit(solution)/shard_map/ppermute | solution.py:74
  8.3 28.0 %collective-permute-start.4 = (f32[128,2048]{1,0:T(8,128)}, f32[128,2048]{1,0:T(8,128)}, u32[]{:S(2)}, u32[]{:S(2)}) collective-permute-start(f32[128,2048]{1,0:T(8,128)} %get-tuple-element.110.refs_0_), channel_id=1, source_target_pairs={{0,8},{2,10},{4,12},{6,14},{8,16},{10,18},{12,20},{14,22},{16,24},... | collective-permute-start | bytes 3145736 | tf_op jit(solution)/shard_map/ppermute | solution.py:74
  37.9 34.6 %collective-permute-start.7 = (f32[512,768]{1,0:T(8,128)}, f32[512,768]{1,0:T(8,128)}, u32[]{:S(2)}, u32[]{:S(2)}) collective-permute-start(f32[512,768]{1,0:T(8,128)} %get-tuple-element.113), channel_id=1, source_target_pairs={{0,2},{2,0},{4,6},{6,4},{8,10},{10,8},{12,14},{14,12},{16,18},{18,... | collective-permute-start | bytes 4718600 | tf_op jit(solution)/shard_map/ppermute | solution.py:74
  38.4 34.4 %collective-permute-start.8 = (f32[512,768]{1,0:T(8,128)}, f32[512,768]{1,0:T(8,128)}, u32[]{:S(2)}, u32[]{:S(2)}) collective-permute-start(f32[512,768]{1,0:T(8,128)} %get-tuple-element.114), channel_id=1, source_target_pairs={{0,4},{2,6},{4,0},{6,2},{8,12},{10,14},{12,8},{14,10},{16,20},{18,... | collective-permute-start | bytes 4718600 | tf_op jit(solution)/shard_map/ppermute | solution.py:74
  39.9 24.7 %collective-permute-start.9 = (f32[128,2048]{1,0:T(8,128)}, f32[128,2048]{1,0:T(8,128)}, u32[]{:S(2)}, u32[]{:S(2)}) collective-permute-start(f32[128,2048]{1,0:T(8,128)} %get-tuple-element.119.refs_3_), channel_id=1, source_target_pairs={{0,8},{2,10},{4,12},{6,14},{8,16},{10,18},{12,20},{14,22},{16,24},... | collective-permute-start | bytes 3145736 | tf_op jit(solution)/shard_map/ppermute | solution.py:74
  72.9 24.1 %collective-permute-start.12 = (f32[128,2048]{1,0:T(8,128)}, f32[128,2048]{1,0:T(8,128)}, u32[]{:S(2)}, u32[]{:S(2)}) collective-permute-start(f32[128,2048]{1,0:T(8,128)} %get-tuple-element.126.refs_2_), channel_id=1, source_target_pairs={{0,8},{2,10},{4,12},{6,14},{8,16},{10,18},{12,20},{14,22},{16,24},... | collective-permute-start | bytes 3145736 | tf_op jit(solution)/shard_map/ppermute | solution.py:74
  78.2 16.4 %collective-permute-start.10 = (f32[256,768]{1,0:T(8,128)}, f32[256,768]{1,0:T(8,128)}, u32[]{:S(2)}, u32[]{:S(2)}) collective-permute-start(f32[256,768]{1,0:T(8,128)} %get-tuple-element.124), channel_id=1, source_target_pairs={{0,4},{2,6},{4,0},{6,2},{8,12},{10,14},{12,8},{14,10},{16,20},{18,... | collective-permute-start | bytes 2359304 | tf_op jit(solution)/shard_map/ppermute | solution.py:74
  79.7 16.1 %collective-permute-start.11 = (f32[256,768]{1,0:T(8,128)}, f32[256,768]{1,0:T(8,128)}, u32[]{:S(2)}, u32[]{:S(2)}) collective-permute-start(f32[256,768]{1,0:T(8,128)} %get-tuple-element.125), channel_id=1, source_target_pairs={{0,2},{2,0},{4,6},{6,4},{8,10},{10,8},{12,14},{14,12},{16,18},{18,... | collective-permute-start | bytes 2359304 | tf_op jit(solution)/shard_map/ppermute | solution.py:74
  101.9 57.1 %collective-permute-start.16 = (f32[512,1024]{1,0:T(8,128)}, f32[512,1024]{1,0:T(8,128)}, u32[]{:S(2)}, u32[]{:S(2)}) collective-permute-start(f32[512,1024]{1,0:T(8,128)} %get-tuple-element.136.refs_0_), channel_id=1, source_target_pairs={{0,2},{2,0},{4,6},{6,4},{8,10},{10,8},{12,14},{14,12},{16,18},{18,... | collective-permute-start | bytes 6291464 | tf_op jit(solution)/shard_map/ppermute | solution.py:74
  103.1 55.8 %collective-permute-start.17 = (f32[512,1024]{1,0:T(8,128)}, f32[512,1024]{1,0:T(8,128)}, u32[]{:S(2)}, u32[]{:S(2)}) collective-permute-start(f32[512,1024]{1,0:T(8,128)} %get-tuple-element.137.refs_0_), channel_id=1, source_target_pairs={{0,4},{2,6},{4,0},{6,2},{8,12},{10,14},{12,8},{14,10},{16,20},{18,... | collective-permute-start | bytes 6291464 | tf_op jit(solution)/shard_map/ppermute | solution.py:74
  119.3 13.9 %collective-permute-start.14 = (f32[64,1536]{1,0:T(8,128)S(1)}, f32[64,1536]{1,0:T(8,128)S(1)}, u32[]{:S(2)}, u32[]{:S(2)}) collective-permute-start(f32[64,1536]{1,0:T(8,128)S(1)} %add.28), channel_id=1, source_target_pairs={{0,8},{2,10},{4,12},{6,14},{8,16},{10,18},{12,20},{14,22},{16,24},... | collective-permute-start | bytes 1179656 | tf_op jit(solution)/shard_map/ppermute | solution.py:74
  119.4 39.6 %collective-permute-start.18 = (f32[256,1024]{1,0:T(8,128)}, f32[256,1024]{1,0:T(8,128)}, u32[]{:S(2)}, u32[]{:S(2)}) collective-permute-start(f32[256,1024]{1,0:T(8,128)} %get-tuple-element.138.refs_0_), channel_id=1, source_target_pairs={{0,8},{2,10},{4,12},{6,14},{8,16},{10,18},{12,20},{14,22},{16,24},... | collective-permute-start | bytes 3145736 | tf_op jit(solution)/shard_map/ppermute | solution.py:74
  134.3 23.0 %collective-permute-start.15 = (f32[64,1536]{1,0:T(8,128)S(1)}, f32[64,1536]{1,0:T(8,128)S(1)}, u32[]{:S(2)}, u32[]{:S(2)}) collective-permute-start(f32[64,1536]{1,0:T(8,128)S(1)} %add.29), channel_id=1, source_target_pairs={{0,8},{2,10},{4,12},{6,14},{8,16},{10,18},{12,20},{14,22},{16,24},... | collective-permute-start | bytes 1179656 | tf_op jit(solution)/shard_map/ppermute | solution.py:74
  159.0 27.9 %collective-permute-start.23 = (f32[256,1024]{1,0:T(8,128)}, f32[256,1024]{1,0:T(8,128)}, u32[]{:S(2)}, u32[]{:S(2)}) collective-permute-start(f32[256,1024]{1,0:T(8,128)} %get-tuple-element.142.refs_0_), channel_id=1, source_target_pairs={{0,4},{2,6},{4,0},{6,2},{8,12},{10,14},{12,8},{14,10},{16,20},{18,... | collective-permute-start | bytes 3145736 | tf_op jit(solution)/shard_map/ppermute | solution.py:74
  163.4 36.9 %collective-permute-start.24 = (f32[256,1024]{1,0:T(8,128)}, f32[256,1024]{1,0:T(8,128)}, u32[]{:S(2)}, u32[]{:S(2)}) collective-permute-start(f32[256,1024]{1,0:T(8,128)} %get-tuple-element.143.refs_1_), channel_id=1, source_target_pairs={{0,4},{2,6},{4,0},{6,2},{8,12},{10,14},{12,8},{14,10},{16,20},{18,... | collective-permute-start | bytes 3145736 | tf_op jit(solution)/shard_map/ppermute | solution.py:74
  164.9 35.4 %collective-permute-start.25 = (f32[256,1024]{1,0:T(8,128)}, f32[256,1024]{1,0:T(8,128)}, u32[]{:S(2)}, u32[]{:S(2)}) collective-permute-start(f32[256,1024]{1,0:T(8,128)} %get-tuple-element.147.refs_0_), channel_id=1, source_target_pairs={{0,2},{2,0},{4,6},{6,4},{8,10},{10,8},{12,14},{14,12},{16,18},{18,... | collective-permute-start | bytes 3145736 | tf_op jit(solution)/shard_map/ppermute | solution.py:74
  165.7 42.2 %collective-permute-start.26 = (f32[256,1024]{1,0:T(8,128)}, f32[256,1024]{1,0:T(8,128)}, u32[]{:S(2)}, u32[]{:S(2)}) collective-permute-start(f32[256,1024]{1,0:T(8,128)} %get-tuple-element.148.refs_1_), channel_id=1, source_target_pairs={{0,2},{2,0},{4,6},{6,4},{8,10},{10,8},{12,14},{14,12},{16,18},{18,... | collective-permute-start | bytes 3145736 | tf_op jit(solution)/shard_map/ppermute | solution.py:74
  172.7 14.1 %collective-permute-start.21 = (f32[64,1536]{1,0:T(8,128)}, f32[64,1536]{1,0:T(8,128)}, u32[]{:S(2)}, u32[]{:S(2)}) collective-permute-start(f32[64,1536]{1,0:T(8,128)} %collective-permute-done.20.refs_3_), channel_id=1, source_target_pairs={{0,8},{2,10},{4,12},{6,14},{8,16},{10,18},{12,20},{14,22},{16,24},... | collective-permute-start | bytes 1179656 | tf_op jit(solution)/shard_map/ppermute | solution.py:74
  186.8 21.1 %collective-permute-start.22 = (f32[64,1536]{1,0:T(8,128)}, f32[64,1536]{1,0:T(8,128)}, u32[]{:S(2)}, u32[]{:S(2)}) collective-permute-start(f32[64,1536]{1,0:T(8,128)} %collective-permute-done.21.refs_2_), channel_id=1, source_target_pairs={{0,8},{2,10},{4,12},{6,14},{8,16},{10,18},{12,20},{14,22},{16,24},... | collective-permute-start | bytes 1179656 | tf_op jit(solution)/shard_map/ppermute | solution.py:74
  186.8 46.1 %collective-permute-start.19 = (f32[256,1024]{1,0:T(8,128)}, f32[256,1024]{1,0:T(8,128)}, u32[]{:S(2)}, u32[]{:S(2)}) collective-permute-start(f32[256,1024]{1,0:T(8,128)} %get-tuple-element.139.refs_3_), channel_id=1, source_target_pairs={{0,8},{2,10},{4,12},{6,14},{8,16},{10,18},{12,20},{14,22},{16,24},... | collective-permute-start | bytes 3145736 | tf_op jit(solution)/shard_map/ppermute | solution.py:74
  210.5 22.5 %collective-permute-start.27 = (f32[256,768]{1,0:T(8,128)}, f32[256,768]{1,0:T(8,128)}, u32[]{:S(2)}, u32[]{:S(2)}) collective-permute-start(f32[256,768]{1,0:T(8,128)} %get-tuple-element.158.refs_0_), channel_id=1, source_target_pairs={{0,4},{2,6},{4,0},{6,2},{8,12},{10,14},{12,8},{14,10},{16,20},{18,... | collective-permute-start | bytes 2359304 | tf_op jit(solution)/shard_map/ppermute | solution.py:74
  210.5 22.5 %collective-permute-start.28 = (f32[256,768]{1,0:T(8,128)}, f32[256,768]{1,0:T(8,128)}, u32[]{:S(2)}, u32[]{:S(2)}) collective-permute-start(f32[256,768]{1,0:T(8,128)} %get-tuple-element.158.refs_0_), channel_id=1, source_target_pairs={{0,2},{2,0},{4,6},{6,4},{8,10},{10,8},{12,14},{14,12},{16,18},{18,... | collective-permute-start | bytes 2359304 | tf_op jit(solution)/shard_map/ppermute | solution.py:74
  211.2 33.7 %collective-permute-start.29 = (f32[256,768]{1,0:T(8,128)}, f32[256,768]{1,0:T(8,128)}, u32[]{:S(2)}, u32[]{:S(2)}) collective-permute-start(f32[256,768]{1,0:T(8,128)} %get-tuple-element.159.refs_3_), channel_id=1, source_target_pairs={{0,2},{2,0},{4,6},{6,4},{8,10},{10,8},{12,14},{14,12},{16,18},{18,... | collective-permute-start | bytes 2359304 | tf_op jit(solution)/shard_map/ppermute | solution.py:74
  212.5 32.5 %collective-permute-start.30 = (f32[256,768]{1,0:T(8,128)}, f32[256,768]{1,0:T(8,128)}, u32[]{:S(2)}, u32[]{:S(2)}) collective-permute-start(f32[256,768]{1,0:T(8,128)} %get-tuple-element.159.refs_3_), channel_id=1, source_target_pairs={{0,4},{2,6},{4,0},{6,2},{8,12},{10,14},{12,8},{14,10},{16,20},{18,... | collective-permute-start | bytes 2359304 | tf_op jit(solution)/shard_map/ppermute | solution.py:74
  245.0 16.9 %collective-permute-start.33 = (f32[256,1024]{1,0:T(8,128)}, f32[256,1024]{1,0:T(8,128)}, u32[]{:S(2)}, u32[]{:S(2)}) collective-permute-start(f32[256,1024]{1,0:T(8,128)} %get-tuple-element.162.refs_2_), channel_id=1, source_target_pairs={{0,8},{2,10},{4,12},{6,14},{8,16},{10,18},{12,20},{14,22},{16,24},... | collective-permute-start | bytes 3145736 | tf_op jit(solution)/shard_map/ppermute | solution.py:74
  245.0 15.4 %collective-permute-start.31 = (f32[256,768]{1,0:T(8,128)}, f32[256,768]{1,0:T(8,128)}, u32[]{:S(2)}, u32[]{:S(2)}) collective-permute-start(f32[256,768]{1,0:T(8,128)} %get-tuple-element.160.refs_1_), channel_id=1, source_target_pairs={{0,2},{2,0},{4,6},{6,4},{8,10},{10,8},{12,14},{14,12},{16,18},{18,... | collective-permute-start | bytes 2359304 | tf_op jit(solution)/shard_map/ppermute | solution.py:74
  246.1 14.2 %collective-permute-start.32 = (f32[256,768]{1,0:T(8,128)}, f32[256,768]{1,0:T(8,128)}, u32[]{:S(2)}, u32[]{:S(2)}) collective-permute-start(f32[256,768]{1,0:T(8,128)} %get-tuple-element.161.refs_4_), channel_id=1, source_target_pairs={{0,4},{2,6},{4,0},{6,2},{8,12},{10,14},{12,8},{14,10},{16,20},{18,... | collective-permute-start | bytes 2359304 | tf_op jit(solution)/shard_map/ppermute | solution.py:74
  269.2 27.2 %collective-permute-start.36 = (f32[256,1024]{1,0:T(8,128)}, f32[256,1024]{1,0:T(8,128)}, u32[]{:S(2)}, u32[]{:S(2)}) collective-permute-start(f32[256,1024]{1,0:T(8,128)} %get-tuple-element.183.refs_3_), channel_id=1, source_target_pairs={{0,8},{2,10},{4,12},{6,14},{8,16},{10,18},{12,20},{14,22},{16,24},... | collective-permute-start | bytes 3145736 | tf_op jit(solution)/shard_map/ppermute | solution.py:74
  269.2 51.2 %collective-permute-start.38 = (f32[512,1024]{1,0:T(8,128)}, f32[512,1024]{1,0:T(8,128)}, u32[]{:S(2)}, u32[]{:S(2)}) collective-permute-start(f32[512,1024]{1,0:T(8,128)} %get-tuple-element.185.refs_4_), channel_id=1, source_target_pairs={{0,2},{2,0},{4,6},{6,4},{8,10},{10,8},{12,14},{14,12},{16,18},{18,... | collective-permute-start | bytes 6291464 | tf_op jit(solution)/shard_map/ppermute | solution.py:74
  270.0 50.4 %collective-permute-start.39 = (f32[512,1024]{1,0:T(8,128)}, f32[512,1024]{1,0:T(8,128)}, u32[]{:S(2)}, u32[]{:S(2)}) collective-permute-start(f32[512,1024]{1,0:T(8,128)} %get-tuple-element.186.refs_6_), channel_id=1, source_target_pairs={{0,4},{2,6},{4,0},{6,2},{8,12},{10,14},{12,8},{14,10},{16,20},{18,... | collective-permute-start | bytes 6291464 | tf_op jit(solution)/shard_map/ppermute | solution.py:74
  296.4 26.4 %collective-permute-start.37 = (f32[256,1024]{1,0:T(8,128)}, f32[256,1024]{1,0:T(8,128)}, u32[]{:S(2)}, u32[]{:S(2)}) collective-permute-start(f32[256,1024]{1,0:T(8,128)} %get-tuple-element.184.refs_6_), channel_id=1, source_target_pairs={{0,8},{2,10},{4,12},{6,14},{8,16},{10,18},{12,20},{14,22},{16,24},... | collective-permute-start | bytes 3145736 | tf_op jit(solution)/shard_map/ppermute | solution.py:74
  322.8 25.4 %collective-permute-start.40 = (f32[256,1024]{1,0:T(8,128)}, f32[256,1024]{1,0:T(8,128)}, u32[]{:S(2)}, u32[]{:S(2)}) collective-permute-start(f32[256,1024]{1,0:T(8,128)} %get-tuple-element.189.refs_5_), channel_id=1, source_target_pairs={{0,8},{2,10},{4,12},{6,14},{8,16},{10,18},{12,20},{14,22},{16,24},... | collective-permute-start | bytes 3145736 | tf_op jit(solution)/shard_map/ppermute | solution.py:74
  (13 other events, 205.7 us)
